TPU v7x, 32 devices: a whole 2x2x4 slice. The times are simulated.
32 devices in a mesh: seq: 8 (over z, x), head: 4 (over y, core).
Axes of the slice: x: 2, y: 2, z: 4, core: 2. Of those that a mesh axis runs over, the one named last changes fastest.
Arguments:
- layer_in: bfloat16 [2048, 2048], P('seq'), may hold values from -6 to 6
- out_grad: bfloat16 [2048, 2048], P('seq'), may hold values from -6 to 6
- doc_ids: int32 [2048], replicated, may hold values from 0 to 5, as said below
- attn_gain: bfloat16 [2048], P('seq'), may hold values from 0.5 to 1.5
- query_weight: bfloat16 [2048, 2048], P('seq', 'head'), may hold values from -0.125 to 0.125
- key_weight: bfloat16 [2048, 2048], P('seq', 'head'), may hold values from -0.125 to 0.125
- value_weight: bfloat16 [2048, 2048], P('seq', 'head'), may hold values from -0.125 to 0.125
- proj_weight: bfloat16 [2048, 2048], P('head', 'seq'), may hold values from -6 to 6
- mlp_gain: bfloat16 [2048], P('seq'), may hold values from 0.5 to 1.5
- gate_weight: bfloat16 [2048, 8192], P('seq', 'head'), may hold values from -0.125 to 0.125
- up_weight: bfloat16 [2048, 8192], P('seq', 'head'), may hold values from -0.125 to 0.125
- down_weight: bfloat16 [8192, 2048], P('head', 'seq'), may hold values from -0.0625 to 0.0625
Outputs:
- layer_out: bfloat16 [2048, 2048], P('seq')
- input_grad: float32 [2048, 2048], P('seq')
- grad_query: float32 [2048, 2048], P('seq', 'head')
- grad_key: float32 [2048, 2048], P('seq', 'head')
- grad_value: float32 [2048, 2048], P('seq', 'head')
- grad_proj: float32 [2048, 2048], P('head', 'seq')
- grad_gate: float32 [2048, 8192], P('seq', 'head')
- grad_up: float32 [2048, 8192], P('seq', 'head')
- grad_down: float32 [8192, 2048], P('head', 'seq')
- grad_attngain: float32 [2048], P('seq')
- grad_mlpgain: float32 [2048], P('seq')
Inputs may be any that keep to these rules, and one draw needn't show every extreme that they name: `doc_ids`: document numbers start at 0 and rise by one at each boundary between documents; every boundary lies among the first 256 or the last 256 tokens of the sequence.
All inputs are finite; a program needn't handle non-finite values.
Results may differ from a plain program's by a relative error of at most 0.017.
Values may be sent and summed in bfloat16 or wider, within the bound.
No kernel may reach another device: no remote copies, remote signals or barrier semaphores. Data moves between devices by JAX's collectives and lax.ppermute only.
A program may use at most 192 MiB of HBM per device.

v0:
```python
import math

import jax
import jax.numpy as jnp
from jax import lax
from jax.sharding import PartitionSpec as P

HD = 128


EPSILON = 1e-05
ROPE_BASE = 10000.0
LOG_BIAS = math.log(4096.0)


def rope_tables(positions, width):
    half_width = width // 2
    frequency = ROPE_BASE ** (-jnp.arange(half_width, dtype=jnp.float32) * 2.0 / width)
    angles = positions.astype(jnp.float32)[:, None] * frequency[None, :]
    return (jnp.cos(angles), jnp.sin(angles))


def rotate(values, cosine, sine_tab):
    half_width = values.shape[-1] // 2
    leading = values[..., :half_width]
    trailing = values[..., half_width:]
    cos_rows = cosine[:, None, :]
    sin_rows = sine_tab[:, None, :]
    return jnp.concatenate(
        [leading * cos_rows - trailing * sin_rows, trailing * cos_rows + leading * sin_rows],
        axis=-1,
    )


def dot_last(left_mat, right_mat):
    return lax.dot_general(
        left_mat, right_mat, (((1,), (1,)), ((), ())), preferred_element_type=jnp.float32
    )


def dot_first(left_mat, right_mat):
    return lax.dot_general(
        left_mat, right_mat, (((0,), (0,)), ((), ())), preferred_element_type=jnp.float32
    )


def rms_forward(values, gain_vec):
    inv_root = lax.rsqrt(jnp.mean(values * values, axis=-1, keepdims=True) + EPSILON)
    normed = values * inv_root
    return (normed, inv_root, (normed * gain_vec).astype(jnp.bfloat16))


def rms_backward(grad_hidden, normed, inv_root, gain_vec):
    grad_normed = grad_hidden * gain_vec
    return inv_root * (
        grad_normed - normed * jnp.mean(grad_normed * normed, axis=-1, keepdims=True)
    )


def masked_probs(query_blk, key_blk, query_pos, key_pos, query_doc, key_doc):
    scaling = query_blk.shape[-1] ** (-0.5)
    raw_scores = jnp.einsum("qhd,khd->hqk", query_blk, key_blk, preferred_element_type=jnp.float32)
    live_mask = (query_doc[:, None] == key_doc[None, :]) & (query_pos[:, None] >= key_pos[None, :])
    return jnp.where(live_mask[None], jax.nn.sigmoid(raw_scores * scaling - LOG_BIAS), 0.0)


def forward_block(query_blk, key_blk, value_blk, query_pos, key_pos, query_doc, key_doc):
    prob_vals = masked_probs(query_blk, key_blk, query_pos, key_pos, query_doc, key_doc)
    return jnp.einsum(
        "hqk,khd->qhd",
        prob_vals.astype(jnp.bfloat16),
        value_blk,
        preferred_element_type=jnp.float32,
    )


def backward_block(query_blk, key_blk, value_blk, grad_blk, query_pos, key_pos, query_doc, key_doc):
    scaling = query_blk.shape[-1] ** (-0.5)
    prob_vals = masked_probs(query_blk, key_blk, query_pos, key_pos, query_doc, key_doc)
    grad_values = jnp.einsum(
        "hqk,qhd->khd", prob_vals.astype(jnp.bfloat16), grad_blk, preferred_element_type=jnp.float32
    )
    grad_probs = jnp.einsum("qhd,khd->hqk", grad_blk, value_blk, preferred_element_type=jnp.float32)
    grad_scores = (grad_probs * prob_vals * (1.0 - prob_vals)).astype(jnp.bfloat16)
    grad_queries = (
        jnp.einsum("hqk,khd->qhd", grad_scores, key_blk, preferred_element_type=jnp.float32)
        * scaling
    )
    grad_keys = (
        jnp.einsum("hqk,qhd->khd", grad_scores, query_blk, preferred_element_type=jnp.float32)
        * scaling
    )
    return (grad_queries, grad_keys, grad_values)


def local(
    layer_in,
    out_grad,
    doc_ids,
    attn_gain,
    query_weight,
    key_weight,
    value_weight,
    proj_weight,
    mlp_gain,
    gate_weight,
    up_weight,
    down_weight,
):
    tok_rows = layer_in.shape[0]
    total_rows = tok_rows * lax.axis_size("seq")
    query_full, key_full, value_full, proj_full, gain_one = (
        lax.all_gather(query_weight, "seq", axis=0, tiled=True),
        lax.all_gather(key_weight, "seq", axis=0, tiled=True),
        lax.all_gather(value_weight, "seq", axis=0, tiled=True),
        lax.all_gather(proj_weight, "seq", axis=1, tiled=True),
        lax.all_gather(attn_gain, "seq", axis=0, tiled=True),
    )
    gate_full, up_full, down_full, gain_two = (
        lax.all_gather(gate_weight, "seq", axis=0, tiled=True),
        lax.all_gather(up_weight, "seq", axis=0, tiled=True),
        lax.all_gather(down_weight, "seq", axis=1, tiled=True),
        lax.all_gather(mlp_gain, "seq", axis=0, tiled=True),
    )
    heads_here = query_full.shape[1] // HD
    offset = lax.axis_index("seq") * tok_rows
    local_pos = offset + jnp.arange(tok_rows, dtype=jnp.int32)
    local_doc = lax.dynamic_slice_in_dim(doc_ids, offset, tok_rows, 0)
    cosine, sine_tab = rope_tables(local_pos, HD)
    inputs = layer_in.astype(jnp.float32)
    gain_a = gain_one.astype(jnp.float32)
    gain_b = gain_two.astype(jnp.float32)
    normed_a, inv_a, hidden_a = rms_forward(inputs, gain_a)
    query_raw = jnp.dot(hidden_a, query_full, preferred_element_type=jnp.float32)
    key_raw = jnp.dot(hidden_a, key_full, preferred_element_type=jnp.float32)
    value_raw = jnp.dot(hidden_a, value_full, preferred_element_type=jnp.float32)
    head_shape = (tok_rows, heads_here, HD)
    query_rot = rotate(query_raw.reshape(head_shape), cosine, sine_tab).astype(jnp.bfloat16)
    key_rot = rotate(key_raw.reshape(head_shape), cosine, sine_tab).astype(jnp.bfloat16)
    value_low = value_raw.reshape(head_shape).astype(jnp.bfloat16)
    zero_local = jnp.zeros(head_shape, jnp.float32)
    key_block = math.gcd(1024, total_rows)
    block_ids = jnp.arange(total_rows // key_block, dtype=jnp.int32)
    query_all = lax.all_gather(query_rot, "seq", axis=0, tiled=True)
    row_block = math.gcd(1024, tok_rows * lax.axis_size("seq"))

    def one_block(block_index):
        first_row = block_index * row_block
        query_blk = lax.dynamic_slice_in_dim(query_all, first_row, row_block, 0)
        query_pos = first_row + jnp.arange(row_block, dtype=jnp.int32)
        query_doc = lax.dynamic_slice_in_dim(doc_ids, first_row, row_block, 0)
        return forward_block(
            query_blk, key_rot, value_low, query_pos, local_pos, query_doc, local_doc
        )

    blocks = lax.map(
        one_block, jnp.arange(tok_rows * lax.axis_size("seq") // row_block, dtype=jnp.int32)
    )
    attn_out = lax.psum_scatter(
        blocks.reshape((tok_rows * lax.axis_size("seq"),) + query_rot.shape[1:]),
        "seq",
        scatter_dimension=0,
        tiled=True,
    )
    attn_low = attn_out.reshape(tok_rows, heads_here * HD).astype(jnp.bfloat16)
    middle = inputs + lax.psum(
        jnp.dot(attn_low, proj_full, preferred_element_type=jnp.float32), "head"
    )
    normed_b, inv_b, hidden_b = rms_forward(middle, gain_b)
    gate_val = jnp.dot(hidden_b, gate_full, preferred_element_type=jnp.float32)
    up_val = jnp.dot(hidden_b, up_full, preferred_element_type=jnp.float32)
    gate_sig = jax.nn.sigmoid(gate_val)
    silu_val = gate_val * gate_sig
    active = (silu_val * up_val).astype(jnp.bfloat16)
    mlp_sum = lax.psum(jnp.dot(active, down_full, preferred_element_type=jnp.float32), "head")
    layer_out = (middle + mlp_sum).astype(jnp.bfloat16)
    grad_top = out_grad.astype(jnp.float32)
    grad_active = dot_last(out_grad, down_full)
    grad_gate_val = (grad_active * up_val * gate_sig * (1.0 + gate_val * (1.0 - gate_sig))).astype(
        jnp.bfloat16
    )
    grad_up_val = (grad_active * silu_val).astype(jnp.bfloat16)
    down_term = dot_first(active, out_grad)
    gate_term = dot_first(hidden_b, grad_gate_val)
    up_term = dot_first(hidden_b, grad_up_val)
    grad_hidden_b = lax.psum(
        dot_last(grad_gate_val, gate_full) + dot_last(grad_up_val, up_full), "head"
    )
    gain_term_b = jnp.sum(grad_hidden_b * normed_b, axis=0)
    grad_middle = grad_top + rms_backward(grad_hidden_b, normed_b, inv_b, gain_b)
    grad_gate, grad_up, grad_down, grad_mlpgain = (
        lax.psum_scatter(gate_term, "seq", scatter_dimension=0, tiled=True),
        lax.psum_scatter(up_term, "seq", scatter_dimension=0, tiled=True),
        lax.psum_scatter(down_term, "seq", scatter_dimension=1, tiled=True),
        lax.psum_scatter(gain_term_b, "seq", scatter_dimension=0, tiled=True),
    )
    grad_mix = grad_middle.astype(jnp.bfloat16)
    proj_term = dot_first(attn_low, grad_mix)
    grad_attn = dot_last(grad_mix, proj_full).astype(jnp.bfloat16).reshape(head_shape)
    grad_all = lax.all_gather(grad_attn, "seq", axis=0, tiled=True)

    def query_back(running, block_index):
        first_row = block_index * key_block
        query_blk = lax.dynamic_slice_in_dim(query_all, first_row, key_block, 0)
        grad_blk = lax.dynamic_slice_in_dim(grad_all, first_row, key_block, 0)
        query_pos = first_row + jnp.arange(key_block, dtype=jnp.int32)
        query_doc = lax.dynamic_slice_in_dim(doc_ids, first_row, key_block, 0)
        grad_queries, grad_keys, grad_values = backward_block(
            query_blk, key_rot, value_low, grad_blk, query_pos, local_pos, query_doc, local_doc
        )
        return ((running[0] + grad_keys, running[1] + grad_values), grad_queries)

    (grad_krot, grad_vfull), query_terms = lax.scan(query_back, (zero_local, zero_local), block_ids)
    grad_qrot = lax.psum_scatter(
        query_terms.reshape(query_all.shape), "seq", scatter_dimension=0, tiled=True
    )
    flat_shape = (tok_rows, heads_here * HD)
    grad_query_low = rotate(grad_qrot, cosine, -sine_tab).reshape(flat_shape).astype(jnp.bfloat16)
    grad_key_low = rotate(grad_krot, cosine, -sine_tab).reshape(flat_shape).astype(jnp.bfloat16)
    grad_value_low = grad_vfull.reshape(flat_shape).astype(jnp.bfloat16)
    query_term = dot_first(hidden_a, grad_query_low)
    key_term = dot_first(hidden_a, grad_key_low)
    value_term = dot_first(hidden_a, grad_value_low)
    grad_hidden_a = lax.psum(
        (
            dot_last(grad_query_low, query_full)
            + dot_last(grad_key_low, key_full)
            + dot_last(grad_value_low, value_full)
        ).astype(jnp.bfloat16),
        "head",
    ).astype(jnp.float32)
    gain_term_a = jnp.sum(grad_hidden_a * normed_a, axis=0)
    input_grad = grad_middle + rms_backward(grad_hidden_a, normed_a, inv_a, gain_a)
    grad_query, grad_key, grad_value, grad_proj, grad_attngain = (
        lax.psum_scatter(query_term, "seq", scatter_dimension=0, tiled=True),
        lax.psum_scatter(key_term, "seq", scatter_dimension=0, tiled=True),
        lax.psum_scatter(value_term, "seq", scatter_dimension=0, tiled=True),
        lax.psum_scatter(proj_term, "seq", scatter_dimension=1, tiled=True),
        lax.psum_scatter(gain_term_a, "seq", scatter_dimension=0, tiled=True),
    )
    return (
        layer_out,
        input_grad,
        grad_query,
        grad_key,
        grad_value,
        grad_proj,
        grad_gate,
        grad_up,
        grad_down,
        grad_attngain,
        grad_mlpgain,
    )


def solution(mesh):
    return jax.shard_map(
        local,
        mesh=mesh,
        in_specs=(
            P("seq", None),
            P("seq", None),
            P(),
            P("seq"),
            P("seq", "head"),
            P("seq", "head"),
            P("seq", "head"),
            P("head", "seq"),
            P("seq"),
            P("seq", "head"),
            P("seq", "head"),
            P("head", "seq"),
        ),
        out_specs=(
            P("seq", None),
            P("seq", None),
            P("seq", "head"),
            P("seq", "head"),
            P("seq", "head"),
            P("head", "seq"),
            P("seq", "head"),
            P("seq", "head"),
            P("head", "seq"),
            P("seq"),
            P("seq"),
        ),
        check_vma=False,
    )
```

profile of v0, /device:TPU:0, one launch (start us, length us, event | category | flops | bytes accessed | tf_op | source)
XLA Modules:
  0.0 2367.6 jit_solution(6433511719798181473)
XLA Ops:
  10.1 22.2 all-gather
  35.1 27.0 %all-gather.12.cloned.1.call-done = bf16[2048,512]{1,0:T(8,128)(2,1)} async-done(((bf16[256,512]{1,0:T(8,128)(2,1)}), bf16[2048,512]{1,0:T(8,128)(2,1)}) %all-gather.12.cloned.1.call-update) | async-done | bytes 2097168 | tf_op jit(solution)/shard_map/all_gather | solution.py:113
  64.7 47.4 %all-gather.16.cloned.1.call-done = bf16[2048,512]{1,0:T(8,128)(2,1)} async-done(((bf16[256,512]{1,0:T(8,128)(2,1)}), bf16[2048,512]{1,0:T(8,128)(2,1)}) %all-gather.16.cloned.1.call-update) | async-done | bytes 2097168 | tf_op jit(solution)/shard_map/all_gather | solution.py:114
  116.6 45.5 %all-gather.18.cloned.1.call-done = bf16[2048,512]{1,0:T(8,128)(2,1)} async-done(((bf16[256,512]{1,0:T(8,128)(2,1)}), bf16[2048,512]{1,0:T(8,128)(2,1)}) %all-gather.18.cloned.1.call-update) | async-done | bytes 2097168 | tf_op jit(solution)/shard_map/all_gather | solution.py:115
  165.3 47.1 %all-gather.14.cloned.1.call-done = bf16[2048,4,128]{2,0,1:T(8,128)(2,1)} async-done(((bf16[256,4,128]{2,0,1:T(8,128)(2,1)}), bf16[2048,4,128]{2,0,1:T(8,128)(2,1)}) %all-gather.14.cloned.1.call-update) | async-done | bytes 2097168 | tf_op jit(solution)/shard_map/all_gather | solution.py:144
  214.8 13.0 while.30
  228.4 86.3 %reduce-scatter.10.cloned.1.call-done = f32[256,4,128]{2,0,1:T(8,128)} async-done(((f32[2048,4,128]{2,0,1:T(8,128)}), f32[256,4,128]{2,0,1:T(8,128)}) %reduce-scatter.10.cloned.1.call-update) | async-done | bytes 524304 | tf_op jit(solution)/shard_map/reduce_scatter | solution.py:159
  316.0 51.7 %all-gather.20.cloned.1.call-done = bf16[512,2048]{1,0:T(8,128)(2,1)} async-done(((bf16[512,256]{1,0:T(8,128)(2,1)}), bf16[512,2048]{1,0:T(8,128)(2,1)}) %all-gather.20.cloned.1.call-update) | async-done | bytes 2097168 | tf_op jit(solution)/shard_map/all_gather | solution.py:116
  373.5 17.9 all-gather.1
  391.4 29.7 %all-reduce.8.cloned.1.call-done = f32[256,2048]{1,0:T(8,128)} async-done(((f32[256,2048]{1,0:T(8,128)}), f32[256,2048]{1,0:T(8,128)}) %all-reduce.8.cloned.1.call-update) | async-done | bytes 2097168 | tf_op jit(solution)/shard_map/psum | solution.py:166
  424.3 124.0 %all-gather.22.cloned.1.call-done = bf16[2048,2048]{1,0:T(8,128)(2,1)} async-done(((bf16[256,2048]{1,0:T(8,128)(2,1)}), bf16[2048,2048]{1,0:T(8,128)(2,1)}) %all-gather.22.cloned.1.call-update) | async-done | bytes 8388624 | tf_op jit(solution)/shard_map/all_gather | solution.py:120
  548.3 7.4 fusion.63
  555.6 117.9 %all-gather.24.cloned.1.call-done = bf16[2048,2048]{1,0:T(8,128)(2,1)} async-done(((bf16[256,2048]{1,0:T(8,128)(2,1)}), bf16[2048,2048]{1,0:T(8,128)(2,1)}) %all-gather.24.cloned.1.call-update) | async-done | bytes 8388624 | tf_op jit(solution)/shard_map/all_gather | solution.py:121
  673.5 7.4 fusion.64
  680.9 118.1 %all-gather.26.cloned.1.call-done = bf16[2048,2048]{1,0:T(8,128)(2,1)} async-done(((bf16[2048,256]{1,0:T(8,128)(2,1)}), bf16[2048,2048]{1,0:T(8,128)(2,1)}) %all-gather.26.cloned.1.call-update) | async-done | bytes 8388624 | tf_op jit(solution)/shard_map/all_gather | solution.py:122
  799.0 7.9 multiply_convert_fusion.1
  814.0 7.2 fusion.65
  825.2 84.0 %all-reduce.12.cloned.1.call-done = (f32[256,2048]{1,0:T(8,128)}, f32[256,2048]{1,0:T(8,128)}) async-done(((f32[256,2048]{1,0:T(8,128)}, f32[256,2048]{1,0:T(8,128)}), (f32[256,2048]{1,0:T(8,128)}, f32[256,2048]{1,0:T(8,128)})) %all-reduce.12.cloned.1.call-update) | async-done | bytes 4194320 | tf_op jit(solution)/shard_map/psum | solution.py:175
  917.4 49.5 %all-gather.28.cloned.1.call-done = bf16[2048,4,128]{2,0,1:T(8,128)(2,1)} async-done(((bf16[256,4,128]{2,0,1:T(8,128)(2,1)}), bf16[2048,4,128]{2,0,1:T(8,128)(2,1)}) %all-gather.28.cloned.1.call-update) | async-done | bytes 2097168 | tf_op jit(solution)/shard_map/all_gather | solution.py:200
  969.2 29.8 %while.31 = (s32[]{:T(128)}, f32[256,4,128]{0,2,1:T(8,128)}, f32[256,4,128]{0,2,1:T(8,128)}, f32[2,1024,4,128]{3,1,0,2:T(8,128)}, s32[2]{0:T(128)S(1)}, /*index=...) while((s32[]{:T(128)}, f32[256,4,128]{0,2,1:T(8,128)}, ...), condition=%wide.region_10.11_spmd.clone, body=%wide.region_9.10_spmd.clone.sunk | while | flops 1355678976 | bytes 71589736 | solution.py:213
  1001.0 85.1 %reduce-scatter.12.cloned.1.call-done = f32[256,4,128]{2,0,1:T(8,128)} async-done(((f32[2048,4,128]{2,0,1:T(8,128)}), f32[256,4,128]{2,0,1:T(8,128)}) %reduce-scatter.12.cloned.1.call-update) | async-done | bytes 524304 | tf_op jit(solution)/shard_map/reduce_scatter | solution.py:214
  1108.8 9.7 fusion.68
  1118.6 9.8 fusion.69
  1128.5 9.7 fusion.70
  1142.1 37.9 %all-reduce.2 = (f32[2048]{0:T(1024)S(1)}, f32[2048]{0:T(1024)S(1)}) all-reduce(f32[2048]{0:T(1024)S(1)} %get-tuple-element.428, f32[2048]{0:T(1024)S(1)} %get-tuple-element.426), channel_id=11, replica_groups=mesh['seq'=8,'head'=4] {'seq'}, use_global_device_ids=true, to_apply=%region_22.23.clone | all-reduce | flops 4096 | bytes 32768
  1184.4 40.2 %reduce-scatter.20.cloned.1.call-done = f32[512,256]{1,0:T(8,128)} async-done(((f32[512,2048]{1,0:T(8,128)}), f32[512,256]{1,0:T(8,128)}) %reduce-scatter.20.cloned.1.call-update) | async-done | bytes 524304 | tf_op jit(solution)/shard_map/reduce_scatter | solution.py:238
  1224.7 91.7 %reduce-scatter.18.cloned.1.call-done = f32[256,512]{1,0:T(8,128)} async-done(((f32[2048,512]{1,0:T(8,128)}), f32[256,512]{1,0:T(8,128)}) %reduce-scatter.18.cloned.1.call-update) | async-done | bytes 524304 | tf_op jit(solution)/shard_map/reduce_scatter | solution.py:237
  1316.4 92.2 %reduce-scatter.16.cloned.1.call-done = f32[256,512]{1,0:T(8,128)} async-done(((f32[2048,512]{1,0:T(8,128)}), f32[256,512]{1,0:T(8,128)}) %reduce-scatter.16.cloned.1.call-update) | async-done | bytes 524304 | tf_op jit(solution)/shard_map/reduce_scatter | solution.py:236
  1408.6 91.7 %reduce-scatter.14.cloned.1.call-done = f32[256,512]{1,0:T(8,128)} async-done(((f32[2048,512]{1,0:T(8,128)}), f32[256,512]{1,0:T(8,128)}) %reduce-scatter.14.cloned.1.call-update) | async-done | bytes 524304 | tf_op jit(solution)/shard_map/reduce_scatter | solution.py:235
  1500.3 287.5 %reduce-scatter.22.cloned.1.call-done = f32[256,2048]{1,0:T(8,128)} async-done(((f32[2048,2048]{1,0:T(8,128)}), f32[256,2048]{1,0:T(8,128)}) %reduce-scatter.22.cloned.1.call-update) | async-done | bytes 2097168 | tf_op jit(solution)/shard_map/reduce_scatter | solution.py:192
  1787.8 285.8 %reduce-scatter.24.cloned.1.call-done = f32[256,2048]{1,0:T(8,128)} async-done(((f32[2048,2048]{1,0:T(8,128)}), f32[256,2048]{1,0:T(8,128)}) %reduce-scatter.24.cloned.1.call-update) | async-done | bytes 2097168 | tf_op jit(solution)/shard_map/reduce_scatter | solution.py:193
  2073.6 286.7 %reduce-scatter.26.cloned.1.call-done = f32[2048,256]{1,0:T(8,128)} async-done(((f32[2048,2048]{1,0:T(8,128)}), f32[2048,256]{1,0:T(8,128)}) %reduce-scatter.26.cloned.1.call-update) | async-done | bytes 2097168 | tf_op jit(solution)/shard_map/reduce_scatter | solution.py:194
  (221 shorter events, 122.5 us)
Async XLA Ops:
  7.2 55.0 %copy-start.2 = (bf16[256,2048]{1,0:T(8,128)(2,1)S(1)}, bf16[256,2048]{1,0:T(8,128)(2,1)}, u32[]{:S(2)}) copy-start(bf16[256,2048]{1,0:T(8,128)(2,1)} %param.16) | copy-start | bytes 3145732
  7.2 55.0 %all-gather.12.cloned.1.call-start = ((), (), s32[]{:S(2)}) async-start(), calls=%async_computation.9 | async-start | bytes 2359296 | tf_op jit(solution)/shard_map/all_gather | solution.py:113
  7.9 104.2 %all-gather.16.cloned.1.call-start = ((), (), s32[]{:S(2)}) async-start(), calls=%async_computation.11 | async-start | bytes 2359296 | tf_op jit(solution)/shard_map/all_gather | solution.py:114
  8.7 153.4 %all-gather.18.cloned.1.call-start = ((), (), s32[]{:S(2)}) async-start(), calls=%async_computation.12 | async-start | bytes 2359296 | tf_op jit(solution)/shard_map/all_gather | solution.py:115
  9.4 203.1 %all-gather.14.cloned.1.call-start = ((), (), s32[]{:S(2)}) async-start(), calls=%async_computation.10 | async-start | bytes 2359296 | tf_op jit(solution)/shard_map/all_gather | solution.py:144
  32.4 129.7 %copy-start.24 = (f32[8,1,256]{2,1,0:T(1,128)}, f32[8,1,256]{2,1,0:T(1,128)S(1)}, u32[]{:S(2)}) copy-start(f32[8,1,256]{2,1,0:T(1,128)S(1)} %convert_element_type.118) | copy-start | bytes 24580
  33.9 128.1 %copy-start.33 = (f32[256]{0:T(256)}, f32[256]{0:T(256)S(1)}, u32[]{:S(2)}) copy-start(f32[256]{0:T(256)S(1)} %add_rsqrt_fusion.1) | copy-start | bytes 3076
  35.1 80.1 %copy-start.26 = (f32[256,64]{1,0:T(8,128)}, f32[256,64]{1,0:T(8,128)S(1)}, u32[]{:S(2)}) copy-start(f32[256,64]{1,0:T(8,128)S(1)} %get-tuple-element.501) | copy-start | bytes 196612
  116.4 198.3 %reduce-scatter.10.cloned.1.call-start = ((), (), s32[]{:S(2)}) async-start(), calls=%async_computation.13 | async-start | bytes 4718592 | tf_op jit(solution)/shard_map/reduce_scatter | solution.py:159
  227.8 139.9 %all-gather.20.cloned.1.call-start = ((), (), s32[]{:S(2)}) async-start(), calls=%async_computation.14 | async-start | bytes 2359296 | tf_op jit(solution)/shard_map/all_gather | solution.py:116
  228.4 192.7 %all-reduce.8.cloned.1.call-start = ((), (), s32[]{:S(2)}) async-start(), calls=%async_computation.15 | async-start | bytes 4194304 | tf_op jit(solution)/shard_map/psum | solution.py:166
  316.0 55.4 %copy-start.14 = (bf16[256,4,128]{0,2,1:T(8,128)(2,1)}, bf16[256,4,128]{0,2,1:T(8,128)(2,1)S(1)}, u32[]{:S(2)}) copy-start(bf16[256,4,128]{0,2,1:T(8,128)(2,1)S(1)} %copy.75) | copy-start | bytes 786436
  371.4 176.9 %all-gather.22.cloned.1.call-start = ((), (), s32[]{:S(2)}) async-start(), calls=%async_computation.16 | async-start | bytes 9437184 | tf_op jit(solution)/shard_map/all_gather | solution.py:120
  372.1 301.4 %all-gather.24.cloned.1.call-start = ((), (), s32[]{:S(2)}) async-start(), calls=%async_computation.17 | async-start | bytes 9437184 | tf_op jit(solution)/shard_map/all_gather | solution.py:121
  372.9 426.2 %all-gather.26.cloned.1.call-start = ((), (), s32[]{:S(2)}) async-start(), calls=%async_computation.18 | async-start | bytes 9437184 | tf_op jit(solution)/shard_map/all_gather | solution.py:122
  373.5 535.7 %all-reduce.12.cloned.1.call-start = ((), (), s32[]{:S(2)}) async-start(), calls=%async_computation.29 | async-start | bytes 8388608 | tf_op jit(solution)/shard_map/psum | solution.py:175
  807.0 7.0 copy-start.30
  807.0 14.2 copy-start.29
  807.0 14.2 slice-start
  814.0 7.2 slice-start.1
  825.2 141.7 %all-gather.28.cloned.1.call-start = ((), (), s32[]{:S(2)}) async-start(), calls=%async_computation.19 | async-start | bytes 2359296 | tf_op jit(solution)/shard_map/all_gather | solution.py:200
  917.3 168.9 %reduce-scatter.12.cloned.1.call-start = ((), (), s32[]{:S(2)}) async-start(), calls=%async_computation.20 | async-start | bytes 4718592 | tf_op jit(solution)/shard_map/reduce_scatter | solution.py:214
  999.1 87.1 %copy-start.27 = (f32[256,64]{1,0:T(8,128)S(1)}, f32[256,64]{1,0:T(8,128)}, u32[]{:S(2)}) copy-start(f32[256,64]{1,0:T(8,128)} %copy-done.26) | copy-start | bytes 196612
  999.1 87.1 %copy-start.31 = (f32[256,64]{1,0:T(8,128)S(1)}, f32[256,64]{1,0:T(8,128)}, u32[]{:S(2)}) copy-start(f32[256,64]{1,0:T(8,128)} %get-tuple-element.499) | copy-start | bytes 196612
  999.1 141.0 %all-reduce.10.cloned.1.call-start = ((), (), s32[]{:S(2)}) async-start(), calls=%async_computation.21 | async-start | bytes 2097152 | tf_op jit(solution)/shard_map/psum | solution.py:224
  1094.5 130.2 %reduce-scatter.20.cloned.1.call-start = ((), (), s32[]{:S(2)}) async-start(), calls=%async_computation.25 | async-start | bytes 4718592 | tf_op jit(solution)/shard_map/reduce_scatter | solution.py:238
  1097.4 219.0 %reduce-scatter.18.cloned.1.call-start = ((), (), s32[]{:S(2)}) async-start(), calls=%async_computation.24 | async-start | bytes 4718592 | tf_op jit(solution)/shard_map/reduce_scatter | solution.py:237
  1101.1 307.5 %reduce-scatter.16.cloned.1.call-start = ((), (), s32[]{:S(2)}) async-start(), calls=%async_computation.23 | async-start | bytes 4718592 | tf_op jit(solution)/shard_map/reduce_scatter | solution.py:236
  1105.0 395.3 %reduce-scatter.14.cloned.1.call-start = ((), (), s32[]{:S(2)}) async-start(), calls=%async_computation.22 | async-start | bytes 4718592 | tf_op jit(solution)/shard_map/reduce_scatter | solution.py:235
  1108.8 679.0 %reduce-scatter.22.cloned.1.call-start = ((), (), s32[]{:S(2)}) async-start(), calls=%async_computation.26 | async-start | bytes 18874368 | tf_op jit(solution)/shard_map/reduce_scatter | solution.py:192
  1118.6 955.0 %reduce-scatter.24.cloned.1.call-start = ((), (), s32[]{:S(2)}) async-start(), calls=%async_computation.27 | async-start | bytes 18874368 | tf_op jit(solution)/shard_map/reduce_scatter | solution.py:193
  1128.4 1231.9 %reduce-scatter.26.cloned.1.call-start = ((), (), s32[]{:S(2)}) async-start(), calls=%async_computation.28 | async-start | bytes 18874368 | tf_op jit(solution)/shard_map/reduce_scatter | solution.py:194
  (32 other events, 67.1 us)
Sparse Core Ops, SparseCore 0:
  10.1 51.9 all-gather.11
  64.3 47.7 all-gather.15
  114.2 47.7 all-gather.17
  164.7 47.7 all-gather.13
  227.9 86.7 reduce-scatter.9
  316.8 50.8 all-gather.19
  371.5 49.5 all-reduce.7
  423.2 124.9 all-gather.21
  550.4 123.1 all-gather.23
  675.4 123.5 all-gather.25
  825.3 83.8 all-reduce.11
  917.4 49.3 all-gather.27
  999.2 86.9 reduce-scatter.11
  1094.6 35.8 all-reduce.9
  1135.0 89.6 reduce-scatter.19
  1228.7 87.6 reduce-scatter.17
  1320.9 87.6 reduce-scatter.15
  1412.7 87.6 reduce-scatter.13
  1505.2 282.5 reduce-scatter.21
  1792.0 281.5 reduce-scatter.23
  2078.5 281.7 reduce-scatter.25
where the time goes:
time: 2370 us
  waiting for transfers between devices  2090 us (88%)
  matrix products  130 us (5%)
  blocking collectives  78 us (3%)
  other arithmetic  25.5 us (1%)
    reduce_scatter x1, waiting for transfers between devices, local(): lax.psum_scatter(gate_term, 'seq', scatter_dimension=0, tiled=True)  287 us
    reduce_scatter x1, waiting for transfers between devices, local(): lax.psum_scatter(down_term, 'seq', scatter_dimension=1, tiled=True)  287 us
    reduce_scatter x1, waiting for transfers between devices, local(): lax.psum_scatter(up_term, 'seq', scatter_dimension=0, tiled=True)  286 us
    all_gather x1, waiting for transfers between devices, local(): lax.all_gather(gate_weight, 'seq', axis=0, tiled=True)  124 us
    all_gather x1, waiting for transfers between devices, local(): lax.all_gather(down_weight, 'seq', axis=1, tiled=True)  118 us
    all_gather x1, waiting for transfers between devices, local(): lax.all_gather(up_weight, 'seq', axis=0, tiled=True)  118 us
    reduce_scatter x1, waiting for transfers between devices, local(): lax.psum_scatter(key_term, 'seq', scatter_dimension=0, tiled=True)  92.2 us
    reduce_scatter x1, waiting for transfers between devices, local(): lax.psum_scatter(query_term, 'seq', scatter_dimension=0, tiled=True)  91.7 us
  transfers between devices with their start and end apart: 21, of which 20 were waited for; matrix products, arithmetic and copies ran while one was open for 3% of the time, Pallas kernels for 0%

commit v1 on v0

v1 whole, which is shorter than its diff:
```python
import math

import jax
import jax.numpy as jnp
from jax import lax
from jax.sharding import PartitionSpec as P

HD = 128
EPSILON = 1e-05
ROPE_BASE = 10000.0
LOG_BIAS = math.log(4096.0)
LOW = jnp.bfloat16
F32 = jnp.float32


def dot(left_mat, right_mat):
    return lax.dot_general(
        left_mat, right_mat, (((1,), (0,)), ((), ())), preferred_element_type=F32
    )


def dot_last(left_mat, right_mat):
    return lax.dot_general(
        left_mat, right_mat, (((1,), (1,)), ((), ())), preferred_element_type=F32
    )


def dot_first(left_mat, right_mat):
    return lax.dot_general(
        left_mat, right_mat, (((0,), (0,)), ((), ())), preferred_element_type=F32
    )


def inv_rms(values):
    return lax.rsqrt(jnp.mean(values * values, axis=-1, keepdims=True) + EPSILON)


def norm_back(grad_normed, normed, inv_root):
    return inv_root * (
        grad_normed - normed * jnp.mean(grad_normed * normed, axis=-1, keepdims=True)
    )


def rope_tables(positions, width):
    half_width = width // 2
    frequency = ROPE_BASE ** (-jnp.arange(half_width, dtype=F32) * 2.0 / width)
    angles = positions.astype(F32)[:, None] * frequency[None, :]
    return (jnp.cos(angles), jnp.sin(angles))


def rotate(values, cosine, sine_tab):
    half_width = values.shape[-1] // 2
    leading = values[:, :half_width]
    trailing = values[:, half_width:]
    return jnp.concatenate(
        [leading * cosine - trailing * sine_tab, trailing * cosine + leading * sine_tab], axis=-1
    )


def pick(stacked, index):
    return lax.dynamic_index_in_dim(stacked, index, 0, keepdims=False)


def local(
    layer_in,
    out_grad,
    doc_ids,
    attn_gain,
    query_weight,
    key_weight,
    value_weight,
    proj_weight,
    mlp_gain,
    gate_weight,
    up_weight,
    down_weight,
):
    tok, width = layer_in.shape
    seq_size, head_size = lax.axis_size("seq"), lax.axis_size("head")
    far = query_weight.shape[1] // HD
    groups = seq_size // far
    own = tok // head_size
    seq_at, head_at = lax.axis_index("seq"), lax.axis_index("head")
    far_at, group_at = seq_at // groups, seq_at % groups
    rows_s = width // seq_size

    def far_swap(value, step):
        return lax.ppermute(
            value,
            "seq",
            [
                (i * groups + g, (i ^ step) * groups + g)
                for i in range(far)
                for g in range(groups)
            ],
        )

    def group_shift(value, step):
        return lax.ppermute(
            value,
            "seq",
            [
                (i * groups + g, i * groups + (g + step) % groups)
                for i in range(far)
                for g in range(groups)
            ],
        )

    def head_swap(value, step):
        return lax.ppermute(value, "head", [(i, i ^ step) for i in range(head_size)])

    def gather_rows(piece):
        gathered = jnp.stack([piece] + [far_swap(piece, k) for k in range(1, far)])
        gathered = jnp.stack([gathered, head_swap(gathered, 2)], axis=1)
        gathered = jnp.stack([gathered, head_swap(gathered, 1)], axis=2)
        return gathered.reshape(far * head_size * own, piece.shape[1])

    def scatter_rows(partial):
        partial = partial.astype(LOW).reshape(far, 2, 2, own, partial.shape[1])
        partial = partial[:, :, 0].astype(F32) + head_swap(partial[:, :, 1], 1).astype(F32)
        partial = partial.astype(LOW)
        partial = partial[:, 0].astype(F32) + head_swap(partial[:, 1], 2).astype(F32)
        partial = partial.astype(LOW)
        total = partial[0].astype(F32)
        for k in range(1, far):
            total = total + far_swap(partial[k], k).astype(F32)
        return total

    def to_absolute(value):
        parts = value.reshape(far * head_size, own, value.shape[1])
        return jnp.concatenate(
            [
                pick(parts, (i ^ far_at) * head_size + (j ^ head_at))
                for i in range(far)
                for j in range(head_size)
            ]
        )

    to_relative = to_absolute

    def spread_weight(blocks):
        got = [pick(blocks, far_at)] + [
            far_swap(pick(blocks, far_at ^ k), k) for k in range(1, far)
        ]
        got = jnp.stack(got)
        got = jnp.stack([pick(got, i ^ far_at) for i in range(far)])
        every = jnp.stack([got] + [group_shift(got, g) for g in range(1, groups)])
        return jnp.stack([pick(every, (group_at - g) % groups) for g in range(groups)], axis=1).reshape(
            (seq_size,) + blocks.shape[1:]
        )

    def collect_grad(blocks):
        blocks = blocks.reshape((far, groups) + blocks.shape[1:])

        def column(at):
            return lax.dynamic_index_in_dim(blocks, at, 1, keepdims=False)

        total = column(group_at)
        for g in range(1, groups):
            total = total + group_shift(column((group_at + g) % groups).astype(LOW), g).astype(F32)
        sent = total.astype(LOW)
        got = [pick(sent, far_at)] + [far_swap(pick(sent, far_at ^ k), k) for k in range(1, far)]
        got = jnp.stack(got)
        return [pick(got, i ^ far_at).astype(F32) for i in range(far)]

    gain_a = attn_gain.astype(F32)[:, None]
    gain_b = mlp_gain.astype(F32)[:, None]

    def gained(weight, gain):
        return (weight.astype(F32) * gain).astype(LOW)

    qkv_local = jnp.stack(
        [gained(w, gain_a).reshape(rows_s, far, HD) for w in (query_weight, key_weight, value_weight)],
        axis=2,
    )
    qkv_full = spread_weight(
        qkv_local.reshape(rows_s, far, 3 * HD).transpose(1, 0, 2)
    ).reshape(width, 3 * HD)
    cols_s = proj_weight.shape[1]
    proj_full = (
        spread_weight(proj_weight.reshape(far, HD, cols_s)).transpose(1, 0, 2).reshape(HD, width)
    )
    hidden = gate_weight.shape[1] // far

    def spread_columns(weight):
        return spread_weight(
            gained(weight, gain_b).reshape(rows_s, far, hidden).transpose(1, 0, 2)
        ).reshape(width, hidden)

    gate_full = spread_columns(gate_weight)
    up_full = spread_columns(up_weight)
    down_full = (
        spread_weight(down_weight.reshape(far, hidden, cols_s))
        .transpose(1, 0, 2)
        .reshape(hidden, width)
    )

    own_in = lax.dynamic_slice_in_dim(layer_in, head_at * own, own, 0).astype(F32)
    own_grad = lax.dynamic_slice_in_dim(out_grad, head_at * own, own, 0)
    inv_a = inv_rms(own_in)
    normed_a = own_in * inv_a
    hidden_a = gather_rows(normed_a.astype(LOW))
    qkv = to_absolute(dot(hidden_a, qkv_full))
    tok_group = far * tok
    row_ids = jnp.arange(tok, dtype=jnp.int32)
    far_ids = jnp.arange(far, dtype=jnp.int32)
    query_pos = ((far_ids * groups + group_at)[:, None] * tok + row_ids[None, :]).reshape(tok_group)
    cosine, sine_tab = rope_tables(query_pos, HD)
    query_rot = rotate(qkv[:, :HD], cosine, sine_tab).astype(LOW)
    key_value = jnp.concatenate(
        [rotate(qkv[:, HD : 2 * HD], cosine, sine_tab).astype(LOW), qkv[:, 2 * HD :].astype(LOW)],
        axis=1,
    ).reshape(far, tok, 2 * HD)
    key_value = jnp.stack(
        [key_value] + [group_shift(key_value, g) for g in range(1, groups)], axis=1
    )
    source = (group_at - jnp.arange(groups, dtype=jnp.int32)) % groups
    docs = doc_ids.reshape(far, groups, tok)
    query_doc = lax.dynamic_index_in_dim(docs, group_at, 1, keepdims=False)
    key_doc = jnp.stack(
        [lax.dynamic_index_in_dim(docs, source[g], 1, keepdims=False) for g in range(groups)], axis=1
    )
    key_pos = (far_ids[:, None] * groups + source[None, :])[:, :, None] * tok + row_ids
    query_pos = query_pos.reshape(far, tok)
    query_blocks = query_rot.reshape(far, tok, HD)
    scaling = HD**-0.5
    probs, keys, values, attended = [], [], [], []
    for i in range(far):
        key_blk = key_value[: i + 1, :, :, :HD].reshape(-1, HD)
        value_blk = key_value[: i + 1, :, :, HD:].reshape(-1, HD)
        live_mask = (query_doc[i][:, None] == key_doc[: i + 1].reshape(-1)[None, :]) & (
            query_pos[i][:, None] >= key_pos[: i + 1].reshape(-1)[None, :]
        )
        scores = dot_last(query_blocks[i], key_blk) * scaling - LOG_BIAS
        prob_vals = jnp.where(live_mask, jax.nn.sigmoid(scores), 0.0)
        keys.append(key_blk)
        values.append(value_blk)
        probs.append(prob_vals)
        attended.append(dot(prob_vals.astype(LOW), value_blk))
    attn_low = to_relative(jnp.concatenate(attended).astype(LOW))
    middle = own_in + scatter_rows(dot(attn_low, proj_full))

    inv_b = inv_rms(middle)
    normed_b = middle * inv_b
    grad_top = gather_rows(own_grad)
    hidden_b = gather_rows(normed_b.astype(LOW))
    gate_val = dot(hidden_b, gate_full)
    up_val = dot(hidden_b, up_full)
    gate_sig = jax.nn.sigmoid(gate_val)
    silu_val = gate_val * gate_sig
    active = (silu_val * up_val).astype(LOW)
    grad_active = dot_last(grad_top, down_full)
    grad_gate_val = (grad_active * up_val * gate_sig * (1.0 + gate_val * (1.0 - gate_sig))).astype(LOW)
    grad_up_val = (grad_active * silu_val).astype(LOW)
    grad_normed_b = scatter_rows(
        dot_last(grad_gate_val, gate_full) + dot_last(grad_up_val, up_full)
    )
    grad_middle = own_grad.astype(F32) + norm_back(grad_normed_b, normed_b, inv_b)
    out_rows = (middle + scatter_rows(dot(active, down_full))).astype(LOW)

    def merge_columns(blocks):
        return jnp.concatenate(blocks, axis=1)

    grad_gate = merge_columns(
        collect_grad(dot_first(hidden_b, grad_gate_val).reshape(seq_size, rows_s, hidden))
    )
    grad_up = merge_columns(
        collect_grad(dot_first(hidden_b, grad_up_val).reshape(seq_size, rows_s, hidden))
    )
    grad_down = jnp.concatenate(
        collect_grad(
            dot_first(active, grad_top).reshape(hidden, seq_size, cols_s).transpose(1, 0, 2)
        )
    )

    grad_mix = gather_rows(grad_middle.astype(LOW))
    grad_proj = jnp.concatenate(
        collect_grad(
            dot_first(attn_low, grad_mix).reshape(HD, seq_size, cols_s).transpose(1, 0, 2)
        )
    )
    grad_attn = to_absolute(dot_last(grad_mix, proj_full).astype(LOW)).reshape(far, tok, HD)
    grad_query, grad_keys, grad_values = [], None, None
    for i in reversed(range(far)):
        prob_low = probs[i].astype(LOW)
        value_term = dot_first(prob_low, grad_attn[i])
        grad_probs = dot_last(grad_attn[i], values[i])
        grad_scores = (grad_probs * probs[i] * (1.0 - probs[i])).astype(LOW)
        grad_query.insert(0, dot(grad_scores, keys[i]) * scaling)
        key_term = dot_first(grad_scores, query_blocks[i]) * scaling
        if grad_keys is None:
            grad_keys, grad_values = key_term, value_term
        else:
            count = key_term.shape[0]
            grad_keys = jnp.concatenate([grad_keys[:count] + key_term, grad_keys[count:]])
            grad_values = jnp.concatenate([grad_values[:count] + value_term, grad_values[count:]])
    grad_kv = jnp.concatenate([grad_keys, grad_values], axis=1).reshape(far, groups, tok, 2 * HD)
    total_kv = grad_kv[:, 0]
    for g in range(1, groups):
        total_kv = total_kv + group_shift(grad_kv[:, g].astype(LOW), groups - g).astype(F32)
    total_kv = total_kv.reshape(tok_group, 2 * HD)
    grad_qkv = to_relative(
        jnp.concatenate(
            [
                rotate(jnp.concatenate(grad_query), cosine, -sine_tab).astype(LOW),
                rotate(total_kv[:, :HD], cosine, -sine_tab).astype(LOW),
                total_kv[:, HD:].astype(LOW),
            ],
            axis=1,
        )
    )
    grad_normed_a = scatter_rows(dot_last(grad_qkv, qkv_full))
    grad_in = (grad_middle + norm_back(grad_normed_a, normed_a, inv_a)).astype(LOW)
    qkv_blocks = collect_grad(dot_first(hidden_a, grad_qkv).reshape(seq_size, rows_s, 3 * HD))
    grad_query_w, grad_key_w, grad_value_w = (
        jnp.concatenate([b[:, n * HD : (n + 1) * HD] for b in qkv_blocks], axis=1) for n in range(3)
    )

    def every_row(piece):
        gathered = jnp.stack([piece, head_swap(piece, 2)])
        gathered = jnp.stack([gathered, head_swap(gathered, 1)], axis=1)
        gathered = gathered.reshape((head_size,) + piece.shape)
        return jnp.concatenate([pick(gathered, j ^ head_at) for j in range(head_size)])

    def head_sum(value):
        value = value + head_swap(value, 1)
        return value + head_swap(value, 2)

    def times(weight, grad):
        return jnp.sum(weight.astype(F32) * grad, axis=1)

    grad_attngain = head_sum(
        times(query_weight, grad_query_w)
        + times(key_weight, grad_key_w)
        + times(value_weight, grad_value_w)
    )
    grad_mlpgain = head_sum(times(gate_weight, grad_gate) + times(up_weight, grad_up))
    return (
        every_row(out_rows),
        every_row(grad_in).astype(F32),
        grad_query_w * gain_a,
        grad_key_w * gain_a,
        grad_value_w * gain_a,
        grad_proj,
        grad_gate * gain_b,
        grad_up * gain_b,
        grad_down,
        grad_attngain,
        grad_mlpgain,
    )


def solution(mesh):
    return jax.shard_map(
        local,
        mesh=mesh,
        in_specs=(
            P("seq", None),
            P("seq", None),
            P(),
            P("seq"),
            P("seq", "head"),
            P("seq", "head"),
            P("seq", "head"),
            P("head", "seq"),
            P("seq"),
            P("seq", "head"),
            P("seq", "head"),
            P("head", "seq"),
        ),
        out_specs=(
            P("seq", None),
            P("seq", None),
            P("seq", "head"),
            P("seq", "head"),
            P("seq", "head"),
            P("head", "seq"),
            P("seq", "head"),
            P("seq", "head"),
            P("head", "seq"),
            P("seq"),
            P("seq"),
        ),
        check_vma=False,
    )
```

time: 2370 us -> 782 us (0.33)
  waiting for transfers between devices: 2090 us -> 303 us
  starting transfers between devices: 1.1 us -> 171 us
  local copies, waits for them, and re-layouts: 20.2 us -> 146 us
  matrix products: 130 us -> 47.5 us
  blocking collectives: 78 us -> 0 us
  other arithmetic: 25.5 us -> 95.8 us
    reduce_scatter x9 -> x0, waiting for transfers between devices: 1350 us -> none  [the longest x1 287 us: local(): lax.psum_scatter(gate_term, 'seq', scatter_dimension=0, tiled=True)]
    all_gather x9 -> x0, waiting for transfers between devices: 628 us -> none  [the longest x1 124 us: local(): lax.all_gather(gate_weight, 'seq', axis=0, tiled=True)]
    ppermute x0 -> x90, waiting for transfers between devices: none -> 303 us  [the longest x54 138 us: far_swap(): lax.ppermute(value, 'seq', [(i * groups + g, (i ^ step) * groups + g) for...]
    ppermute x0 -> x90, starting transfers between devices: none -> 171 us  [the longest x54 137 us: far_swap(): lax.ppermute(value, 'seq', [(i * groups + g, (i ^ step) * groups + g) for...]
    psum x3 -> x0, waiting for transfers between devices: 114 us -> none  [the longest x1 84 us: local(): lax.psum(jnp.dot(active, down_full, preferred_element_type=jnp.float32),...]
    dot_general x19 -> x13, matrix products: 64.9 us -> 14.4 us  [dot(): lax.dot_general(left_mat, right_mat, (((1,), (0,)), ((), ())), preferred_...]
    another operation x2 -> x49, other arithmetic: 1.92 us -> 46.3 us  [the longest x8 19.2 us: gather_rows(): gathered = jnp.stack([gathered, head_swap(gathered, 1)], axis=2)]
    all_gather x2 -> x0, blocking collectives: 40.1 us -> none  [the longest x1 22.2 us: local(): lax.all_gather(attn_gain, 'seq', axis=0, tiled=True)]
  transfers between devices with their start and end apart: 21 -> 90, of which waited for: 20 -> 39; matrix products, arithmetic and copies ran while one was open for 3% -> 30% of each run, Pallas kernels for 0% -> 0%
where the time goes in v1:
time: 782 us; the launch traced here: 771 us
  waiting for transfers between devices  303 us (39%)
  starting transfers between devices  171 us (22%)
  local copies, waits for them, and re-layouts  146 us (19%)
  other arithmetic  95.8 us (12%)
  matrix products  47.5 us (6%)
    ppermute x54, waiting for transfers between devices, far_swap(): lax.ppermute(value, 'seq', [(i * groups + g, (i ^ step) * groups + g) for...  138 us
    ppermute x54, starting transfers between devices, far_swap(): lax.ppermute(value, 'seq', [(i * groups + g, (i ^ step) * groups + g) for...  137 us
    ppermute x12, waiting for transfers between devices, group_shift(): lax.ppermute(value, 'seq', [(i * groups + g, i * groups + (g + step) % gr...  98.3 us
    ppermute x24, waiting for transfers between devices, head_swap(): lax.ppermute(value, 'head', [(i, i ^ step) for i in range(head_size)])  66.6 us
    unnamed x257, local copies, waits for them, and re-layouts  34.4 us
    dynamic_slice x49, local copies, waits for them, and re-layouts, pick(): return lax.dynamic_index_in_dim(stacked, index, 0, keepdims=False)  30.3 us
    dot_general x4, local copies, waits for them, and re-layouts, dot_first(): lax.dot_general(left_mat, right_mat, (((0,), (0,)), ((), ())), preferred_...  25.6 us
    another operation x8, other arithmetic, gather_rows(): gathered = jnp.stack([gathered, head_swap(gathered, 1)], axis=2)  19.2 us
  transfers between devices with their start and end apart: 90, of which 39 were waited for; matrix products, arithmetic and copies ran while one was open for 30% of the time, Pallas kernels for 0%

profile of v1, /device:TPU:0, one launch (start us, length us, event | category | flops | bytes accessed | tf_op | source)
XLA Modules:
  0.0 771.4 jit_solution(7700255424409383332)
XLA Ops:
  20.1 7.3 collective-permute-done.1
  38.9 11.1 %collective-permute-done.3 = bf16[4,64,2048]{2,1,0:T(8,128)(2,1)S(1)} collective-permute-done((bf16[4,64,2048]{2,1,0:T(8,128)(2,1)S(1)}, bf16[4,64,2048]{2,1,0:T(8,128)(2,1)S(1)}, u32[]{:S(2)}, u32[]{:S(2)}) %collective-permute-start.3) | collective-permute-done | bytes 1048608 | tf_op jit(solution)/shard_map/ppermute | solution.py:110
  57.5 8.2 %collective-permute-start.11 = (bf16[128,256]{1,0:T(8,128)(2,1)}, bf16[128,256]{1,0:T(8,128)(2,1)S(1)}, u32[]{:S(2)}, u32[]{:S(2)}) collective-permute-start(bf16[128,256]{1,0:T(8,128)(2,1)} %get-tuple-element.275), channel_id=1, source_target_pairs={{0,16},{4,20},{8,24},{12,28},{16,0},{20,4},{24,8},{28,12},{1,17},{... | collective-permute-start | bytes 196616 | tf_op jit(solution)/shard_map/ppermute | solution.py:88
  74.2 14.6 %collective-permute-done.8 = bf16[4,256,384]{1,2,0:T(8,128)(2,1)S(1)} collective-permute-done((bf16[4,256,384]{1,2,0:T(8,128)(2,1)S(1)}, bf16[4,256,384]{1,2,0:T(8,128)(2,1)S(1)}, u32[]{:S(2)}, u32[]{:S(2)}) %collective-permute-start.8) | collective-permute-done | bytes 786464 | tf_op jit(solution)/shard_map/ppermute | solution.py:99
  208.0 5.4 collective-permute-done.17
  214.7 19.3 %collective-permute-start.19 = (bf16[64,2048]{1,0:T(8,128)(2,1)S(1)}, bf16[64,2048]{1,0:T(8,128)(2,1)S(1)}, u32[]{:S(2)}, u32[]{:S(2)}) collective-permute-start(bf16[64,2048]{1,0:T(8,128)(2,1)S(1)} %multiply_convert_fusion.3), channel_id=1, source_target_pairs={{0,8},{4,12},{8,0},{12,4},{16,24},{20,28},{24,16},{28,20},{1,9},{5... | collective-permute-start | bytes 786440 | tf_op jit(solution)/shard_map/ppermute | solution.py:88
  245.2 18.7 %collective-permute-done.20 = bf16[64,2048]{1,0:T(8,128)(2,1)S(1)} collective-permute-done((bf16[64,2048]{1,0:T(8,128)(2,1)S(1)}, bf16[64,2048]{1,0:T(8,128)(2,1)S(1)}, u32[]{:S(2)}, u32[]{:S(2)}) %collective-permute-start.20) | collective-permute-done | bytes 262176 | tf_op jit(solution)/shard_map/ppermute | solution.py:88
  266.4 5.8 collective-permute-done.21
  272.2 12.5 %collective-permute-start.28 = (bf16[256,512]{1,0:T(8,128)(2,1)S(1)}, bf16[256,512]{1,0:T(8,128)(2,1)S(1)}, u32[]{:S(2)}, u32[]{:S(2)}) collective-permute-start(bf16[256,512]{1,0:T(8,128)(2,1)S(1)} %bitcast.794), channel_id=1, source_target_pairs={{0,8},{4,12},{8,0},{12,4},{16,24},{20,28},{24,16},{28,20},{1,9},{5... | collective-permute-start | bytes 786440 | tf_op jit(solution)/shard_map/ppermute | solution.py:88
  294.2 11.6 %collective-permute-done.29 = bf16[256,512]{1,0:T(8,128)(2,1)S(1)} collective-permute-done((bf16[256,512]{1,0:T(8,128)(2,1)S(1)}, bf16[256,512]{1,0:T(8,128)(2,1)S(1)}, u32[]{:S(2)}, u32[]{:S(2)}) %collective-permute-start.29) | collective-permute-done | bytes 262176 | tf_op jit(solution)/shard_map/ppermute | solution.py:88
  325.0 16.3 %collective-permute-done.27 = bf16[4,256,512]{2,1,0:T(8,128)(2,1)} collective-permute-done((bf16[4,256,512]{2,1,0:T(8,128)(2,1)}, bf16[4,256,512]{2,1,0:T(8,128)(2,1)}, u32[]{:S(2)}, u32[]{:S(2)}) %collective-permute-start.27) | collective-permute-done | bytes 1048608 | tf_op jit(solution)/shard_map/ppermute | solution.py:99
  341.4 17.7 %collective-permute-done.31 = bf16[4,256,512]{2,1,0:T(8,128)(2,1)} collective-permute-done((bf16[4,256,512]{2,1,0:T(8,128)(2,1)}, bf16[4,256,512]{2,1,0:T(8,128)(2,1)}, u32[]{:S(2)}, u32[]{:S(2)}) %collective-permute-start.31) | collective-permute-done | bytes 1048608 | tf_op jit(solution)/shard_map/ppermute | solution.py:99
  393.9 6.4 copy.402
  400.3 6.4 copy.413
  406.7 6.4 copy.404
  413.1 5.0 fusion.67
  428.6 18.0 %collective-permute-done.49 = bf16[4,64,2048]{2,1,0:T(8,128)(2,1)S(1)} collective-permute-done((bf16[4,64,2048]{2,1,0:T(8,128)(2,1)S(1)}, bf16[4,64,2048]{2,1,0:T(8,128)(2,1)S(1)}, u32[]{:S(2)}, u32[]{:S(2)}) %collective-permute-start.49) | collective-permute-done | bytes 1048608 | tf_op jit(solution)/shard_map/ppermute | solution.py:110
  451.6 16.6 %collective-permute-done.37 = bf16[4,64,2048]{2,1,0:T(8,128)(2,1)S(1)} collective-permute-done((bf16[4,64,2048]{2,1,0:T(8,128)(2,1)S(1)}, bf16[4,64,2048]{2,1,0:T(8,128)(2,1)S(1)}, u32[]{:S(2)}, u32[]{:S(2)}) %collective-permute-start.37) | collective-permute-done | bytes 1048608 | tf_op jit(solution)/shard_map/ppermute | solution.py:110
  473.4 7.3 collective-permute-done.38
  480.7 9.5 %collective-permute-done.39 = bf16[64,2048]{1,0:T(8,128)(2,1)S(1)} collective-permute-done((bf16[64,2048]{1,0:T(8,128)(2,1)S(1)}, bf16[64,2048]{1,0:T(8,128)(2,1)S(1)}, u32[]{:S(2)}, u32[]{:S(2)}) %collective-permute-start.39) | collective-permute-done | bytes 262176 | tf_op jit(solution)/shard_map/ppermute | solution.py:88
  505.5 12.2 %collective-permute-done.54 = bf16[64,2048]{1,0:T(8,128)(2,1)S(1)} collective-permute-done((bf16[64,2048]{1,0:T(8,128)(2,1)S(1)}, bf16[64,2048]{1,0:T(8,128)(2,1)S(1)}, u32[]{:S(2)}, u32[]{:S(2)}) %collective-permute-start.54) | collective-permute-done | bytes 262176 | tf_op jit(solution)/shard_map/ppermute | solution.py:88
  528.6 19.4 %collective-permute-done.74 = bf16[4,256,512]{2,1,0:T(8,128)(2,1)S(1)} collective-permute-done((bf16[4,256,512]{2,1,0:T(8,128)(2,1)S(1)}, bf16[4,256,512]{2,1,0:T(8,128)(2,1)S(1)}, u32[]{:S(2)}, u32[]{:S(2)}) %collective-permute-start.74) | collective-permute-done | bytes 1048608 | tf_op jit(solution)/shard_map/ppermute | solution.py:99
  554.1 13.2 %collective-permute-done.82 = bf16[4,512,256]{2,1,0:T(8,128)(2,1)S(1)} collective-permute-done((bf16[4,512,256]{2,1,0:T(8,128)(2,1)S(1)}, bf16[4,512,256]{2,1,0:T(8,128)(2,1)S(1)}, u32[]{:S(2)}, u32[]{:S(2)}) %collective-permute-start.82) | collective-permute-done | bytes 1048608 | tf_op jit(solution)/shard_map/ppermute | solution.py:99
  577.6 12.8 %collective-permute-done.76 = bf16[256,512]{1,0:T(8,128)(2,1)} collective-permute-done((bf16[256,512]{1,0:T(8,128)(2,1)}, bf16[256,512]{1,0:T(8,128)(2,1)}, u32[]{:S(2)}, u32[]{:S(2)}) %collective-permute-start.76) | collective-permute-done | bytes 262176 | tf_op jit(solution)/shard_map/ppermute | solution.py:88
  606.5 6.0 collective-permute-done.84
  646.7 6.4 copy.403
  680.6 9.8 %collective-permute-start.71 = (bf16[128,256]{1,0:T(8,128)(2,1)S(1)}, bf16[128,256]{1,0:T(8,128)(2,1)S(1)}, u32[]{:S(2)}, u32[]{:S(2)}) collective-permute-start(bf16[128,256]{1,0:T(8,128)(2,1)S(1)} %get-tuple-element.250), channel_id=1, source_target_pairs={{0,8},{4,12},{8,0},{12,4},{16,24},{20,28},{24,16},{28,20},{1,9},{5... | collective-permute-start | bytes 196616 | tf_op jit(solution)/shard_map/ppermute | solution.py:88
  696.9 9.8 %collective-permute-start.67 = (bf16[256,384]{1,0:T(8,128)(2,1)S(1)}, bf16[256,384]{1,0:T(8,128)(2,1)S(1)}, u32[]{:S(2)}, u32[]{:S(2)}) collective-permute-start(bf16[256,384]{1,0:T(8,128)(2,1)S(1)} %get-tuple-element.207), channel_id=1, source_target_pairs={{0,8},{4,12},{8,0},{12,4},{16,24},{20,28},{24,16},{28,20},{1,9},{5... | collective-permute-start | bytes 589832 | tf_op jit(solution)/shard_map/ppermute | solution.py:88
  714.0 9.7 %collective-permute-done.68 = bf16[256,384]{1,0:T(8,128)(2,1)S(1)} collective-permute-done((bf16[256,384]{1,0:T(8,128)(2,1)S(1)}, bf16[256,384]{1,0:T(8,128)(2,1)S(1)}, u32[]{:S(2)}, u32[]{:S(2)}) %collective-permute-start.68) | collective-permute-done | bytes 196640 | tf_op jit(solution)/shard_map/ppermute | solution.py:88
  724.0 10.1 %collective-permute-done.60 = bf16[4,64,2048]{2,1,0:T(8,128)(2,1)S(1)} collective-permute-done((bf16[4,64,2048]{2,1,0:T(8,128)(2,1)S(1)}, bf16[4,64,2048]{2,1,0:T(8,128)(2,1)S(1)}, u32[]{:S(2)}, u32[]{:S(2)}) %collective-permute-start.60) | collective-permute-done | bytes 1048608 | tf_op jit(solution)/shard_map/ppermute | solution.py:110
  739.2 7.2 collective-permute-done.61
  746.3 9.2 %collective-permute-done.62 = bf16[64,2048]{1,0:T(8,128)(2,1)S(1)} collective-permute-done((bf16[64,2048]{1,0:T(8,128)(2,1)S(1)}, bf16[64,2048]{1,0:T(8,128)(2,1)S(1)}, u32[]{:S(2)}, u32[]{:S(2)}) %collective-permute-start.62) | collective-permute-done | bytes 262176 | tf_op jit(solution)/shard_map/ppermute | solution.py:88
  (692 shorter events, 414.0 us)
Async XLA Ops:
  10.1 60.9 %collective-permute-start.10 = (bf16[128,256]{1,0:T(8,128)(2,1)}, bf16[128,256]{1,0:T(8,128)(2,1)S(1)}, u32[]{:S(2)}, u32[]{:S(2)}) collective-permute-start(bf16[128,256]{1,0:T(8,128)(2,1)} %get-tuple-element.276), channel_id=1, source_target_pairs={{0,8},{4,12},{8,0},{12,4},{16,24},{20,28},{24,16},{28,20},{1,9},{5... | collective-permute-start | bytes 196616 | tf_op jit(solution)/shard_map/ppermute | solution.py:88
  14.4 43.2 %collective-permute-start.5 = (bf16[256,384]{0,1:T(8,128)(2,1)}, bf16[256,384]{0,1:T(8,128)(2,1)}, u32[]{:S(2)}, u32[]{:S(2)}) collective-permute-start(bf16[256,384]{0,1:T(8,128)(2,1)} %get-tuple-element.217), channel_id=1, source_target_pairs={{0,8},{4,12},{8,0},{12,4},{16,24},{20,28},{24,16},{28,20},{1,9},{5... | collective-permute-start | bytes 589832 | tf_op jit(solution)/shard_map/ppermute | solution.py:88
  17.9 47.8 %collective-permute-start.6 = (bf16[256,384]{0,1:T(8,128)(2,1)}, bf16[256,384]{0,1:T(8,128)(2,1)}, u32[]{:S(2)}, u32[]{:S(2)}) collective-permute-start(bf16[256,384]{0,1:T(8,128)(2,1)} %get-tuple-element.216), channel_id=1, source_target_pairs={{0,16},{4,20},{8,24},{12,28},{16,0},{20,4},{24,8},{28,12},{1,17},{... | collective-permute-start | bytes 589832 | tf_op jit(solution)/shard_map/ppermute | solution.py:88
  27.4 39.5 %collective-permute-start.7 = (bf16[256,384]{0,1:T(8,128)(2,1)}, bf16[256,384]{0,1:T(8,128)(2,1)}, u32[]{:S(2)}, u32[]{:S(2)}) collective-permute-start(bf16[256,384]{0,1:T(8,128)(2,1)} %get-tuple-element.215), channel_id=1, source_target_pairs={{0,24},{4,28},{8,16},{12,20},{16,8},{20,12},{24,0},{28,4},{1,25},{... | collective-permute-start | bytes 589832 | tf_op jit(solution)/shard_map/ppermute | solution.py:88
  53.8 41.4 %collective-permute-start.4 = (bf16[4,2,64,2048]{3,2,0,1:T(8,128)(2,1)}, bf16[4,2,64,2048]{3,2,0,1:T(8,128)(2,1)}, u32[]{:S(2)}, u32[]{:S(2)}) collective-permute-start(bf16[4,2,64,2048]{3,2,0,1:T(8,128)(2,1)} %get-tuple-element.83), channel_id=1, source_target_pairs={{0,1},{1,0},{2,3},{3,2},{4,5},{5,4},{6,7},{7,6},{8,9},{9,8},{10,11... | collective-permute-start | bytes 6291464 | tf_op jit(solution)/shard_map/ppermute | solution.py:110
  72.7 46.1 %collective-permute-start.13 = (bf16[4,128,256]{2,1,0:T(8,128)(2,1)}, bf16[4,128,256]{2,1,0:T(8,128)(2,1)}, u32[]{:S(2)}, u32[]{:S(2)}) collective-permute-start(bf16[4,128,256]{2,1,0:T(8,128)(2,1)} %get-tuple-element.267), channel_id=1, source_target_pairs={{0,4},{4,0},{8,12},{12,8},{16,20},{20,16},{24,28},{28,24},{1,5},{5... | collective-permute-start | bytes 786440 | tf_op jit(solution)/shard_map/ppermute | solution.py:99
  151.4 43.4 %collective-permute-start.32 = (bf16[512,256]{1,0:T(8,128)(2,1)}, bf16[512,256]{1,0:T(8,128)(2,1)}, u32[]{:S(2)}, u32[]{:S(2)}) collective-permute-start(bf16[512,256]{1,0:T(8,128)(2,1)} %get-tuple-element.164), channel_id=1, source_target_pairs={{0,8},{4,12},{8,0},{12,4},{16,24},{20,28},{24,16},{28,20},{1,9},{5... | collective-permute-start | bytes 786440 | tf_op jit(solution)/shard_map/ppermute | solution.py:88
  151.5 45.4 %collective-permute-start.33 = (bf16[512,256]{1,0:T(8,128)(2,1)}, bf16[512,256]{1,0:T(8,128)(2,1)}, u32[]{:S(2)}, u32[]{:S(2)}) collective-permute-start(bf16[512,256]{1,0:T(8,128)(2,1)} %get-tuple-element.163), channel_id=1, source_target_pairs={{0,16},{4,20},{8,24},{12,28},{16,0},{20,4},{24,8},{28,12},{1,17},{... | collective-permute-start | bytes 786440 | tf_op jit(solution)/shard_map/ppermute | solution.py:88
  154.7 42.3 %collective-permute-start.34 = (bf16[512,256]{1,0:T(8,128)(2,1)}, bf16[512,256]{1,0:T(8,128)(2,1)}, u32[]{:S(2)}, u32[]{:S(2)}) collective-permute-start(bf16[512,256]{1,0:T(8,128)(2,1)} %get-tuple-element.162), channel_id=1, source_target_pairs={{0,24},{4,28},{8,16},{12,20},{16,8},{20,12},{24,0},{28,4},{1,25},{... | collective-permute-start | bytes 786440 | tf_op jit(solution)/shard_map/ppermute | solution.py:88
  196.9 39.1 %collective-permute-start.43 = (bf16[64,2048]{1,0:T(8,128)(2,1)S(1)}, bf16[64,2048]{1,0:T(8,128)(2,1)S(1)}, u32[]{:S(2)}, u32[]{:S(2)}) collective-permute-start(bf16[64,2048]{1,0:T(8,128)(2,1)S(1)} %constant_dynamic-slice_fusion.23), channel_id=1, source_target_pairs={{0,8},{4,12},{8,0},{12,4},{16,24},{20,28},{24,16},{28,20},{1,9},{5... | collective-permute-start | bytes 786440 | tf_op jit(solution)/shard_map/ppermute | solution.py:88
  197.0 43.7 %collective-permute-start.44 = (bf16[64,2048]{1,0:T(8,128)(2,1)S(1)}, bf16[64,2048]{1,0:T(8,128)(2,1)S(1)}, u32[]{:S(2)}, u32[]{:S(2)}) collective-permute-start(bf16[64,2048]{1,0:T(8,128)(2,1)S(1)} %constant_dynamic-slice_fusion.23), channel_id=1, source_target_pairs={{0,16},{4,20},{8,24},{12,28},{16,0},{20,4},{24,8},{28,12},{1,17},{... | collective-permute-start | bytes 786440 | tf_op jit(solution)/shard_map/ppermute | solution.py:88
  205.5 35.3 %collective-permute-start.45 = (bf16[64,2048]{1,0:T(8,128)(2,1)S(1)}, bf16[64,2048]{1,0:T(8,128)(2,1)S(1)}, u32[]{:S(2)}, u32[]{:S(2)}) collective-permute-start(bf16[64,2048]{1,0:T(8,128)(2,1)S(1)} %constant_dynamic-slice_fusion.23), channel_id=1, source_target_pairs={{0,24},{4,28},{8,16},{12,20},{16,8},{20,12},{24,0},{28,4},{1,25},{... | collective-permute-start | bytes 786440 | tf_op jit(solution)/shard_map/ppermute | solution.py:88
  236.1 48.8 %collective-permute-start.24 = (bf16[256,512]{1,0:T(8,128)(2,1)S(1)}, bf16[256,512]{1,0:T(8,128)(2,1)S(1)}, u32[]{:S(2)}, u32[]{:S(2)}) collective-permute-start(bf16[256,512]{1,0:T(8,128)(2,1)S(1)} %bitcast.797), channel_id=1, source_target_pairs={{0,8},{4,12},{8,0},{12,4},{16,24},{20,28},{24,16},{28,20},{1,9},{5... | collective-permute-start | bytes 786440 | tf_op jit(solution)/shard_map/ppermute | solution.py:88
  240.8 45.2 %collective-permute-start.25 = (bf16[256,512]{1,0:T(8,128)(2,1)S(1)}, bf16[256,512]{1,0:T(8,128)(2,1)S(1)}, u32[]{:S(2)}, u32[]{:S(2)}) collective-permute-start(bf16[256,512]{1,0:T(8,128)(2,1)S(1)} %bitcast.796), channel_id=1, source_target_pairs={{0,16},{4,20},{8,24},{12,28},{16,0},{20,4},{24,8},{28,12},{1,17},{... | collective-permute-start | bytes 786440 | tf_op jit(solution)/shard_map/ppermute | solution.py:88
  240.8 46.8 %collective-permute-start.26 = (bf16[256,512]{1,0:T(8,128)(2,1)S(1)}, bf16[256,512]{1,0:T(8,128)(2,1)S(1)}, u32[]{:S(2)}, u32[]{:S(2)}) collective-permute-start(bf16[256,512]{1,0:T(8,128)(2,1)S(1)} %bitcast.795), channel_id=1, source_target_pairs={{0,24},{4,28},{8,16},{12,20},{16,8},{20,12},{24,0},{28,4},{1,25},{... | collective-permute-start | bytes 786440 | tf_op jit(solution)/shard_map/ppermute | solution.py:88
  243.6 63.8 %collective-permute-start.46 = (bf16[4,64,2048]{2,1,0:T(8,128)(2,1)S(1)}, bf16[4,64,2048]{2,1,0:T(8,128)(2,1)S(1)}, u32[]{:S(2)}, u32[]{:S(2)}) collective-permute-start(bf16[4,64,2048]{2,1,0:T(8,128)(2,1)S(1)} %get-tuple-element.147), channel_id=1, source_target_pairs={{0,2},{1,3},{2,0},{3,1},{4,6},{5,7},{6,4},{7,5},{8,10},{9,11},{10,... | collective-permute-start | bytes 3145736 | tf_op jit(solution)/shard_map/ppermute | solution.py:110
  305.8 35.6 %collective-permute-start.27 = (bf16[4,256,512]{2,1,0:T(8,128)(2,1)}, bf16[4,256,512]{2,1,0:T(8,128)(2,1)}, u32[]{:S(2)}, u32[]{:S(2)}) collective-permute-start(bf16[4,256,512]{2,1,0:T(8,128)(2,1)} %get-tuple-element.165), channel_id=1, source_target_pairs={{0,4},{4,0},{8,12},{12,8},{16,20},{20,16},{24,28},{28,24},{1,5},{5... | collective-permute-start | bytes 3145736 | tf_op jit(solution)/shard_map/ppermute | solution.py:99
  309.7 53.0 %collective-permute-start.47 = (bf16[4,2,64,2048]{3,2,0,1:T(8,128)(2,1)}, bf16[4,2,64,2048]{3,2,0,1:T(8,128)(2,1)}, u32[]{:S(2)}, u32[]{:S(2)}) collective-permute-start(bf16[4,2,64,2048]{3,2,0,1:T(8,128)(2,1)} %get-tuple-element.73), channel_id=1, source_target_pairs={{0,1},{1,0},{2,3},{3,2},{4,5},{5,4},{6,7},{7,6},{8,9},{9,8},{10,11... | collective-permute-start | bytes 6291464 | tf_op jit(solution)/shard_map/ppermute | solution.py:110
  312.3 54.3 %collective-permute-start.23 = (bf16[4,2,64,2048]{3,2,1,0:T(8,128)(2,1)}, bf16[4,2,64,2048]{3,2,1,0:T(8,128)(2,1)}, u32[]{:S(2)}, u32[]{:S(2)}) collective-permute-start(bf16[4,2,64,2048]{3,2,1,0:T(8,128)(2,1)} %get-tuple-element.81), channel_id=1, source_target_pairs={{0,1},{1,0},{2,3},{3,2},{4,5},{5,4},{6,7},{7,6},{8,9},{9,8},{10,11... | collective-permute-start | bytes 6291464 | tf_op jit(solution)/shard_map/ppermute | solution.py:110
  314.1 44.9 %collective-permute-start.31 = (bf16[4,256,512]{2,1,0:T(8,128)(2,1)}, bf16[4,256,512]{2,1,0:T(8,128)(2,1)}, u32[]{:S(2)}, u32[]{:S(2)}) collective-permute-start(bf16[4,256,512]{2,1,0:T(8,128)(2,1)} %get-tuple-element.175), channel_id=1, source_target_pairs={{0,4},{4,0},{8,12},{12,8},{16,20},{20,16},{24,28},{28,24},{1,5},{5... | collective-permute-start | bytes 3145736 | tf_op jit(solution)/shard_map/ppermute | solution.py:99
  387.1 30.9 %collective-permute-start.48 = (bf16[4,2,64,2048]{3,2,0,1:T(8,128)(2,1)}, bf16[4,2,64,2048]{3,2,0,1:T(8,128)(2,1)}, u32[]{:S(2)}, u32[]{:S(2)}) collective-permute-start(bf16[4,2,64,2048]{3,2,0,1:T(8,128)(2,1)} %bitcast.654), channel_id=1, source_target_pairs={{0,1},{1,0},{2,3},{3,2},{4,5},{5,4},{6,7},{7,6},{8,9},{9,8},{10,11... | collective-permute-start | bytes 6291464 | tf_op jit(solution)/shard_map/ppermute | solution.py:110
  424.8 43.4 %collective-permute-start.37 = (bf16[4,64,2048]{2,1,0:T(8,128)(2,1)S(1)}, bf16[4,64,2048]{2,1,0:T(8,128)(2,1)S(1)}, u32[]{:S(2)}, u32[]{:S(2)}) collective-permute-start(bf16[4,64,2048]{2,1,0:T(8,128)(2,1)S(1)} %slice_bitcast_fusion.4), channel_id=1, source_target_pairs={{0,2},{1,3},{2,0},{3,1},{4,6},{5,7},{6,4},{7,5},{8,10},{9,11},{10,... | collective-permute-start | bytes 3145736 | tf_op jit(solution)/shard_map/ppermute | solution.py:110
  501.1 46.9 %collective-permute-start.74 = (bf16[4,256,512]{2,1,0:T(8,128)(2,1)S(1)}, bf16[4,256,512]{2,1,0:T(8,128)(2,1)S(1)}, u32[]{:S(2)}, u32[]{:S(2)}) collective-permute-start(bf16[4,256,512]{2,1,0:T(8,128)(2,1)S(1)} %fusion.52), channel_id=1, source_target_pairs={{0,4},{4,0},{8,12},{12,8},{16,20},{20,16},{24,28},{28,24},{1,5},{5... | collective-permute-start | bytes 3145736 | tf_op jit(solution)/shard_map/ppermute | solution.py:99
  517.8 33.7 %collective-permute-start.56 = (bf16[4,64,2048]{2,1,0:T(8,128)(2,1)S(1)}, bf16[4,64,2048]{2,1,0:T(8,128)(2,1)S(1)}, u32[]{:S(2)}, u32[]{:S(2)}) collective-permute-start(bf16[4,64,2048]{2,1,0:T(8,128)(2,1)S(1)} %get-tuple-element.142), channel_id=1, source_target_pairs={{0,2},{1,3},{2,0},{3,1},{4,6},{5,7},{6,4},{7,5},{8,10},{9,11},{10,... | collective-permute-start | bytes 3145736 | tf_op jit(solution)/shard_map/ppermute | solution.py:110
  521.9 45.3 %collective-permute-start.82 = (bf16[4,512,256]{2,1,0:T(8,128)(2,1)S(1)}, bf16[4,512,256]{2,1,0:T(8,128)(2,1)S(1)}, u32[]{:S(2)}, u32[]{:S(2)}) collective-permute-start(bf16[4,512,256]{2,1,0:T(8,128)(2,1)S(1)} %fusion.54), channel_id=1, source_target_pairs={{0,4},{4,0},{8,12},{12,8},{16,20},{20,16},{24,28},{28,24},{1,5},{5... | collective-permute-start | bytes 3145736 | tf_op jit(solution)/shard_map/ppermute | solution.py:99
  526.0 42.5 %collective-permute-start.79 = (bf16[256,512]{1,0:T(8,128)(2,1)S(1)}, bf16[256,512]{1,0:T(8,128)(2,1)S(1)}, u32[]{:S(2)}, u32[]{:S(2)}) collective-permute-start(bf16[256,512]{1,0:T(8,128)(2,1)S(1)} %get-tuple-element.125), channel_id=1, source_target_pairs={{0,8},{4,12},{8,0},{12,4},{16,24},{20,28},{24,16},{28,20},{1,9},{5... | collective-permute-start | bytes 786440 | tf_op jit(solution)/shard_map/ppermute | solution.py:88
  527.8 41.8 %collective-permute-start.80 = (bf16[256,512]{1,0:T(8,128)(2,1)S(1)}, bf16[256,512]{1,0:T(8,128)(2,1)S(1)}, u32[]{:S(2)}, u32[]{:S(2)}) collective-permute-start(bf16[256,512]{1,0:T(8,128)(2,1)S(1)} %get-tuple-element.124), channel_id=1, source_target_pairs={{0,16},{4,20},{8,24},{12,28},{16,0},{20,4},{24,8},{28,12},{1,17},{... | collective-permute-start | bytes 786440 | tf_op jit(solution)/shard_map/ppermute | solution.py:88
  567.2 58.4 %collective-permute-start.57 = (bf16[4,2,64,2048]{3,2,0,1:T(8,128)(2,1)}, bf16[4,2,64,2048]{3,2,0,1:T(8,128)(2,1)}, u32[]{:S(2)}, u32[]{:S(2)}) collective-permute-start(bf16[4,2,64,2048]{3,2,0,1:T(8,128)(2,1)} %get-tuple-element.71), channel_id=1, source_target_pairs={{0,1},{1,0},{2,3},{3,2},{4,5},{5,4},{6,7},{7,6},{8,9},{9,8},{10,11... | collective-permute-start | bytes 6291464 | tf_op jit(solution)/shard_map/ppermute | solution.py:110
  571.7 34.7 %collective-permute-start.83 = (bf16[512,256]{1,0:T(8,128)(2,1)}, bf16[512,256]{1,0:T(8,128)(2,1)}, u32[]{:S(2)}, u32[]{:S(2)}) collective-permute-start(bf16[512,256]{1,0:T(8,128)(2,1)} %get-tuple-element.117), channel_id=1, source_target_pairs={{0,8},{4,12},{8,0},{12,4},{16,24},{20,28},{24,16},{28,20},{1,9},{5... | collective-permute-start | bytes 786440 | tf_op jit(solution)/shard_map/ppermute | solution.py:88
  575.6 36.9 %collective-permute-start.84 = (bf16[512,256]{1,0:T(8,128)(2,1)}, bf16[512,256]{1,0:T(8,128)(2,1)}, u32[]{:S(2)}, u32[]{:S(2)}) collective-permute-start(bf16[512,256]{1,0:T(8,128)(2,1)} %get-tuple-element.116), channel_id=1, source_target_pairs={{0,16},{4,20},{8,24},{12,28},{16,0},{20,4},{24,8},{28,12},{1,17},{... | collective-permute-start | bytes 786440 | tf_op jit(solution)/shard_map/ppermute | solution.py:88
  625.6 50.2 %collective-permute-start.42 = (bf16[2,64,2048]{2,1,0:T(8,128)(2,1)}, bf16[2,64,2048]{2,1,0:T(8,128)(2,1)}, u32[]{:S(2)}, u32[]{:S(2)}) collective-permute-start(bf16[2,64,2048]{2,1,0:T(8,128)(2,1)} %get-tuple-element.228), channel_id=1, source_target_pairs={{0,1},{1,0},{2,3},{3,2},{4,5},{5,4},{6,7},{7,6},{8,9},{9,8},{10,11... | collective-permute-start | bytes 1572872 | tf_op jit(solution)/shard_map/ppermute | solution.py:110
  667.7 39.1 %collective-permute-start.59 = (bf16[4,2,64,2048]{3,2,0,1:T(8,128)(2,1)S(1)}, bf16[4,2,64,2048]{3,2,0,1:T(8,128)(2,1)S(1)}, u32[]{:S(2)}, u32[]{:S(2)}) collective-permute-start(bf16[4,2,64,2048]{3,2,0,1:T(8,128)(2,1)S(1)} %bitcast.726), channel_id=1, source_target_pairs={{0,1},{1,0},{2,3},{3,2},{4,5},{5,4},{6,7},{7,6},{8,9},{9,8},{10,11... | collective-permute-start | bytes 6291464 | tf_op jit(solution)/shard_map/ppermute | solution.py:110
  (171 other events, 1921.8 us)

commit v2 on v0

v2 whole, which is shorter than its diff:
```python
import functools
import math

import jax
import jax.numpy as jnp
from jax import lax
from jax.experimental import pallas as pl
from jax.experimental.pallas import tpu as pltpu
from jax.sharding import PartitionSpec as P

HD = 128
EPSILON = 1e-05
ROPE_BASE = 10000.0
LOG_BIAS = math.log(4096.0)
LOW = jnp.bfloat16
F32 = jnp.float32
G_ATTN_X = [("x0", "x1"), ("x0", "x1"), ("x0", "x2"), ("x0", "x2")]
G_TOP = (("start", "x0"), ("x2", "attend"), ("qkv", "z0"), ("z0", "z1"))
G_MLP_Z = [("x1", "x2"), ("x2", "z0"), ("kv", "z2")]
G_MLP_X = [("attend", "z2"), ("z1", "h1"), ("z2", "h2"), ("h0", "mlp")]
G_MLPG_X = [("turn", "r1"), ("m0", "m2"), ("g2", "m1"), ("g1", "m0")]
G_MLPG_Z = [("turn", "r2"), ("back", "r1"), ("m1", "turn")]
G_OUT = (("g1", "g2"), ("g2", "m0"), ("m0", "m1"), ("in", "end"))
G_ATTNG_X = [("r1", "in")] * 4
G_ATTNG_Z = [("in", "end")] * 3
VMEM_ASK = 40 * 1024 * 1024


def dot(left_mat, right_mat):
    return lax.dot_general(
        left_mat, right_mat, (((1,), (0,)), ((), ())), preferred_element_type=F32
    )


def dot_last(left_mat, right_mat):
    return lax.dot_general(
        left_mat, right_mat, (((1,), (1,)), ((), ())), preferred_element_type=F32
    )


def dot_first(left_mat, right_mat):
    return lax.dot_general(
        left_mat, right_mat, (((0,), (0,)), ((), ())), preferred_element_type=F32
    )


def inv_rms(values):
    return lax.rsqrt(jnp.mean(values * values, axis=-1, keepdims=True) + EPSILON)


def norm_back(grad_normed, normed, inv_root):
    return inv_root * (
        grad_normed - normed * jnp.mean(grad_normed * normed, axis=-1, keepdims=True)
    )


class Flow:
    def __init__(self):
        self.plans, self.got, self.due = {}, {}, {}

    def plan(self, name, start, end, make, send):
        self.plans.setdefault(start, []).append((name, end, make, send))

    def gate(self, label, values):
        values, ended = list(values), self.due.pop(label, [])
        planned = self.plans.pop(label, [])
        tied = list(
            lax.optimization_barrier(
                tuple(values) + tuple(ended) + tuple(make() for _, _, make, _ in planned)
            )
        )
        for (name, end, _, send), operand in zip(planned, tied[len(values) + len(ended) :]):
            result = self.got[name] = send(operand)
            self.due.setdefault(end, []).extend(result if isinstance(result, list) else [result])
        return tied[: len(values)]


def shape_of(rows, cols, kind):
    return jax.ShapeDtypeStruct((rows, cols), kind)


def at_rows(index, count):
    return pl.ds(pl.multiple_of(index * count, count), count)


SMEM_SPEC = pl.BlockSpec(memory_space=pltpu.SMEM)
ANY_SPEC = pl.BlockSpec(memory_space=pl.ANY)
VMEM_SPEC = pl.BlockSpec(memory_space=pltpu.VMEM)


def call(body, outs, scalars, arrays, scratch=(), space=VMEM_SPEC, flops=0):
    outs = tuple(outs)
    moved = sum(math.prod(a.shape) * a.dtype.itemsize for a in tuple(arrays) + outs)
    return pl.pallas_call(
        body,
        out_shape=outs,
        in_specs=[SMEM_SPEC] + [space] * len(arrays),
        out_specs=tuple([space] * len(outs)),
        scratch_shapes=list(scratch),
        compiler_params=pltpu.CompilerParams(vmem_limit_bytes=VMEM_ASK),
        cost_estimate=pl.CostEstimate(flops=flops, bytes_accessed=moved, transcendentals=0),
    )(scalars, *arrays)


def place(scalars, pieces, spots, rows, widths):
    count, many = len(pieces), len(widths)
    height = pieces[0].shape[0]

    def body(at, *refs):
        ins, outs, sems = refs[:count], refs[count:-1], refs[-1]
        copies = []
        for n in range(count):
            where, start = at_rows(spots[n](at), height), 0
            for m, breadth in enumerate(widths):
                copies.append(
                    pltpu.make_async_copy(
                        ins[n].at[:, start : start + breadth], outs[m].at[where, :], sems.at[n * many + m]
                    )
                )
                start += breadth
        for copy in copies:
            copy.start()
        for copy in copies:
            copy.wait()

    return call(
        body,
        [shape_of(rows, breadth, pieces[0].dtype) for breadth in widths],
        scalars,
        pieces,
        [pltpu.SemaphoreType.DMA((count * many,))],
        ANY_SPEC,
    )


def place_wide(scalars, pieces, spots, rows, cols, kind=F32):
    count = len(pieces)

    def body(at, *refs):
        out = refs[count]
        for n in range(count):
            out[at_rows(spots[n](at), pieces[n].shape[0]), :] = refs[n][...].astype(kind)

    return call(body, [shape_of(rows, cols, kind)], scalars, pieces)[0]


def finish_weights(scalars, pieces, weights, gain, spots):
    count, many = len(pieces), len(weights)
    height, breadth = weights[0].shape
    block = pieces[0].shape[1] // (many + 1)

    def body(at, *refs):
        ins, held, gains = refs[:count], refs[count : count + many], refs[count + many]
        outs, turned, terms = refs[count + many + 1 : -2], refs[-2], refs[-1]
        total = jnp.zeros((height, 1), F32)
        scale = gains[...]
        for n in range(count):
            where = at_rows(spots[n](at), block)
            for m in range(many):
                grad = ins[n][:, m * block : (m + 1) * block].astype(F32)
                outs[m][:, where] = grad * scale
                total += jnp.sum(grad * held[m][:, where].astype(F32), axis=1, keepdims=True)
            turned[where, :] = ins[n][:, many * block :].astype(F32).T
        terms[...] = total

    outs = [shape_of(height, breadth, F32) for _ in weights]
    outs += [shape_of(breadth, height, F32), shape_of(height, 1, F32)]
    return call(body, outs, scalars, list(pieces) + list(weights) + [gain])


def turn(values, cosine, signed):
    return values * cosine + pltpu.roll(values, HD // 2, 1) * signed


def piece_spots(far, head_size, own):
    for c in range(2):
        row = 0
        for first in (0, far // 2):
            for y in range(head_size // 2):
                for k in range(first, first + far // 2):
                    yield c, row, k, 2 * y + c
                    row += own


def rotate_all(scalars, chunks, cosine, signed, far, head_size, own):
    tok = own * head_size

    def body(at, low_ref, high_ref, cos_ref, sin_ref, query_ref, kv_ref):
        ins = (low_ref, high_ref)
        for c, row, k, m in piece_spots(far, head_size, own):
            spot = pl.ds(
                pl.multiple_of((at[0] ^ k) * tok + (at[1] ^ m) * own, own), own
            )
            cos_rows, sin_rows = cos_ref[spot, :], sin_ref[spot, :]
            value = ins[c][row : row + own, :]
            query_ref[spot, :] = turn(value[:, :HD], cos_rows, sin_rows).astype(LOW)
            kv_ref[spot, :HD] = turn(value[:, HD : 2 * HD], cos_rows, sin_rows).astype(LOW)
            kv_ref[spot, HD:] = value[:, 2 * HD :].astype(LOW)

    rows = far * tok
    return call(
        body,
        [shape_of(rows, HD, LOW), shape_of(rows, 2 * HD, LOW)],
        scalars,
        list(chunks) + [cosine, signed],
    )


def live_pairs(at, groups, far, tok):
    for i in range(far):
        for g in range(groups):
            for j in range(i + 1):
                yield i, g, j


def probabilities(at, query, key, query_doc, key_doc, i, g, j, groups):
    scores = lax.dot_general(query, key, (((1,), (1,)), ((), ())), preferred_element_type=F32)
    live = query_doc == key_doc
    if i == j:
        if g == 0:
            rows = lax.broadcasted_iota(jnp.int32, scores.shape, 0)
            cols = lax.broadcasted_iota(jnp.int32, scores.shape, 1)
            live = live & (rows >= cols)
        else:
            source = lax.rem(at[2] - g + groups, groups)
            live = live & (query_doc >= jnp.where(source < at[2], 0, 1 << 30))
    return jnp.where(live, jax.nn.sigmoid(scores * HD**-0.5 - LOG_BIAS), 0.0)


def attend(scalars, query, keys, query_doc, key_doc, far, head_size, own):
    tok, groups = own * head_size, len(keys)

    def body(at, query_ref, doc_ref, key_doc_ref, *refs):
        key_refs, (low_ref, high_ref, held) = refs[:groups], refs[groups:]
        for i in range(far):
            block = query_ref[i * tok : (i + 1) * tok, :]
            docs = doc_ref[i * tok : (i + 1) * tok, :]
            total = jnp.zeros((tok, HD), F32)
            for j in range(i + 1):
                for g in range(groups):
                    span = slice(j * tok, (j + 1) * tok)
                    probs = probabilities(
                        at, block, key_refs[g][span, :HD], docs, key_doc_ref[g : g + 1, span], i, g, j, groups
                    )
                    total += dot(probs.astype(LOW), key_refs[g][span, HD:])
            held[i * tok : (i + 1) * tok, :] = total.astype(LOW)
        outs = (low_ref, high_ref)
        for c, row, k, m in piece_spots(far, head_size, own):
            spot = pl.ds(
                pl.multiple_of((at[0] ^ k) * tok + (at[1] ^ m) * own, own), own
            )
            outs[c][row : row + own, :] = held[spot, :]

    rows = far * tok
    return call(
        body,
        [shape_of(rows // 2, HD, LOW)] * 2,
        scalars,
        [query, query_doc, key_doc] + list(keys),
        [pltpu.VMEM((rows, HD), LOW)],
        flops=4 * rows * rows * groups * HD // 2,
    )


def attend_back(scalars, query, keys, query_doc, key_doc, grads, far, head_size, own):
    tok, groups = own * head_size, len(keys)

    def body(at, query_ref, doc_ref, key_doc_ref, low_ref, high_ref, *refs):
        key_refs, outs, held = refs[:groups], refs[groups:-1], refs[-1]
        query_out, key_outs = outs[0], outs[1:]
        ins = (low_ref, high_ref)
        for c, row, k, m in piece_spots(far, head_size, own):
            spot = pl.ds(
                pl.multiple_of((at[0] ^ k) * tok + (at[1] ^ m) * own, own), own
            )
            held[spot, :] = ins[c][row : row + own, :]
        for j in range(far):
            for g in range(groups):
                span = slice(j * tok, (j + 1) * tok)
                key, value = key_refs[g][span, :HD], key_refs[g][span, HD:]
                key_total = jnp.zeros((tok, HD), F32)
                value_total = jnp.zeros((tok, HD), F32)
                for i in range(j, far):
                    rows = slice(i * tok, (i + 1) * tok)
                    block, grad = query_ref[rows, :], held[rows, :]
                    probs = probabilities(
                        at, block, key, doc_ref[rows, :], key_doc_ref[g : g + 1, span], i, g, j, groups
                    )
                    value_total += dot_first(probs.astype(LOW), grad)
                    terms = (dot_last(grad, value) * probs * (1.0 - probs)).astype(LOW)
                    key_total += dot_first(terms, block)
                    part = dot(terms, key) * HD**-0.5
                    if j == 0 and g == 0:
                        query_out[rows, :] = part
                    else:
                        query_out[rows, :] += part
                kind = key_outs[g].dtype
                key_outs[g][span, :HD] = (key_total * HD**-0.5).astype(kind)
                key_outs[g][span, HD:] = value_total.astype(kind)

    rows = far * tok
    return call(
        body,
        [shape_of(rows, HD, F32), shape_of(rows, 2 * HD, F32)]
        + [shape_of(rows, 2 * HD, LOW)] * (groups - 1),
        scalars,
        [query, query_doc, key_doc] + list(grads) + list(keys),
        [pltpu.VMEM((rows, HD), LOW)],
        flops=10 * rows * rows * groups * HD // 2,
    )


def rotate_back(scalars, query, keys, cosine, signed, far, head_size, own):
    tok, count = own * head_size, len(keys)

    def body(at, query_ref, cos_ref, sin_ref, *refs):
        key_refs, outs = refs[:count], refs[count:]
        for c, row, k, m in piece_spots(far, head_size, own):
            spot = pl.ds(
                pl.multiple_of((at[0] ^ k) * tok + (at[1] ^ m) * own, own), own
            )
            cos_rows, sin_rows = cos_ref[spot, :], -sin_ref[spot, :]
            total = key_refs[0][spot, :]
            for ref in key_refs[1:]:
                total += ref[spot, :].astype(F32)
            rows = slice(row, row + own)
            outs[c][rows, :HD] = turn(query_ref[spot, :], cos_rows, sin_rows).astype(LOW)
            outs[c][rows, HD : 2 * HD] = turn(total[:, :HD], cos_rows, sin_rows).astype(LOW)
            outs[c][rows, 2 * HD :] = total[:, HD:].astype(LOW)

    rows = far * tok
    return call(
        body,
        [shape_of(rows // 2, 3 * HD, LOW)] * 2,
        scalars,
        [query, cosine, signed] + list(keys),
    )


def local(
    layer_in,
    out_grad,
    doc_ids,
    attn_gain,
    query_weight,
    key_weight,
    value_weight,
    proj_weight,
    mlp_gain,
    gate_weight,
    up_weight,
    down_weight,
):
    tok, width = layer_in.shape
    seq_size, head_size = lax.axis_size("seq"), lax.axis_size("head")
    far = query_weight.shape[1] // HD
    groups = seq_size // far
    own = tok // head_size
    seq_at, head_at = lax.axis_index("seq"), lax.axis_index("head")
    far_at, group_at = seq_at // groups, seq_at % groups
    scalars = jnp.stack([far_at, head_at, group_at]).astype(jnp.int32)
    rows_s = width // seq_size
    hidden = gate_weight.shape[1] // far
    tok_group = far * tok

    def far_swap(value, step):
        return lax.ppermute(
            value,
            "seq",
            [(i * groups + g, (i ^ step) * groups + g) for i in range(far) for g in range(groups)],
        )

    def gather_far(piece):
        return [piece] + [far_swap(piece, k) for k in range(1, far)]

    def scatter_far(parts):
        total = parts[0].astype(F32)
        for k in reversed(range(1, far)):
            total = total + far_swap(parts[k].astype(LOW), k).astype(F32)
        return total

    def group_shift(value, step):
        return lax.ppermute(
            value,
            "seq",
            [
                (i * groups + g, i * groups + (g + step) % groups)
                for i in range(far)
                for g in range(groups)
            ],
        )

    def head_swap(value, step):
        return lax.ppermute(value, "head", [(i, i ^ step) for i in range(head_size)])

    flow = Flow()
    gate, plan, got = flow.gate, flow.plan, flow.got
    half_far = far // 2
    many_rows = half_far * own

    def core_swap(value):
        parts = [value[i : i + own] for i in range(0, value.shape[0], own)]
        return jnp.concatenate([head_swap(part, 1) for part in parts])

    def gather_rows(labels, piece):
        (piece,) = gate(labels[0], [piece])
        parts = gather_far(piece)
        near = jnp.concatenate(
            parts[:half_far] + [head_swap(part, 2) for part in parts[:half_far]]
        )
        rest = jnp.concatenate(parts[half_far:])
        near, rest = gate(labels[1], [near, rest])
        rest = jnp.concatenate([rest, head_swap(rest, 2)])
        near_got = core_swap(near)
        near, rest, near_got = gate(labels[2], [near, rest, near_got])
        return [
            jnp.concatenate([near, rest]),
            jnp.concatenate([near_got, core_swap(rest)]),
        ]

    def split_rows(chunks):
        return [[c[: 2 * many_rows], c[2 * many_rows :]] for c in chunks]

    def scatter_rows(labels, chunks):
        mine, other = split_rows(chunks)
        *mine, other[0], other[1] = gate(labels[0], mine + other)
        half = mine[1].astype(F32) + core_swap(other[1]).astype(F32)
        kept, sent, *left = gate(
            labels[1], [half[:many_rows], half[many_rows:].astype(LOW), mine[0], other[0]]
        )
        near = left[0].astype(F32) + core_swap(left[1]).astype(F32)
        rest = kept + head_swap(sent, 2).astype(F32)
        near, near_sent, rest = gate(
            labels[2], [near[:many_rows], near[many_rows:].astype(LOW), rest]
        )
        near = near + head_swap(near_sent, 2).astype(F32)
        return scatter_far(
            [part[k * own : (k + 1) * own] for part in (near, rest) for k in range(half_far)]
        )

    def plan_gather(tag, piece, far_gates, near_gates, rest_gates, core_gates):
        plan((tag, "far"), *far_gates, lambda: piece, gather_far)
        halves = (("near", range(half_far), near_gates), ("rest", range(half_far, far), rest_gates))
        for name, ks, gates in halves:
            plan(
                (tag, name),
                *gates,
                lambda ks=ks: jnp.concatenate([got[tag, "far"][k] for k in ks]),
                lambda v: head_swap(v, 2),
            )

            def both(name=name, ks=ks):
                return jnp.concatenate([got[tag, "far"][k] for k in ks] + [got[tag, name]])

            plan((tag, name, "core"), *core_gates, both, core_swap)

        def finish():
            parts = got[tag, "far"]
            mine = parts[:half_far] + [got[tag, "near"]] + parts[half_far:] + [got[tag, "rest"]]
            other = [got[tag, "near", "core"], got[tag, "rest", "core"]]
            return [jnp.concatenate(mine), jnp.concatenate(other)]

        return finish

    def plan_scatter(tag, chunks, core_gates, rest_gates, near_gates, far_gates):
        mine, other = split_rows(chunks)

        def half(n):
            return mine[n].astype(F32) + got[tag, "core", n].astype(F32)

        def part(k):
            n, at = k // half_far, k % half_far * own
            value = half(n)[:many_rows] + got[tag, "head", n].astype(F32)
            return value[at : at + own].astype(LOW)

        for n, gates in ((1, rest_gates), (0, near_gates)):
            plan((tag, "core", n), *core_gates, lambda n=n: other[n], core_swap)
            plan(
                (tag, "head", n),
                *gates,
                lambda n=n: half(n)[many_rows:].astype(LOW),
                lambda v: head_swap(v, 2),
            )
        plan(
            (tag, "far"),
            *far_gates,
            lambda: jnp.stack([part(k) for k in range(far)]),
            lambda v: scatter_far([v[k] for k in range(far)]),
        )
        return lambda: got[tag, "far"]

    steps = [(k, g) for k in range(far) for g in range(groups)]

    def source_of(k, g):
        return lambda at: (at[0] ^ k) * groups + lax.rem(at[2] + groups - g, groups)

    def plan_weights(tag, block_of, far_gates, group_gates):
        got[tag, 0, 0] = block_of(far_at)
        for k in range(far):
            if k:
                plan(
                    (tag, k, 0),
                    *far_gates[k],
                    lambda k=k: block_of(far_at ^ k),
                    lambda v, k=k: far_swap(v, k),
                )
            for g in range(1, groups):
                plan(
                    (tag, k, g),
                    *group_gates[k],
                    lambda k=k: got[tag, k, 0],
                    lambda v, g=g: group_shift(v, g),
                )

    def place_weights(tag, widths):
        pieces = [got[tag, k, g] for k, g in steps]
        return place(scalars, pieces, [source_of(*s) for s in steps], width, widths)

    def plan_grads(tag, grads, group_gates, far_gates):
        def rows(at):
            return jnp.concatenate(
                [lax.dynamic_slice_in_dim(v, at * rows_s, rows_s, 0) for v in grads], axis=1
            )

        def total(k):
            value = rows((far_at ^ k) * groups + group_at)
            for g in range(1, groups):
                value = value + got[tag, "x", k, g].astype(F32)
            return value.astype(LOW)

        for k in reversed(range(far)):
            for g in range(1, groups):
                plan(
                    (tag, "x", k, g),
                    *group_gates[k],
                    lambda k=k, g=g: rows((far_at ^ k) * groups + (group_at + g) % groups).astype(LOW),
                    lambda v, g=g: group_shift(v, g),
                )
            if k:
                plan((tag, k), *far_gates[k], lambda k=k: total(k), lambda v, k=k: far_swap(v, k))

        return lambda: [got[tag, k] if k else total(0) for k in range(far)]

    far_spots = [(lambda at, k=k: at[0] ^ k) for k in range(far)]
    head_spots = [(lambda at, m=m: at[1] ^ m) for m in (0, 2, 1, 3)]

    def every_row(piece):
        half = [piece, head_swap(piece, 2)]
        return half + [head_swap(part, 1) for part in half]

    def head_sum(value):
        value = value + head_swap(value, 1)
        return value + head_swap(value, 2)

    gain_a = attn_gain.astype(F32)[:, None]
    gain_b = mlp_gain.astype(F32)[:, None]

    def weight_block(weights, gain, turned, breadth):
        turned = turned.T

        def block_of(i):
            def columns(w):
                return lax.dynamic_slice_in_dim(w, i * breadth, breadth, 1)

            parts = [(columns(w).astype(F32) * gain).astype(LOW) for w in weights]
            return jnp.concatenate(parts + [columns(turned)], axis=1)

        return block_of

    own_in = lax.dynamic_slice_in_dim(layer_in, head_at * own, own, 0).astype(F32)
    own_grad = lax.dynamic_slice_in_dim(out_grad, head_at * own, own, 0)
    inv_a = inv_rms(own_in)
    normed_a = own_in * inv_a
    plan_weights(
        "attn",
        weight_block((query_weight, key_weight, value_weight), gain_a, proj_weight, HD),
        [None] + [("start", "x0")] * 3,
        G_ATTN_X,
    )
    finish_top = plan_gather(
        "top", own_grad, *G_TOP
    )
    plan_weights(
        "mlp",
        weight_block((gate_weight, up_weight), gain_b, down_weight, hidden),
        [None] + G_MLP_Z,
        G_MLP_X,
    )
    got["x"] = gate("start", [normed_a.astype(LOW)])[0]
    hidden_a = gather_rows(("x0", "x1", "x2"), got["x"])
    qkv_full, proj_turned = place_weights("attn", (3 * HD, HD))

    far_ids = jnp.arange(far, dtype=jnp.int32)
    positions = (far_ids * groups + group_at)[:, None] * tok + jnp.arange(tok, dtype=jnp.int32)
    frequency = ROPE_BASE ** (-jnp.arange(HD // 2, dtype=F32) * 2.0 / HD)
    angles = positions.reshape(tok_group).astype(F32)[:, None] * frequency[None, :]
    cosine, sine_tab = jnp.cos(angles), jnp.sin(angles)
    cosine = jnp.concatenate([cosine, cosine], axis=1)
    signed = jnp.concatenate([-sine_tab, sine_tab], axis=1)
    docs = doc_ids.reshape(far, groups, tok)
    query_doc = lax.dynamic_index_in_dim(docs, group_at, 1, keepdims=False).reshape(tok_group, 1)
    key_doc = jnp.stack(
        [
            lax.dynamic_index_in_dim(docs, (group_at - g) % groups, 1, keepdims=False).reshape(
                tok_group
            )
            for g in range(groups)
        ]
    )
    hidden_a = gate("qkv", hidden_a)
    query_rot, key_own = rotate_all(
        scalars, [dot(h, qkv_full) for h in hidden_a], cosine, signed, far, head_size, own
    )
    key_own, query_rot = gate("kv", [key_own, query_rot])
    keys = [key_own] + [group_shift(key_own, g) for g in range(1, groups)]

    query_rot, *keys = gate("attend", [query_rot] + keys)
    attn_low = attend(scalars, query_rot, keys, query_doc, key_doc, far, head_size, own)
    middle = own_in + scatter_rows(("z0", "z1", "z2"), [dot_last(a, proj_turned).astype(LOW) for a in attn_low])

    inv_b = inv_rms(middle)
    normed_b = middle * inv_b
    hidden_b = gather_rows(("h0", "h1", "h2"), normed_b.astype(LOW))
    hidden_b = gate("mlp", hidden_b)
    gate_up, down_turned = place_weights("mlp", (2 * hidden, hidden))
    grad_top = finish_top()
    active, grad_gu = [], []
    for h, top in zip(hidden_b, grad_top):
        gate_up_val = dot(h, gate_up)
        gate_val, up_val = gate_up_val[:, :hidden], gate_up_val[:, hidden:]
        gate_sig = jax.nn.sigmoid(gate_val)
        silu_val = gate_val * gate_sig
        active.append((silu_val * up_val).astype(LOW))
        grad_active = dot(top, down_turned)
        grad_gu.append(
            jnp.concatenate(
                [
                    (
                        grad_active * up_val * gate_sig * (1.0 + gate_val * (1.0 - gate_sig))
                    ).astype(LOW),
                    (grad_active * silu_val).astype(LOW),
                ],
                axis=1,
            )
        )
    def over_tokens(left_mats, right_mats):
        return sum(dot_first(a, b) for a, b in zip(left_mats, right_mats))

    grad_gu = gate("mlp done", grad_gu)
    finish_out = plan_scatter(
        "out",
        [dot_last(a, down_turned).astype(LOW) for a in active],
        *G_OUT,
    )
    finish_mlp = plan_grads(
        "mlp grads",
        [over_tokens(hidden_b, grad_gu), over_tokens(grad_top, active)],
        G_MLPG_X,
        [None] + G_MLPG_Z,
    )
    grad_normed_b = scatter_rows(
        ("g0", "g1", "g2"), [dot_last(g, gate_up).astype(LOW) for g in grad_gu]
    )
    grad_middle = own_grad.astype(F32) + norm_back(grad_normed_b, normed_b, inv_b)
    grad_mix = gather_rows(("m0", "m1", "m2"), grad_middle.astype(LOW))

    grad_mix = gate("back", grad_mix)
    grad_attn = [dot(g, proj_turned).astype(LOW) for g in grad_mix]
    grad_query, *grad_keys = attend_back(
        scalars, query_rot, keys, query_doc, key_doc, grad_attn, far, head_size, own
    )
    grad_query, *grad_keys = gate("kvb", [grad_query] + grad_keys)
    grad_keys = [grad_keys[0]] + [
        group_shift(grad_keys[g], groups - g) for g in range(1, groups)
    ]
    grad_query, *grad_keys = gate("turn", [grad_query] + grad_keys)
    grad_qkv = rotate_back(
        scalars, grad_query, grad_keys, cosine, signed, far, head_size, own
    )
    finish_attn = plan_grads(
        "attn grads",
        [over_tokens(hidden_a, grad_qkv), over_tokens(grad_mix, attn_low)],
        G_ATTNG_X,
        [None] + G_ATTNG_Z,
    )
    grad_normed_a = scatter_rows(
        ("r0", "r1", "r2"), [dot_last(g, qkv_full).astype(LOW) for g in grad_qkv]
    )
    grad_in = (grad_middle + norm_back(grad_normed_a, normed_a, inv_a)).astype(LOW)

    (grad_in,) = gate("in", [grad_in])
    in_rows = every_row(grad_in)
    in_rows = gate("end", in_rows)
    out_rows = every_row((middle + finish_out()).astype(LOW))
    grad_gate, grad_up, grad_down, mlp_terms = finish_weights(
        scalars, finish_mlp(), [gate_weight, up_weight], gain_b, far_spots
    )
    grad_query_w, grad_key_w, grad_value_w, grad_proj, attn_terms = finish_weights(
        scalars, finish_attn(), [query_weight, key_weight, value_weight], gain_a, far_spots
    )
    layer_out = place_wide(scalars, out_rows, head_spots, tok, width, LOW)
    input_grad = place_wide(scalars, in_rows, head_spots, tok, width)
    terms = head_sum(jnp.concatenate([attn_terms, mlp_terms], axis=1).T)
    return (
        layer_out,
        input_grad,
        grad_query_w,
        grad_key_w,
        grad_value_w,
        grad_proj,
        grad_gate,
        grad_up,
        grad_down,
        terms[0],
        terms[1],
    )


def solution(mesh):
    return jax.shard_map(
        local,
        mesh=mesh,
        in_specs=(
            P("seq", None),
            P("seq", None),
            P(),
            P("seq"),
            P("seq", "head"),
            P("seq", "head"),
            P("seq", "head"),
            P("head", "seq"),
            P("seq"),
            P("seq", "head"),
            P("seq", "head"),
            P("head", "seq"),
        ),
        out_specs=(
            P("seq", None),
            P("seq", None),
            P("seq", "head"),
            P("seq", "head"),
            P("seq", "head"),
            P("head", "seq"),
            P("seq", "head"),
            P("seq", "head"),
            P("head", "seq"),
            P("seq"),
            P("seq"),
        ),
        check_vma=False,
    )
```

time: 2370 us -> 593 us (0.25)
  waiting for transfers between devices: 2090 us -> 286 us
  starting transfers between devices: 1.1 us -> 143 us
  matrix products: 130 us -> 45.2 us
  blocking collectives: 78 us -> 0 us
  Pallas kernels: 0 us -> 25.8 us
    reduce_scatter x9 -> x0, waiting for transfers between devices: 1350 us -> none  [the longest x1 287 us: local(): lax.psum_scatter(gate_term, 'seq', scatter_dimension=0, tiled=True)]
    all_gather x9 -> x0, waiting for transfers between devices: 628 us -> none  [the longest x1 124 us: local(): lax.all_gather(gate_weight, 'seq', axis=0, tiled=True)]
    ppermute x0 -> x145, waiting for transfers between devices: none -> 286 us  [the longest x36 163 us: far_swap(): lax.ppermute(value, 'seq', [(i * groups + g, (i ^ step) * groups + g) for...]
    ppermute x0 -> x145, starting transfers between devices: none -> 143 us  [the longest x36 75.7 us: far_swap(): lax.ppermute(value, 'seq', [(i * groups + g, (i ^ step) * groups + g) for...]
    psum x3 -> x0, waiting for transfers between devices: 114 us -> none  [the longest x1 84 us: local(): lax.psum(jnp.dot(active, down_full, preferred_element_type=jnp.float32),...]
    dot_general x19 -> x8, matrix products: 64.9 us -> 13.7 us  [dot(): lax.dot_general(left_mat, right_mat, (((1,), (0,)), ((), ())), preferred_...]
    all_gather x2 -> x0, blocking collectives: 40.1 us -> none  [the longest x1 22.2 us: local(): lax.all_gather(attn_gain, 'seq', axis=0, tiled=True)]
    unnamed x1 -> x0, blocking collectives: 37.9 us -> none
  transfers between devices with their start and end apart: 21 -> 145, of which waited for: 20 -> 62; matrix products, arithmetic and copies ran while one was open for 3% -> 13% of each run, Pallas kernels for 0% -> 4%
where the time goes in v2:
time: 593 us; the launch traced here: 587 us
  waiting for transfers between devices  286 us (48%)
  starting transfers between devices  143 us (24%)
  matrix products  45.2 us (8%)
  local copies, waits for them, and re-layouts  43.3 us (7%)
  other arithmetic  41 us (7%)
  Pallas kernels  25.8 us (4%)
    ppermute x36, waiting for transfers between devices, far_swap(): lax.ppermute(value, 'seq', [(i * groups + g, (i ^ step) * groups + g) for...  163 us
    ppermute x91, waiting for transfers between devices, head_swap(): lax.ppermute(value, 'head', [(i, i ^ step) for i in range(head_size)])  83.3 us
    ppermute x36, starting transfers between devices, far_swap(): lax.ppermute(value, 'seq', [(i * groups + g, (i ^ step) * groups + g) for...  75.7 us
    ppermute x91, starting transfers between devices, head_swap(): lax.ppermute(value, 'head', [(i, i ^ step) for i in range(head_size)])  43.5 us
    ppermute x18, waiting for transfers between devices, group_shift(): lax.ppermute(value, 'seq', [(i * groups + g, i * groups + (g + step) % gr...  39.5 us
    pallas_call x10, Pallas kernels, call(): pl.pallas_call(body, out_shape=outs, in_specs=[SMEM_SPEC] + [space] * len...  25.8 us
    unnamed x163, local copies, waits for them, and re-layouts  24.2 us
    ppermute x18, starting transfers between devices, group_shift(): lax.ppermute(value, 'seq', [(i * groups + g, i * groups + (g + step) % gr...  23.5 us
  transfers between devices with their start and end apart: 145, of which 62 were waited for; matrix products, arithmetic and copies ran while one was open for 13% of the time, Pallas kernels for 4%

profile of v2, /device:TPU:0, one launch (start us, length us, event | category | flops | bytes accessed | tf_op | source)
XLA Modules:
  0.0 586.8 jit_solution(638140303997339978)
XLA Ops:
  10.0 5.0 collective-permute-start.5
  30.8 8.7 %collective-permute-done.refs_2_ = bf16[256,512]{1,0:T(8,128)(2,1)S(1)} collective-permute-done((bf16[256,512]{1,0:T(8,128)(2,1)}, bf16[256,512]{1,0:T(8,128)(2,1)S(1)}, u32[]{:S(2)}, u32[]{:S(2)}) %collective-permute-start) | collective-permute-done | bytes 262176 | tf_op jit(solution)/shard_map/ppermute | solution.py:367
  39.5 4.6 collective-permute-start.2
  47.2 8.3 %collective-permute-done.1.refs_4_ = bf16[256,512]{1,0:T(8,128)(2,1)} collective-permute-done((bf16[256,512]{1,0:T(8,128)(2,1)}, bf16[256,512]{1,0:T(8,128)(2,1)}, u32[]{:S(2)}, u32[]{:S(2)}) %collective-permute-start.1) | collective-permute-done | bytes 262176 | tf_op jit(solution)/shard_map/ppermute | solution.py:367
  55.5 5.3 collective-permute-start.6
  70.9 5.6 collective-permute-done.10
  77.9 8.5 %collective-permute-done.9 = bf16[64,2048]{1,0:T(8,128)(2,1)S(1)} collective-permute-done((bf16[64,2048]{1,0:T(8,128)(2,1)}, bf16[64,2048]{1,0:T(8,128)(2,1)S(1)}, u32[]{:S(2)}, u32[]{:S(2)}) %collective-permute-start.9) | collective-permute-done | bytes 262176 | tf_op jit(solution)/shard_map/ppermute | solution.py:367
  110.3 6.7 %collective-permute-done.20.refs_2_ = bf16[256,1536]{1,0:T(8,128)(2,1)S(1)} collective-permute-done((bf16[256,1536]{1,0:T(8,128)(2,1)}, bf16[256,1536]{1,0:T(8,128)(2,1)S(1)}, u32[]{:S(2)}, u32[]{:S(2)}) %collective-permute-start.20) | collective-permute-done | bytes 786464 | tf_op jit(solution)/shard_map/ppermute | solution.py:367
  135.1 6.7 %collective-permute-done.25.refs_1_ = bf16[1024,256]{1,0:T(8,128)(2,1)S(1)} collective-permute-done((bf16[1024,256]{1,0:T(8,128)(2,1)S(1)}, bf16[1024,256]{1,0:T(8,128)(2,1)S(1)}, u32[]{:S(2)}, u32[]{:S(2)}) %collective-permute-start.25) | collective-permute-done | bytes 524320 | tf_op jit(solution)/shard_map/ppermute | solution.py:383
  147.8 23.6 %collective-permute-done.27.refs_4_ = bf16[256,1536]{1,0:T(8,128)(2,1)S(1)} collective-permute-done((bf16[256,1536]{1,0:T(8,128)(2,1)S(1)}, bf16[256,1536]{1,0:T(8,128)(2,1)S(1)}, u32[]{:S(2)}, u32[]{:S(2)}) %collective-permute-start.27) | collective-permute-done | bytes 786464 | tf_op jit(solution)/shard_map/ppermute | solution.py:367
  181.5 11.9 %collective-permute-done.37 = bf16[128,2048]{1,0:T(8,128)(2,1)S(1)} collective-permute-done((bf16[128,2048]{1,0:T(8,128)(2,1)S(1)}, bf16[128,2048]{1,0:T(8,128)(2,1)S(1)}, u32[]{:S(2)}, u32[]{:S(2)}) %collective-permute-start.37) | collective-permute-done | bytes 524320 | tf_op jit(solution)/shard_map/ppermute | solution.py:394
  201.9 8.3 %collective-permute-done.40 = bf16[128,2048]{1,0:T(8,128)(2,1)S(1)} collective-permute-done((bf16[128,2048]{1,0:T(8,128)(2,1)S(1)}, bf16[128,2048]{1,0:T(8,128)(2,1)S(1)}, u32[]{:S(2)}, u32[]{:S(2)}) %collective-permute-start.40) | collective-permute-done | bytes 524320 | tf_op jit(solution)/shard_map/ppermute | solution.py:394
  215.5 7.8 %collective-permute-done.42 = bf16[64,2048]{1,0:T(8,128)(2,1)S(1)} collective-permute-done((bf16[64,2048]{1,0:T(8,128)(2,1)S(1)}, bf16[64,2048]{1,0:T(8,128)(2,1)S(1)}, u32[]{:S(2)}, u32[]{:S(2)}) %collective-permute-start.42) | collective-permute-done | bytes 262176 | tf_op jit(solution)/shard_map/ppermute | solution.py:367
  232.7 6.3 %collective-permute-done.47 = bf16[64,2048]{1,0:T(8,128)(2,1)S(1)} collective-permute-done((bf16[64,2048]{1,0:T(8,128)(2,1)S(1)}, bf16[64,2048]{1,0:T(8,128)(2,1)S(1)}, u32[]{:S(2)}, u32[]{:S(2)}) %collective-permute-start.47) | collective-permute-done | bytes 262176 | tf_op jit(solution)/shard_map/ppermute | solution.py:367
  241.7 11.2 %collective-permute-done.50 = bf16[64,2048]{1,0:T(8,128)(2,1)S(1)} collective-permute-done((bf16[64,2048]{1,0:T(8,128)(2,1)S(1)}, bf16[64,2048]{1,0:T(8,128)(2,1)S(1)}, u32[]{:S(2)}, u32[]{:S(2)}) %collective-permute-start.50) | collective-permute-done | bytes 262176 | tf_op jit(solution)/shard_map/ppermute | solution.py:367
  261.7 14.7 %collective-permute-done.46.refs_7_ = bf16[256,1536]{1,0:T(8,128)(2,1)S(1)} collective-permute-done((bf16[256,1536]{1,0:T(8,128)(2,1)S(1)}, bf16[256,1536]{1,0:T(8,128)(2,1)S(1)}, u32[]{:S(2)}, u32[]{:S(2)}) %collective-permute-start.46) | collective-permute-done | bytes 786464 | tf_op jit(solution)/shard_map/ppermute | solution.py:383
  300.8 5.7 fusion.64
  345.6 6.4 %collective-permute-start.88 = (bf16[64,2048]{1,0:T(8,128)(2,1)S(1)}, bf16[64,2048]{1,0:T(8,128)(2,1)S(1)}, u32[]{:S(2)}, u32[]{:S(2)}) collective-permute-start(bf16[64,2048]{1,0:T(8,128)(2,1)S(1)} %get-tuple-element.423), channel_id=1, source_target_pairs={{0,16},{4,20},{8,24},{12,28},{16,0},{20,4},{24,8},{28,12},{1,17},{... | collective-permute-start | bytes 786440 | tf_op jit(solution)/shard_map/ppermute | solution.py:367
  357.8 6.3 %collective-permute-start.89 = (bf16[64,2048]{1,0:T(8,128)(2,1)S(1)}, bf16[64,2048]{1,0:T(8,128)(2,1)S(1)}, u32[]{:S(2)}, u32[]{:S(2)}) collective-permute-start(bf16[64,2048]{1,0:T(8,128)(2,1)S(1)} %slice.642), channel_id=1, source_target_pairs={{0,8},{4,12},{8,0},{12,4},{16,24},{20,28},{24,16},{28,20},{1,9},{5... | collective-permute-start | bytes 786440 | tf_op jit(solution)/shard_map/ppermute | solution.py:367
  381.2 4.7 collective-permute-done.92
  390.9 8.4 %collective-permute-done.95 = bf16[64,2048]{1,0:T(8,128)(2,1)S(1)} collective-permute-done((bf16[64,2048]{1,0:T(8,128)(2,1)S(1)}, bf16[64,2048]{1,0:T(8,128)(2,1)S(1)}, u32[]{:S(2)}, u32[]{:S(2)}) %collective-permute-start.95) | collective-permute-done | bytes 262176 | tf_op jit(solution)/shard_map/ppermute | solution.py:367
  405.7 10.9 %collective-permute-done.99 = bf16[128,2048]{1,0:T(8,128)(2,1)S(1)} collective-permute-done((bf16[128,2048]{1,0:T(8,128)(2,1)S(1)}, bf16[128,2048]{1,0:T(8,128)(2,1)S(1)}, u32[]{:S(2)}, u32[]{:S(2)}) %collective-permute-start.99) | collective-permute-done | bytes 524320 | tf_op jit(solution)/shard_map/ppermute | solution.py:394
  421.1 7.2 %shard_map.207 = (f32[1024,128]{1,0:T(8,128)S(1)}, f32[1024,256]{1,0:T(8,128)S(1)}, bf16[1024,256]{1,0:T(8,128)(2,1)S(1)}) custom-call(s32[3]{0:T(128)S(1)} %pad_add_fusion.1.at, bf16[1024,128]{1,0:T(8,128)(2,1)S(1)} %get-tuple-element.168.query_ref, s32[1024,1]{1,0:T(8,128)S(1)} %copy-done.9, s32[2,1024]{1,0:T(2,128)S(1)} %pad_add_fusion.key_doc_ref, ...), custom_call_target="tpu_custom_call" | custom-call | flops 1342177280 | bytes 3682304 | tf_op jit(solution)/shard_map/pallas_call | solution.py:94
  433.0 10.5 %collective-permute-done.109.refs_1_ = bf16[1024,256]{1,0:T(8,128)(2,1)S(1)} collective-permute-done((bf16[1024,256]{1,0:T(8,128)(2,1)S(1)}, bf16[1024,256]{1,0:T(8,128)(2,1)S(1)}, u32[]{:S(2)}, u32[]{:S(2)}) %collective-permute-start.109) | collective-permute-done | bytes 524320 | tf_op jit(solution)/shard_map/ppermute | solution.py:383
  456.2 18.7 %collective-permute-done.115.refs_2_ = bf16[256,1536]{1,0:T(8,128)(2,1)S(1)} collective-permute-done((bf16[256,1536]{1,0:T(8,128)(2,1)S(1)}, bf16[256,1536]{1,0:T(8,128)(2,1)S(1)}, u32[]{:S(2)}, u32[]{:S(2)}) %collective-permute-start.115) | collective-permute-done | bytes 786464 | tf_op jit(solution)/shard_map/ppermute | solution.py:367
  476.1 6.9 %collective-permute-start.122 = (bf16[256,1536]{1,0:T(8,128)(2,1)S(1)}, bf16[256,1536]{1,0:T(8,128)(2,1)S(1)}, u32[]{:S(2)}, u32[]{:S(2)}) collective-permute-start(bf16[256,1536]{1,0:T(8,128)(2,1)S(1)} %fusion.2), channel_id=1, source_target_pairs={{0,8},{4,12},{8,0},{12,4},{16,24},{20,28},{24,16},{28,20},{1,9},{5... | collective-permute-start | bytes 2359304 | tf_op jit(solution)/shard_map/ppermute | solution.py:367
  488.2 11.4 %collective-permute-done.121 = bf16[128,2048]{1,0:T(8,128)(2,1)S(1)} collective-permute-done((bf16[128,2048]{1,0:T(8,128)(2,1)S(1)}, bf16[128,2048]{1,0:T(8,128)(2,1)S(1)}, u32[]{:S(2)}, u32[]{:S(2)}) %collective-permute-start.121) | collective-permute-done | bytes 524320 | tf_op jit(solution)/shard_map/ppermute | solution.py:394
  503.9 10.2 %collective-permute-done.123 = bf16[128,2048]{1,0:T(8,128)(2,1)S(1)} collective-permute-done((bf16[128,2048]{1,0:T(8,128)(2,1)S(1)}, bf16[128,2048]{1,0:T(8,128)(2,1)S(1)}, u32[]{:S(2)}, u32[]{:S(2)}) %collective-permute-start.123) | collective-permute-done | bytes 524320 | tf_op jit(solution)/shard_map/ppermute | solution.py:394
  517.8 9.9 %collective-permute-done.125 = bf16[64,2048]{1,0:T(8,128)(2,1)S(1)} collective-permute-done((bf16[64,2048]{1,0:T(8,128)(2,1)S(1)}, bf16[64,2048]{1,0:T(8,128)(2,1)S(1)}, u32[]{:S(2)}, u32[]{:S(2)}) %collective-permute-start.125) | collective-permute-done | bytes 262176 | tf_op jit(solution)/shard_map/ppermute | solution.py:367
  543.8 4.6 collective-permute-done.133
  549.9 15.8 %collective-permute-done.132 = bf16[64,2048]{1,0:T(8,128)(2,1)} collective-permute-done((bf16[64,2048]{1,0:T(8,128)(2,1)}, bf16[64,2048]{1,0:T(8,128)(2,1)}, u32[]{:S(2)}, u32[]{:S(2)}) %collective-permute-start.132) | collective-permute-done | bytes 262176 | tf_op jit(solution)/shard_map/ppermute | solution.py:367
  568.0 6.8 %collective-permute-done.141.refs_2_ = bf16[256,512]{1,0:T(8,128)(2,1)S(1)} collective-permute-done((bf16[256,512]{1,0:T(8,128)(2,1)}, bf16[256,512]{1,0:T(8,128)(2,1)S(1)}, u32[]{:S(2)}, u32[]{:S(2)}) %collective-permute-start.141) | collective-permute-done | bytes 262176 | tf_op jit(solution)/shard_map/ppermute | solution.py:367
  (621 shorter events, 296.1 us)
Async XLA Ops:
  10.0 45.5 %collective-permute-start.5 = (bf16[64,2048]{1,0:T(8,128)(2,1)}, bf16[64,2048]{1,0:T(8,128)(2,1)}, u32[]{:S(2)}, u32[]{:S(2)}) collective-permute-start(bf16[64,2048]{1,0:T(8,128)(2,1)} %constant_dynamic-slice_fusion.24), channel_id=1, source_target_pairs={{0,24},{4,28},{8,16},{12,20},{16,8},{20,12},{24,0},{28,4},{1,25},{... | collective-permute-start | bytes 786440 | tf_op jit(solution)/shard_map/ppermute | solution.py:367
  15.0 40.5 %collective-permute-start.4 = (bf16[64,2048]{1,0:T(8,128)(2,1)}, bf16[64,2048]{1,0:T(8,128)(2,1)}, u32[]{:S(2)}, u32[]{:S(2)}) collective-permute-start(bf16[64,2048]{1,0:T(8,128)(2,1)} %constant_dynamic-slice_fusion.24), channel_id=1, source_target_pairs={{0,16},{4,20},{8,24},{12,28},{16,0},{20,4},{24,8},{28,12},{1,17},{... | collective-permute-start | bytes 786440 | tf_op jit(solution)/shard_map/ppermute | solution.py:367
  15.0 40.5 %collective-permute-start.3 = (bf16[64,2048]{1,0:T(8,128)(2,1)}, bf16[64,2048]{1,0:T(8,128)(2,1)}, u32[]{:S(2)}, u32[]{:S(2)}) collective-permute-start(bf16[64,2048]{1,0:T(8,128)(2,1)} %constant_dynamic-slice_fusion.24), channel_id=1, source_target_pairs={{0,8},{4,12},{8,0},{12,4},{16,24},{20,28},{24,16},{28,20},{1,9},{5... | collective-permute-start | bytes 786440 | tf_op jit(solution)/shard_map/ppermute | solution.py:367
  15.6 23.8 %collective-permute-start = (bf16[256,512]{1,0:T(8,128)(2,1)}, bf16[256,512]{1,0:T(8,128)(2,1)S(1)}, u32[]{:S(2)}, u32[]{:S(2)}) collective-permute-start(bf16[256,512]{1,0:T(8,128)(2,1)} %get-tuple-element.145), channel_id=1, source_target_pairs={{0,8},{4,12},{8,0},{12,4},{16,24},{20,28},{24,16},{28,20},{1,9},{5... | collective-permute-start | bytes 786440 | tf_op jit(solution)/shard_map/ppermute | solution.py:367
  17.0 38.5 %collective-permute-start.1 = (bf16[256,512]{1,0:T(8,128)(2,1)}, bf16[256,512]{1,0:T(8,128)(2,1)}, u32[]{:S(2)}, u32[]{:S(2)}) collective-permute-start(bf16[256,512]{1,0:T(8,128)(2,1)} %get-tuple-element.146), channel_id=1, source_target_pairs={{0,16},{4,20},{8,24},{12,28},{16,0},{20,4},{24,8},{28,12},{1,17},{... | collective-permute-start | bytes 786440 | tf_op jit(solution)/shard_map/ppermute | solution.py:367
  117.5 53.9 %collective-permute-start.27 = (bf16[256,1536]{1,0:T(8,128)(2,1)S(1)}, bf16[256,1536]{1,0:T(8,128)(2,1)S(1)}, u32[]{:S(2)}, u32[]{:S(2)}) collective-permute-start(bf16[256,1536]{1,0:T(8,128)(2,1)S(1)} %copy-done.49), channel_id=1, source_target_pairs={{0,16},{4,20},{8,24},{12,28},{16,0},{20,4},{24,8},{28,12},{1,17},{... | collective-permute-start | bytes 2359304 | tf_op jit(solution)/shard_map/ppermute | solution.py:367
  123.0 23.3 %collective-permute-start.28 = (bf16[128,2048]{1,0:T(8,128)(2,1)S(1)}, bf16[128,2048]{1,0:T(8,128)(2,1)S(1)}, u32[]{:S(2)}, u32[]{:S(2)}) collective-permute-start(bf16[128,2048]{1,0:T(8,128)(2,1)S(1)} %pad_maximum_fusion.27), channel_id=1, source_target_pairs={{0,2},{1,3},{2,0},{3,1},{4,6},{5,7},{6,4},{7,5},{8,10},{9,11},{10,... | collective-permute-start | bytes 1572872 | tf_op jit(solution)/shard_map/ppermute | solution.py:394
  129.6 64.0 %collective-permute-start.38 = (bf16[256,1536]{1,0:T(8,128)(2,1)S(1)}, bf16[256,1536]{1,0:T(8,128)(2,1)S(1)}, u32[]{:S(2)}, u32[]{:S(2)}) collective-permute-start(bf16[256,1536]{1,0:T(8,128)(2,1)S(1)} %copy-done.48), channel_id=1, source_target_pairs={{0,24},{4,28},{8,16},{12,20},{16,8},{20,12},{24,0},{28,4},{1,25},{... | collective-permute-start | bytes 2359304 | tf_op jit(solution)/shard_map/ppermute | solution.py:367
  179.0 47.2 %collective-permute-start.64 = (bf16[64,2048]{1,0:T(8,128)(2,1)S(1)}, bf16[64,2048]{1,0:T(8,128)(2,1)S(1)}, u32[]{:S(2)}, u32[]{:S(2)}) collective-permute-start(bf16[64,2048]{1,0:T(8,128)(2,1)S(1)} %get-tuple-element.384), channel_id=1, source_target_pairs={{0,1},{1,0},{2,3},{3,2},{4,5},{5,4},{6,7},{7,6},{8,9},{9,8},{10,11... | collective-permute-start | bytes 786440 | tf_op jit(solution)/shard_map/ppermute | solution.py:394
  179.0 35.2 %collective-permute-start.63 = (bf16[64,2048]{1,0:T(8,128)(2,1)S(1)}, bf16[64,2048]{1,0:T(8,128)(2,1)S(1)}, u32[]{:S(2)}, u32[]{:S(2)}) collective-permute-start(bf16[64,2048]{1,0:T(8,128)(2,1)S(1)} %get-tuple-element.385), channel_id=1, source_target_pairs={{0,1},{1,0},{2,3},{3,2},{4,5},{5,4},{6,7},{7,6},{8,9},{9,8},{10,11... | collective-permute-start | bytes 786440 | tf_op jit(solution)/shard_map/ppermute | solution.py:394
  223.3 30.9 %collective-permute-start.44 = (bf16[256,1536]{1,0:T(8,128)(2,1)S(1)}, bf16[256,1536]{1,0:T(8,128)(2,1)S(1)}, u32[]{:S(2)}, u32[]{:S(2)}) collective-permute-start(bf16[256,1536]{1,0:T(8,128)(2,1)S(1)} %collective-permute-done.20.refs_2_), channel_id=1, source_target_pairs={{0,4},{4,0},{8,12},{12,8},{16,20},{20,16},{24,28},{28,24},{1,5},{5... | collective-permute-start | bytes 2359304 | tf_op jit(solution)/shard_map/ppermute | solution.py:383
  228.3 24.5 %collective-permute-start.50 = (bf16[64,2048]{1,0:T(8,128)(2,1)S(1)}, bf16[64,2048]{1,0:T(8,128)(2,1)S(1)}, u32[]{:S(2)}, u32[]{:S(2)}) collective-permute-start(bf16[64,2048]{1,0:T(8,128)(2,1)S(1)} %multiply_convert_fusion.14), channel_id=1, source_target_pairs={{0,16},{4,20},{8,24},{12,28},{16,0},{20,4},{24,8},{28,12},{1,17},{... | collective-permute-start | bytes 786440 | tf_op jit(solution)/shard_map/ppermute | solution.py:367
  231.2 22.3 %collective-permute-start.48 = (bf16[64,2048]{1,0:T(8,128)(2,1)S(1)}, bf16[64,2048]{1,0:T(8,128)(2,1)S(1)}, u32[]{:S(2)}, u32[]{:S(2)}) collective-permute-start(bf16[64,2048]{1,0:T(8,128)(2,1)S(1)} %multiply_convert_fusion.14), channel_id=1, source_target_pairs={{0,2},{1,3},{2,0},{3,1},{4,6},{5,7},{6,4},{7,5},{8,10},{9,11},{10,... | collective-permute-start | bytes 786440 | tf_op jit(solution)/shard_map/ppermute | solution.py:394
  252.9 23.5 %collective-permute-start.46 = (bf16[256,1536]{1,0:T(8,128)(2,1)S(1)}, bf16[256,1536]{1,0:T(8,128)(2,1)S(1)}, u32[]{:S(2)}, u32[]{:S(2)}) collective-permute-start(bf16[256,1536]{1,0:T(8,128)(2,1)S(1)} %collective-permute-done.38.refs_6_), channel_id=1, source_target_pairs={{0,4},{4,0},{8,12},{12,8},{16,20},{20,16},{24,28},{28,24},{1,5},{5... | collective-permute-start | bytes 2359304 | tf_op jit(solution)/shard_map/ppermute | solution.py:383
  254.2 26.2 %collective-permute-start.52 = (bf16[128,2048]{1,0:T(8,128)(2,1)S(1)}, bf16[128,2048]{1,0:T(8,128)(2,1)S(1)}, u32[]{:S(2)}, u32[]{:S(2)}) collective-permute-start(bf16[128,2048]{1,0:T(8,128)(2,1)S(1)} %pad_maximum_fusion.30), channel_id=1, source_target_pairs={{0,2},{1,3},{2,0},{3,1},{4,6},{5,7},{6,4},{7,5},{8,10},{9,11},{10,... | collective-permute-start | bytes 1572872 | tf_op jit(solution)/shard_map/ppermute | solution.py:394
  257.1 22.0 %collective-permute-start.56 = (bf16[64,2048]{1,0:T(8,128)(2,1)}, bf16[64,2048]{1,0:T(8,128)(2,1)}, u32[]{:S(2)}, u32[]{:S(2)}) collective-permute-start(bf16[64,2048]{1,0:T(8,128)(2,1)} %get-tuple-element.393), channel_id=1, source_target_pairs={{0,1},{1,0},{2,3},{3,2},{4,5},{5,4},{6,7},{7,6},{8,9},{9,8},{10,11... | collective-permute-start | bytes 786440 | tf_op jit(solution)/shard_map/ppermute | solution.py:394
  344.5 23.9 %collective-permute-start.87 = (bf16[64,2048]{1,0:T(8,128)(2,1)S(1)}, bf16[64,2048]{1,0:T(8,128)(2,1)S(1)}, u32[]{:S(2)}, u32[]{:S(2)}) collective-permute-start(bf16[64,2048]{1,0:T(8,128)(2,1)S(1)} %get-tuple-element.422), channel_id=1, source_target_pairs={{0,24},{4,28},{8,16},{12,20},{16,8},{20,12},{24,0},{28,4},{1,25},{... | collective-permute-start | bytes 786440 | tf_op jit(solution)/shard_map/ppermute | solution.py:367
  345.6 25.8 %collective-permute-start.88 = (bf16[64,2048]{1,0:T(8,128)(2,1)S(1)}, bf16[64,2048]{1,0:T(8,128)(2,1)S(1)}, u32[]{:S(2)}, u32[]{:S(2)}) collective-permute-start(bf16[64,2048]{1,0:T(8,128)(2,1)S(1)} %get-tuple-element.423), channel_id=1, source_target_pairs={{0,16},{4,20},{8,24},{12,28},{16,0},{20,4},{24,8},{28,12},{1,17},{... | collective-permute-start | bytes 786440 | tf_op jit(solution)/shard_map/ppermute | solution.py:367
  352.6 27.2 %collective-permute-start.97 = (bf16[256,1536]{1,0:T(8,128)(2,1)S(1)}, bf16[256,1536]{1,0:T(8,128)(2,1)S(1)}, u32[]{:S(2)}, u32[]{:S(2)}) collective-permute-start(bf16[256,1536]{1,0:T(8,128)(2,1)S(1)} %pad_maximum_fusion.22), channel_id=1, source_target_pairs={{0,4},{4,0},{8,12},{12,8},{16,20},{20,16},{24,28},{28,24},{1,5},{5... | collective-permute-start | bytes 2359304 | tf_op jit(solution)/shard_map/ppermute | solution.py:383
  376.0 23.3 %collective-permute-start.95 = (bf16[64,2048]{1,0:T(8,128)(2,1)S(1)}, bf16[64,2048]{1,0:T(8,128)(2,1)S(1)}, u32[]{:S(2)}, u32[]{:S(2)}) collective-permute-start(bf16[64,2048]{1,0:T(8,128)(2,1)S(1)} %get-tuple-element.221), channel_id=1, source_target_pairs={{0,16},{4,20},{8,24},{12,28},{16,0},{20,4},{24,8},{28,12},{1,17},{... | collective-permute-start | bytes 786440 | tf_op jit(solution)/shard_map/ppermute | solution.py:367
  403.1 29.9 %collective-permute-start.110 = (bf16[256,1536]{1,0:T(8,128)(2,1)S(1)}, bf16[256,1536]{1,0:T(8,128)(2,1)S(1)}, u32[]{:S(2)}, u32[]{:S(2)}) collective-permute-start(bf16[256,1536]{1,0:T(8,128)(2,1)S(1)} %fusion), channel_id=1, source_target_pairs={{0,24},{4,28},{8,16},{12,20},{16,8},{20,12},{24,0},{28,4},{1,25},{... | collective-permute-start | bytes 2359304 | tf_op jit(solution)/shard_map/ppermute | solution.py:367
  431.8 43.1 %collective-permute-start.115 = (bf16[256,1536]{1,0:T(8,128)(2,1)S(1)}, bf16[256,1536]{1,0:T(8,128)(2,1)S(1)}, u32[]{:S(2)}, u32[]{:S(2)}) collective-permute-start(bf16[256,1536]{1,0:T(8,128)(2,1)S(1)} %fusion.1), channel_id=1, source_target_pairs={{0,16},{4,20},{8,24},{12,28},{16,0},{20,4},{24,8},{28,12},{1,17},{... | collective-permute-start | bytes 2359304 | tf_op jit(solution)/shard_map/ppermute | solution.py:367
  447.0 27.8 %collective-permute-start.116 = (bf16[256,1536]{1,0:T(8,128)(2,1)S(1)}, bf16[256,1536]{1,0:T(8,128)(2,1)S(1)}, u32[]{:S(2)}, u32[]{:S(2)}) collective-permute-start(bf16[256,1536]{1,0:T(8,128)(2,1)S(1)} %pad_maximum_fusion.24), channel_id=1, source_target_pairs={{0,4},{4,0},{8,12},{12,8},{16,20},{20,16},{24,28},{28,24},{1,5},{5... | collective-permute-start | bytes 2359304 | tf_op jit(solution)/shard_map/ppermute | solution.py:383
  476.1 24.6 %collective-permute-start.122 = (bf16[256,1536]{1,0:T(8,128)(2,1)S(1)}, bf16[256,1536]{1,0:T(8,128)(2,1)S(1)}, u32[]{:S(2)}, u32[]{:S(2)}) collective-permute-start(bf16[256,1536]{1,0:T(8,128)(2,1)S(1)} %fusion.2), channel_id=1, source_target_pairs={{0,8},{4,12},{8,0},{12,4},{16,24},{20,28},{24,16},{28,20},{1,9},{5... | collective-permute-start | bytes 2359304 | tf_op jit(solution)/shard_map/ppermute | solution.py:367
  484.7 30.9 %collective-permute-start.128 = (bf16[256,512]{1,0:T(8,128)(2,1)S(1)}, bf16[256,512]{1,0:T(8,128)(2,1)S(1)}, u32[]{:S(2)}, u32[]{:S(2)}) collective-permute-start(bf16[256,512]{1,0:T(8,128)(2,1)S(1)} %pad_maximum_fusion.37), channel_id=1, source_target_pairs={{0,4},{4,0},{8,12},{12,8},{16,20},{20,16},{24,28},{28,24},{1,5},{5... | collective-permute-start | bytes 786440 | tf_op jit(solution)/shard_map/ppermute | solution.py:383
  485.2 31.9 %collective-permute-start.129 = (bf16[256,512]{1,0:T(8,128)(2,1)S(1)}, bf16[256,512]{1,0:T(8,128)(2,1)S(1)}, u32[]{:S(2)}, u32[]{:S(2)}) collective-permute-start(bf16[256,512]{1,0:T(8,128)(2,1)S(1)} %pad_maximum_fusion.38), channel_id=1, source_target_pairs={{0,4},{4,0},{8,12},{12,8},{16,20},{20,16},{24,28},{28,24},{1,5},{5... | collective-permute-start | bytes 786440 | tf_op jit(solution)/shard_map/ppermute | solution.py:383
  499.5 28.7 %collective-permute-start.130 = (bf16[256,512]{1,0:T(8,128)(2,1)S(1)}, bf16[256,512]{1,0:T(8,128)(2,1)S(1)}, u32[]{:S(2)}, u32[]{:S(2)}) collective-permute-start(bf16[256,512]{1,0:T(8,128)(2,1)S(1)} %pad_maximum_fusion.39), channel_id=1, source_target_pairs={{0,4},{4,0},{8,12},{12,8},{16,20},{20,16},{24,28},{28,24},{1,5},{5... | collective-permute-start | bytes 786440 | tf_op jit(solution)/shard_map/ppermute | solution.py:383
  531.1 34.6 %collective-permute-start.132 = (bf16[64,2048]{1,0:T(8,128)(2,1)}, bf16[64,2048]{1,0:T(8,128)(2,1)}, u32[]{:S(2)}, u32[]{:S(2)}) collective-permute-start(bf16[64,2048]{1,0:T(8,128)(2,1)} %get-tuple-element.343), channel_id=1, source_target_pairs={{0,16},{4,20},{8,24},{12,28},{16,0},{20,4},{24,8},{28,12},{1,17},{... | collective-permute-start | bytes 786440 | tf_op jit(solution)/shard_map/ppermute | solution.py:367
  539.1 28.9 %collective-permute-start.140 = (bf16[256,512]{1,0:T(8,128)(2,1)}, bf16[256,512]{1,0:T(8,128)(2,1)S(1)}, u32[]{:S(2)}, u32[]{:S(2)}) collective-permute-start(bf16[256,512]{1,0:T(8,128)(2,1)} %fusion.23), channel_id=1, source_target_pairs={{0,24},{4,28},{8,16},{12,20},{16,8},{20,12},{24,0},{28,4},{1,25},{... | collective-permute-start | bytes 786440 | tf_op jit(solution)/shard_map/ppermute | solution.py:367
  541.2 33.6 %collective-permute-start.141 = (bf16[256,512]{1,0:T(8,128)(2,1)}, bf16[256,512]{1,0:T(8,128)(2,1)S(1)}, u32[]{:S(2)}, u32[]{:S(2)}) collective-permute-start(bf16[256,512]{1,0:T(8,128)(2,1)} %fusion.24), channel_id=1, source_target_pairs={{0,16},{4,20},{8,24},{12,28},{16,0},{20,4},{24,8},{28,12},{1,17},{... | collective-permute-start | bytes 786440 | tf_op jit(solution)/shard_map/ppermute | solution.py:367
  541.2 33.6 %collective-permute-start.142 = (bf16[256,512]{1,0:T(8,128)(2,1)}, bf16[256,512]{1,0:T(8,128)(2,1)S(1)}, u32[]{:S(2)}, u32[]{:S(2)}) collective-permute-start(bf16[256,512]{1,0:T(8,128)(2,1)} %fusion.25), channel_id=1, source_target_pairs={{0,8},{4,12},{8,0},{12,4},{16,24},{20,28},{24,16},{28,20},{1,9},{5... | collective-permute-start | bytes 786440 | tf_op jit(solution)/shard_map/ppermute | solution.py:367
  548.4 32.0 %collective-permute-start.137 = (bf16[64,2048]{1,0:T(8,128)(2,1)S(1)}, bf16[64,2048]{1,0:T(8,128)(2,1)S(1)}, u32[]{:S(2)}, u32[]{:S(2)}) collective-permute-start(bf16[64,2048]{1,0:T(8,128)(2,1)S(1)} %fusion.15.refs_0_), channel_id=1, source_target_pairs={{0,2},{1,3},{2,0},{3,1},{4,6},{5,7},{6,4},{7,5},{8,10},{9,11},{10,... | collective-permute-start | bytes 786440 | tf_op jit(solution)/shard_map/ppermute | solution.py:394
  (181 other events, 2035.8 us)

commit v3 on v2

--- a/solution.py
+++ b/solution.py
@@ -14,15 +14,12 @@
 LOG_BIAS = math.log(4096.0)
 LOW = jnp.bfloat16
 F32 = jnp.float32
-G_ATTN_X = [("x0", "x1"), ("x0", "x1"), ("x0", "x2"), ("x0", "x2")]
-G_TOP = (("start", "x0"), ("x2", "attend"), ("qkv", "z0"), ("z0", "z1"))
-G_MLP_Z = [("x1", "x2"), ("x2", "z0"), ("kv", "z2")]
-G_MLP_X = [("attend", "z2"), ("z1", "h1"), ("z2", "h2"), ("h0", "mlp")]
-G_MLPG_X = [("turn", "r1"), ("m0", "m2"), ("g2", "m1"), ("g1", "m0")]
-G_MLPG_Z = [("turn", "r2"), ("back", "r1"), ("m1", "turn")]
-G_OUT = (("g1", "g2"), ("g2", "m0"), ("m0", "m1"), ("in", "end"))
-G_ATTNG_X = [("r1", "in")] * 4
-G_ATTNG_Z = [("in", "end")] * 3
+G_ATTN = (("start", "x1"), ("x1", "x2"))
+G_TOP = (("z1", "z2"), ("z2", "h1"), ("h0", "h2"))
+G_MLP = (("x1", "z0"), ("z0", "h0"))
+G_GRAD_MLP = (("g1n", "m2"), ("back", "r2"))
+G_OUT = (("m0", "m1"), ("m1", "kvb"), ("m2", "kvb"), ("r2n", "end"))
+G_GRAD_ATTN = (("r1n", "r2n"), ("r2n", "end"))
 VMEM_ASK = 40 * 1024 * 1024
 
 
@@ -62,17 +59,17 @@
         self.plans.setdefault(start, []).append((name, end, make, send))
 
     def gate(self, label, values):
-        values, ended = list(values), self.due.pop(label, [])
         planned = self.plans.pop(label, [])
-        tied = list(
-            lax.optimization_barrier(
-                tuple(values) + tuple(ended) + tuple(make() for _, _, make, _ in planned)
-            )
-        )
-        for (name, end, _, send), operand in zip(planned, tied[len(values) + len(ended) :]):
-            result = self.got[name] = send(operand)
-            self.due.setdefault(end, []).extend(result if isinstance(result, list) else [result])
-        return tied[: len(values)]
+        names = self.due.pop(label, [])
+        ended = [self.got[name] for name in names]
+        values, ended, operands = lax.optimization_barrier(
+            (list(values), ended, [make() for _, _, make, _ in planned])
+        )
+        self.got.update(zip(names, ended))
+        for (name, end, _, send), operand in zip(planned, operands):
+            self.got[name] = send(operand)
+            self.due.setdefault(end, []).append(name)
+        return values
 
 
 def shape_of(rows, cols, kind):
@@ -102,22 +99,22 @@
     )(scalars, *arrays)
 
 
-def place(scalars, pieces, spots, rows, widths):
-    count, many = len(pieces), len(widths)
-    height = pieces[0].shape[0]
+def place(scalars, pieces, rows, height, breadth):
+    count = len(pieces)
+    blocks = pieces[0][0].shape[0] // height
 
     def body(at, *refs):
-        ins, outs, sems = refs[:count], refs[count:-1], refs[-1]
+        ins, out, sems = refs[:count], refs[count], refs[count + 1]
         copies = []
-        for n in range(count):
-            where, start = at_rows(spots[n](at), height), 0
-            for m, breadth in enumerate(widths):
+        for n, (_, first, spot) in enumerate(pieces):
+            for i in range(blocks):
                 copies.append(
                     pltpu.make_async_copy(
-                        ins[n].at[:, start : start + breadth], outs[m].at[where, :], sems.at[n * many + m]
+                        ins[n].at[i * height : (i + 1) * height, first : first + breadth],
+                        out.at[at_rows(spot(at, i), height), :],
+                        sems.at[n * blocks + i],
                     )
                 )
-                start += breadth
         for copy in copies:
             copy.start()
         for copy in copies:
@@ -125,12 +122,12 @@
 
     return call(
         body,
-        [shape_of(rows, breadth, pieces[0].dtype) for breadth in widths],
+        [shape_of(rows, breadth, LOW)],
         scalars,
-        pieces,
-        [pltpu.SemaphoreType.DMA((count * many,))],
+        [piece[0] for piece in pieces],
+        [pltpu.SemaphoreType.DMA((count * blocks,))],
         ANY_SPEC,
-    )
+    )[0]
 
 
 def place_wide(scalars, pieces, spots, rows, cols, kind=F32):
@@ -144,28 +141,28 @@
     return call(body, [shape_of(rows, cols, kind)], scalars, pieces)[0]
 
 
-def finish_weights(scalars, pieces, weights, gain, spots):
-    count, many = len(pieces), len(weights)
+def finish_weights(scalars, pieces, weights, gain):
+    many = len(weights)
     height, breadth = weights[0].shape
-    block = pieces[0].shape[1] // (many + 1)
-
-    def body(at, *refs):
-        ins, held, gains = refs[:count], refs[count : count + many], refs[count + many]
-        outs, turned, terms = refs[count + many + 1 : -2], refs[-2], refs[-1]
+    count, block = pieces.shape[0], pieces.shape[2] // (many + 1)
+
+    def body(at, piece_ref, *refs):
+        held, gains = refs[:many], refs[many]
+        outs, turned, terms = refs[many + 1 : -2], refs[-2], refs[-1]
         total = jnp.zeros((height, 1), F32)
         scale = gains[...]
-        for n in range(count):
-            where = at_rows(spots[n](at), block)
+        for i in range(count):
+            where = slice(i * block, (i + 1) * block)
             for m in range(many):
-                grad = ins[n][:, m * block : (m + 1) * block].astype(F32)
+                grad = piece_ref[i, :, m * block : (m + 1) * block].astype(F32)
                 outs[m][:, where] = grad * scale
                 total += jnp.sum(grad * held[m][:, where].astype(F32), axis=1, keepdims=True)
-            turned[where, :] = ins[n][:, many * block :].astype(F32).T
+            turned[where, :] = piece_ref[i, :, many * block :].astype(F32).T
         terms[...] = total
 
     outs = [shape_of(height, breadth, F32) for _ in weights]
     outs += [shape_of(breadth, height, F32), shape_of(height, 1, F32)]
-    return call(body, outs, scalars, list(pieces) + list(weights) + [gain])
+    return call(body, outs, scalars, [pieces] + list(weights) + [gain])
 
 
 def turn(values, cosine, signed):
@@ -379,6 +376,16 @@
             total = total + far_swap(parts[k].astype(LOW), k).astype(F32)
         return total
 
+    def far_exchange(blocks):
+        return lax.all_to_all(
+            blocks,
+            "seq",
+            0,
+            0,
+            axis_index_groups=[[i * groups + g for i in range(far)] for g in range(groups)],
+            tiled=True,
+        )
+
     def group_shift(value, step):
         return lax.ppermute(
             value,
@@ -395,6 +402,10 @@
 
     flow = Flow()
     gate, plan, got = flow.gate, flow.plan, flow.got
+
+    def keep(name, value, label):
+        got[name] = value
+        flow.due.setdefault(label, []).append(name)
     half_far = far // 2
     many_rows = half_far * own
 
@@ -408,6 +419,7 @@
         near = jnp.concatenate(
             parts[:half_far] + [head_swap(part, 2) for part in parts[:half_far]]
         )
+        (near,) = gate(labels[0] + "n", [near])
         rest = jnp.concatenate(parts[half_far:])
         near, rest = gate(labels[1], [near, rest])
         rest = jnp.concatenate([rest, head_swap(rest, 2)])
@@ -429,16 +441,18 @@
             labels[1], [half[:many_rows], half[many_rows:].astype(LOW), mine[0], other[0]]
         )
         near = left[0].astype(F32) + core_swap(left[1]).astype(F32)
+        (near,) = gate(labels[1] + "n", [near])
         rest = kept + head_swap(sent, 2).astype(F32)
         near, near_sent, rest = gate(
             labels[2], [near[:many_rows], near[many_rows:].astype(LOW), rest]
         )
         near = near + head_swap(near_sent, 2).astype(F32)
+        (near,) = gate(labels[2] + "n", [near])
         return scatter_far(
             [part[k * own : (k + 1) * own] for part in (near, rest) for k in range(half_far)]
         )
 
-    def plan_gather(tag, piece, far_gates, near_gates, rest_gates, core_gates):
+    def plan_gather(tag, piece, far_gates, near_gates, rest_gates):
         plan((tag, "far"), *far_gates, lambda: piece, gather_far)
         halves = (("near", range(half_far), near_gates), ("rest", range(half_far, far), rest_gates))
         for name, ks, gates in halves:
@@ -449,23 +463,24 @@
                 lambda v: head_swap(v, 2),
             )
 
-            def both(name=name, ks=ks):
-                return jnp.concatenate([got[tag, "far"][k] for k in ks] + [got[tag, name]])
-
-            plan((tag, name, "core"), *core_gates, both, core_swap)
-
         def finish():
             parts = got[tag, "far"]
             mine = parts[:half_far] + [got[tag, "near"]] + parts[half_far:] + [got[tag, "rest"]]
-            other = [got[tag, "near", "core"], got[tag, "rest", "core"]]
-            return [jnp.concatenate(mine), jnp.concatenate(other)]
+            mine = jnp.concatenate(mine)
+            return [mine, core_swap(mine)]
 
         return finish
 
     def plan_scatter(tag, chunks, core_gates, rest_gates, near_gates, far_gates):
-        mine, other = split_rows(chunks)
+        made = []
+
+        def halves():
+            if not made:
+                made.extend(split_rows(chunks()))
+            return made
 
         def half(n):
+            mine = halves()[0]
             return mine[n].astype(F32) + got[tag, "core", n].astype(F32)
 
         def part(k):
@@ -474,7 +489,7 @@
             return value[at : at + own].astype(LOW)
 
         for n, gates in ((1, rest_gates), (0, near_gates)):
-            plan((tag, "core", n), *core_gates, lambda n=n: other[n], core_swap)
+            plan((tag, "core", n), *core_gates, lambda n=n: halves()[1][n], core_swap)
             plan(
                 (tag, "head", n),
                 *gates,
@@ -487,61 +502,58 @@
             lambda: jnp.stack([part(k) for k in range(far)]),
             lambda v: scatter_far([v[k] for k in range(far)]),
         )
-        return lambda: got[tag, "far"]
-
-    steps = [(k, g) for k in range(far) for g in range(groups)]
-
-    def source_of(k, g):
-        return lambda at: (at[0] ^ k) * groups + lax.rem(at[2] + groups - g, groups)
-
-    def plan_weights(tag, block_of, far_gates, group_gates):
-        got[tag, 0, 0] = block_of(far_at)
-        for k in range(far):
-            if k:
-                plan(
-                    (tag, k, 0),
-                    *far_gates[k],
-                    lambda k=k: block_of(far_at ^ k),
-                    lambda v, k=k: far_swap(v, k),
-                )
+
+    def column_blocks(weight, gain=None):
+        breadth = weight.shape[1] // far
+        blocks = [weight[:, i * breadth : (i + 1) * breadth] for i in range(far)]
+        if gain is not None:
+            blocks = [(block.astype(F32) * gain).astype(LOW) for block in blocks]
+        return jnp.stack(blocks)
+
+    def row_blocks(weight):
+        return weight.reshape(far, weight.shape[0] // far, weight.shape[1]).transpose(0, 2, 1)
+
+    def plan_weight(name, make, far_gates, group_gates):
+        plan(name, *far_gates, make, far_exchange)
+        for g in range(1, groups):
+            plan((name, g), *group_gates, lambda: got[name], lambda v, g=g: group_shift(v, g))
+
+    def place_weight(name, first, breadth):
+        def flat(value):
+            return value.reshape(-1, value.shape[2])
+
+        def spot(g):
+            return lambda at, i: i * groups + lax.rem(at[2] + groups - g, groups)
+
+        pieces = [(flat(got[name]), first, spot(0))]
+        pieces += [(flat(got[name, g]), first, spot(g)) for g in range(1, groups)]
+        return place(scalars, pieces, width, rows_s, breadth)
+
+    def plan_grad(name, make, group_gates, far_gates):
+        made = []
+
+        def part(at):
+            if not made:
+                made.extend(v.reshape(far, groups, rows_s, -1) for v in make())
+            return jnp.concatenate(
+                [lax.dynamic_index_in_dim(v, at, 1, keepdims=False) for v in made], axis=2
+            )
+
+        def total():
+            value = part(group_at)
             for g in range(1, groups):
-                plan(
-                    (tag, k, g),
-                    *group_gates[k],
-                    lambda k=k: got[tag, k, 0],
-                    lambda v, g=g: group_shift(v, g),
-                )
-
-    def place_weights(tag, widths):
-        pieces = [got[tag, k, g] for k, g in steps]
-        return place(scalars, pieces, [source_of(*s) for s in steps], width, widths)
-
-    def plan_grads(tag, grads, group_gates, far_gates):
-        def rows(at):
-            return jnp.concatenate(
-                [lax.dynamic_slice_in_dim(v, at * rows_s, rows_s, 0) for v in grads], axis=1
-            )
-
-        def total(k):
-            value = rows((far_at ^ k) * groups + group_at)
-            for g in range(1, groups):
-                value = value + got[tag, "x", k, g].astype(F32)
+                value = value + got[name, "group", g].astype(F32)
             return value.astype(LOW)
 
-        for k in reversed(range(far)):
-            for g in range(1, groups):
-                plan(
-                    (tag, "x", k, g),
-                    *group_gates[k],
-                    lambda k=k, g=g: rows((far_at ^ k) * groups + (group_at + g) % groups).astype(LOW),
-                    lambda v, g=g: group_shift(v, g),
-                )
-            if k:
-                plan((tag, k), *far_gates[k], lambda k=k: total(k), lambda v, k=k: far_swap(v, k))
-
-        return lambda: [got[tag, k] if k else total(0) for k in range(far)]
-
-    far_spots = [(lambda at, k=k: at[0] ^ k) for k in range(far)]
+        for g in range(1, groups):
+            plan(
+                (name, "group", g),
+                *group_gates,
+                lambda g=g: part((group_at + g) % groups).astype(LOW),
+                lambda v, g=g: group_shift(v, g),
+            )
+        plan(name, *far_gates, total, far_exchange)
+
     head_spots = [(lambda at, m=m: at[1] ^ m) for m in (0, 2, 1, 3)]
 
     def every_row(piece):
@@ -554,41 +566,32 @@
 
     gain_a = attn_gain.astype(F32)[:, None]
     gain_b = mlp_gain.astype(F32)[:, None]
-
-    def weight_block(weights, gain, turned, breadth):
-        turned = turned.T
-
-        def block_of(i):
-            def columns(w):
-                return lax.dynamic_slice_in_dim(w, i * breadth, breadth, 1)
-
-            parts = [(columns(w).astype(F32) * gain).astype(LOW) for w in weights]
-            return jnp.concatenate(parts + [columns(turned)], axis=1)
-
-        return block_of
 
     own_in = lax.dynamic_slice_in_dim(layer_in, head_at * own, own, 0).astype(F32)
     own_grad = lax.dynamic_slice_in_dim(out_grad, head_at * own, own, 0)
     inv_a = inv_rms(own_in)
     normed_a = own_in * inv_a
-    plan_weights(
+    plan_weight(
         "attn",
-        weight_block((query_weight, key_weight, value_weight), gain_a, proj_weight, HD),
-        [None] + [("start", "x0")] * 3,
-        G_ATTN_X,
-    )
-    finish_top = plan_gather(
-        "top", own_grad, *G_TOP
-    )
-    plan_weights(
+        lambda: jnp.concatenate(
+            [column_blocks(w, gain_a) for w in (query_weight, key_weight, value_weight)]
+            + [row_blocks(proj_weight)],
+            axis=2,
+        ),
+        *G_ATTN,
+    )
+    plan_weight(
         "mlp",
-        weight_block((gate_weight, up_weight), gain_b, down_weight, hidden),
-        [None] + G_MLP_Z,
-        G_MLP_X,
-    )
-    got["x"] = gate("start", [normed_a.astype(LOW)])[0]
-    hidden_a = gather_rows(("x0", "x1", "x2"), got["x"])
-    qkv_full, proj_turned = place_weights("attn", (3 * HD, HD))
+        lambda: jnp.concatenate(
+            [column_blocks(w, gain_b) for w in (gate_weight, up_weight)] + [row_blocks(down_weight)],
+            axis=2,
+        ),
+        *G_MLP,
+    )
+    finish_top = plan_gather("top", own_grad, *G_TOP)
+    gate("start", [])
+    hidden_a = gather_rows(("x0", "x1", "x2"), normed_a.astype(LOW))
+    qkv_full, proj_turned = place_weight("attn", 0, 3 * HD), place_weight("attn", 3 * HD, HD)
 
     far_ids = jnp.arange(far, dtype=jnp.int32)
     positions = (far_ids * groups + group_at)[:, None] * tok + jnp.arange(tok, dtype=jnp.int32)
@@ -622,44 +625,49 @@
     normed_b = middle * inv_b
     hidden_b = gather_rows(("h0", "h1", "h2"), normed_b.astype(LOW))
     hidden_b = gate("mlp", hidden_b)
-    gate_up, down_turned = place_weights("mlp", (2 * hidden, hidden))
-    grad_top = finish_top()
-    active, grad_gu = [], []
-    for h, top in zip(hidden_b, grad_top):
+    gate_up = place_weight("mlp", 0, 2 * hidden)
+    down_turned = place_weight("mlp", 2 * hidden, hidden)
+    parts, active = [], []
+    for h in hidden_b:
         gate_up_val = dot(h, gate_up)
         gate_val, up_val = gate_up_val[:, :hidden], gate_up_val[:, hidden:]
         gate_sig = jax.nn.sigmoid(gate_val)
         silu_val = gate_val * gate_sig
         active.append((silu_val * up_val).astype(LOW))
+        parts.append(
+            (silu_val, up_val * gate_sig * (1.0 + gate_val * (1.0 - gate_sig)))
+        )
+    plan_scatter(
+        "out", lambda: [dot_last(a, down_turned).astype(LOW) for a in active], *G_OUT
+    )
+    parts = gate("mlpb", [parts])[0]
+    parts = gate("mlpc", [parts])[0]
+    grad_top = finish_top()
+    grad_gu = []
+    for top, (silu_val, gate_slope) in zip(grad_top, parts):
         grad_active = dot(top, down_turned)
         grad_gu.append(
             jnp.concatenate(
-                [
-                    (
-                        grad_active * up_val * gate_sig * (1.0 + gate_val * (1.0 - gate_sig))
-                    ).astype(LOW),
-                    (grad_active * silu_val).astype(LOW),
-                ],
+                [(grad_active * gate_slope).astype(LOW), (grad_active * silu_val).astype(LOW)],
                 axis=1,
             )
         )
+
     def over_tokens(left_mats, right_mats):
         return sum(dot_first(a, b) for a, b in zip(left_mats, right_mats))
 
-    grad_gu = gate("mlp done", grad_gu)
-    finish_out = plan_scatter(
-        "out",
-        [dot_last(a, down_turned).astype(LOW) for a in active],
-        *G_OUT,
-    )
-    finish_mlp = plan_grads(
-        "mlp grads",
-        [over_tokens(hidden_b, grad_gu), over_tokens(grad_top, active)],
-        G_MLPG_X,
-        [None] + G_MLPG_Z,
-    )
+    keep("mlp kept", (hidden_b, grad_gu, grad_top, active), "g1")
+
+    def mlp_grads():
+        hidden_b, grad_gu, grad_top, active = got["mlp kept"]
+        return [over_tokens(hidden_b, grad_gu), over_tokens(grad_top, active)]
+
+    plan_grad("mlp grads", mlp_grads, *G_GRAD_MLP)
     grad_normed_b = scatter_rows(
-        ("g0", "g1", "g2"), [dot_last(g, gate_up).astype(LOW) for g in grad_gu]
+        ("g0", "g1", "g2"),
+        [
+            dot_last(g, gate_up).astype(LOW) for g in grad_gu
+        ],
     )
     grad_middle = own_grad.astype(F32) + norm_back(grad_normed_b, normed_b, inv_b)
     grad_mix = gather_rows(("m0", "m1", "m2"), grad_middle.astype(LOW))
@@ -677,12 +685,13 @@
     grad_qkv = rotate_back(
         scalars, grad_query, grad_keys, cosine, signed, far, head_size, own
     )
-    finish_attn = plan_grads(
-        "attn grads",
-        [over_tokens(hidden_a, grad_qkv), over_tokens(grad_mix, attn_low)],
-        G_ATTNG_X,
-        [None] + G_ATTNG_Z,
-    )
+    keep("attn kept", (hidden_a, grad_qkv, grad_mix, attn_low), "r1")
+
+    def attn_grads():
+        hidden_a, grad_qkv, grad_mix, attn_low = got["attn kept"]
+        return [over_tokens(hidden_a, grad_qkv), over_tokens(grad_mix, attn_low)]
+
+    plan_grad("attn grads", attn_grads, *G_GRAD_ATTN)
     grad_normed_a = scatter_rows(
         ("r0", "r1", "r2"), [dot_last(g, qkv_full).astype(LOW) for g in grad_qkv]
     )
@@ -691,12 +700,12 @@
     (grad_in,) = gate("in", [grad_in])
     in_rows = every_row(grad_in)
     in_rows = gate("end", in_rows)
-    out_rows = every_row((middle + finish_out()).astype(LOW))
+    out_rows = every_row((middle + got["out", "far"]).astype(LOW))
     grad_gate, grad_up, grad_down, mlp_terms = finish_weights(
-        scalars, finish_mlp(), [gate_weight, up_weight], gain_b, far_spots
+        scalars, got["mlp grads"], [gate_weight, up_weight], gain_b
     )
     grad_query_w, grad_key_w, grad_value_w, grad_proj, attn_terms = finish_weights(
-        scalars, finish_attn(), [query_weight, key_weight, value_weight], gain_a, far_spots
+        scalars, got["attn grads"], [query_weight, key_weight, value_weight], gain_a
     )
     layer_out = place_wide(scalars, out_rows, head_spots, tok, width, LOW)
     input_grad = place_wide(scalars, in_rows, head_spots, tok, width)

time: 593 us -> 572 us (0.965)
  starting transfers between devices: 143 us -> 93.2 us
  waiting for transfers between devices: 286 us -> 304 us
  other arithmetic: 41 us -> 50.8 us
  Pallas kernels: 25.8 us -> 33.2 us
  matrix products: 45.2 us -> 38.7 us
    ppermute x36 -> x24, waiting for transfers between devices: 163 us -> 111 us  [far_swap(): lax.ppermute(value, 'seq', [(i * groups + g, (i ^ step) * groups + g) for...]
    all_to_all x0 -> x4, waiting for transfers between devices: none -> 50.9 us  [far_exchange(): lax.all_to_all(blocks, 'seq', 0, 0, axis_index_groups=[[i * groups + g fo...]
    ppermute x36 -> x24, starting transfers between devices: 75.7 us -> 32.8 us  [far_swap(): lax.ppermute(value, 'seq', [(i * groups + g, (i ^ step) * groups + g) for...]
    ppermute x18 -> x6, starting transfers between devices: 23.5 us -> 5.36 us  [group_shift(): lax.ppermute(value, 'seq', [(i * groups + g, i * groups + (g + step) % gr...]
    all_to_all x0 -> x4, starting transfers between devices: none -> 17.3 us  [far_exchange(): lax.all_to_all(blocks, 'seq', 0, 0, axis_index_groups=[[i * groups + g fo...]
    unnamed x163 -> x180, local copies, waits for them, and re-layouts: 24.2 us -> 13.3 us
    ppermute x91, waiting for transfers between devices: 83.3 us -> 94 us  [head_swap(): lax.ppermute(value, 'head', [(i, i ^ step) for i in range(head_size)])]
    ppermute x18 -> x6, waiting for transfers between devices: 39.5 us -> 47.5 us  [group_shift(): lax.ppermute(value, 'seq', [(i * groups + g, i * groups + (g + step) % gr...]
  transfers between devices with their start and end apart: 145 -> 125, of which waited for: 62 -> 52; matrix products, arithmetic and copies ran while one was open for 13% -> 19% of each run, Pallas kernels for 4% -> 6%
where the time goes in v3:
time: 572 us; the launch traced here: 566 us
  waiting for transfers between devices  304 us (53%)
  starting transfers between devices  93.2 us (16%)
  other arithmetic  50.8 us (9%)
  local copies, waits for them, and re-layouts  43.2 us (8%)
  matrix products  38.7 us (7%)
  Pallas kernels  33.2 us (6%)
    ppermute x24, waiting for transfers between devices, far_swap(): lax.ppermute(value, 'seq', [(i * groups + g, (i ^ step) * groups + g) for...  111 us
    ppermute x91, waiting for transfers between devices, head_swap(): lax.ppermute(value, 'head', [(i, i ^ step) for i in range(head_size)])  94 us
    all_to_all x4, waiting for transfers between devices, far_exchange(): lax.all_to_all(blocks, 'seq', 0, 0, axis_index_groups=[[i * groups + g fo...  50.9 us
    ppermute x6, waiting for transfers between devices, group_shift(): lax.ppermute(value, 'seq', [(i * groups + g, i * groups + (g + step) % gr...  47.5 us
    ppermute x91, starting transfers between devices, head_swap(): lax.ppermute(value, 'head', [(i, i ^ step) for i in range(head_size)])  37.8 us
    pallas_call x12, Pallas kernels, call(): pl.pallas_call(body, out_shape=outs, in_specs=[SMEM_SPEC] + [space] * len...  33.2 us
    ppermute x24, starting transfers between devices, far_swap(): lax.ppermute(value, 'seq', [(i * groups + g, (i ^ step) * groups + g) for...  32.8 us
    all_to_all x4, starting transfers between devices, far_exchange(): lax.all_to_all(blocks, 'seq', 0, 0, axis_index_groups=[[i * groups + g fo...  17.3 us
  transfers between devices with their start and end apart: 125, of which 52 were waited for; matrix products, arithmetic and copies ran while one was open for 19% of the time, Pallas kernels for 6%

profile of v3, /device:TPU:0, one launch (start us, length us, event | category | flops | bytes accessed | tf_op | source)
XLA Modules:
  0.0 566.2 jit_solution(1018440352674876405)
XLA Ops:
  3.5 5.0 collective-permute-start.4
  15.3 4.9 all-to-all-start
  28.4 10.2 %collective-permute-done.3 = bf16[64,2048]{1,0:T(8,128)(2,1)} collective-permute-done((bf16[64,2048]{1,0:T(8,128)(2,1)}, bf16[64,2048]{1,0:T(8,128)(2,1)}, u32[]{:S(2)}, u32[]{:S(2)}) %collective-permute-start.3) | collective-permute-done | bytes 262176 | tf_op jit(solution)/shard_map/ppermute | solution.py:364
  41.7 12.0 %all-to-all-done = bf16[4,256,512]{2,1,0:T(8,128)(2,1)} async-done(((bf16[4,256,512]{2,1,0:T(8,128)(2,1)}), bf16[4,256,512]{2,1,0:T(8,128)(2,1)}, u32[]{:S(2)}, u32[]{:S(2)}) %all-to-all-start) | async-done | bytes 1048608 | tf_op jit(solution)/shard_map/all_to_all | solution.py:380
  61.6 4.0 all-to-all-start.1
  66.8 3.8 collective-permute-done.5
  71.9 8.6 %collective-permute-done.10 = bf16[4,256,512]{2,1,0:T(8,128)(2,1)} collective-permute-done((bf16[4,256,512]{2,1,0:T(8,128)(2,1)}, bf16[4,256,512]{2,1,0:T(8,128)(2,1)}, u32[]{:S(2)}, u32[]{:S(2)}) %collective-permute-start.10) | collective-permute-done | bytes 1048608 | tf_op jit(solution)/shard_map/ppermute | solution.py:390
  93.4 9.9 %collective-permute-done.15.refs_1_ = bf16[1024,256]{1,0:T(8,128)(2,1)} collective-permute-done((bf16[1024,256]{1,0:T(8,128)(2,1)}, bf16[1024,256]{1,0:T(8,128)(2,1)}, u32[]{:S(2)}, u32[]{:S(2)}) %collective-permute-start.15) | collective-permute-done | bytes 524320 | tf_op jit(solution)/shard_map/ppermute | solution.py:390
  112.3 24.7 %all-to-all-done.1 = bf16[4,256,1536]{2,1,0:T(8,128)(2,1)S(1)} async-done(((bf16[4,256,1536]{2,1,0:T(8,128)(2,1)}), bf16[4,256,1536]{2,1,0:T(8,128)(2,1)S(1)}, u32[]{:S(2)}, u32[]{:S(2)}) %all-to-all-start.1) | async-done | bytes 3145760 | tf_op jit(solution)/shard_map/all_to_all | solution.py:380
  152.4 11.4 %collective-permute-done.25 = bf16[64,2048]{1,0:T(8,128)(2,1)S(1)} collective-permute-done((bf16[64,2048]{1,0:T(8,128)(2,1)S(1)}, bf16[64,2048]{1,0:T(8,128)(2,1)S(1)}, u32[]{:S(2)}, u32[]{:S(2)}) %collective-permute-start.25) | collective-permute-done | bytes 262176 | tf_op jit(solution)/shard_map/ppermute | solution.py:364
  173.4 9.3 %collective-permute-done.28 = bf16[128,2048]{1,0:T(8,128)(2,1)} collective-permute-done((bf16[128,2048]{1,0:T(8,128)(2,1)}, bf16[128,2048]{1,0:T(8,128)(2,1)}, u32[]{:S(2)}, u32[]{:S(2)}) %collective-permute-start.28) | collective-permute-done | bytes 524320 | tf_op jit(solution)/shard_map/ppermute | solution.py:401
  184.9 11.5 %collective-permute-done.30 = bf16[64,2048]{1,0:T(8,128)(2,1)S(1)} collective-permute-done((bf16[64,2048]{1,0:T(8,128)(2,1)S(1)}, bf16[64,2048]{1,0:T(8,128)(2,1)S(1)}, u32[]{:S(2)}, u32[]{:S(2)}) %collective-permute-start.30) | collective-permute-done | bytes 262176 | tf_op jit(solution)/shard_map/ppermute | solution.py:364
  199.1 15.8 %collective-permute-done.32 = bf16[4,256,1536]{2,1,0:T(8,128)(2,1)} collective-permute-done((bf16[4,256,1536]{2,1,0:T(8,128)(2,1)S(1)}, bf16[4,256,1536]{2,1,0:T(8,128)(2,1)}, u32[]{:S(2)}, u32[]{:S(2)}) %collective-permute-start.32) | collective-permute-done | bytes 3145760 | tf_op jit(solution)/shard_map/ppermute | solution.py:390
  219.1 8.3 %collective-permute-done.33 = bf16[64,2048]{1,0:T(8,128)(2,1)S(1)} collective-permute-done((bf16[64,2048]{1,0:T(8,128)(2,1)S(1)}, bf16[64,2048]{1,0:T(8,128)(2,1)S(1)}, u32[]{:S(2)}, u32[]{:S(2)}) %collective-permute-start.33) | collective-permute-done | bytes 262176 | tf_op jit(solution)/shard_map/ppermute | solution.py:364
  232.4 8.2 %collective-permute-done.36 = bf16[64,2048]{1,0:T(8,128)(2,1)S(1)} collective-permute-done((bf16[64,2048]{1,0:T(8,128)(2,1)S(1)}, bf16[64,2048]{1,0:T(8,128)(2,1)S(1)}, u32[]{:S(2)}, u32[]{:S(2)}) %collective-permute-start.36) | collective-permute-done | bytes 262176 | tf_op jit(solution)/shard_map/ppermute | solution.py:364
  245.8 10.6 %collective-permute-done.39 = bf16[128,2048]{1,0:T(8,128)(2,1)S(1)} collective-permute-done((bf16[128,2048]{1,0:T(8,128)(2,1)S(1)}, bf16[128,2048]{1,0:T(8,128)(2,1)S(1)}, u32[]{:S(2)}, u32[]{:S(2)}) %collective-permute-start.39) | collective-permute-done | bytes 524320 | tf_op jit(solution)/shard_map/ppermute | solution.py:401
  256.5 10.7 %collective-permute-done.44 = bf16[128,2048]{1,0:T(8,128)(2,1)S(1)} collective-permute-done((bf16[128,2048]{1,0:T(8,128)(2,1)S(1)}, bf16[128,2048]{1,0:T(8,128)(2,1)S(1)}, u32[]{:S(2)}, u32[]{:S(2)}) %collective-permute-start.44) | collective-permute-done | bytes 524320 | tf_op jit(solution)/shard_map/ppermute | solution.py:401
  312.8 9.6 %collective-permute-done.66 = bf16[128,2048]{1,0:T(8,128)(2,1)S(1)} collective-permute-done((bf16[128,2048]{1,0:T(8,128)(2,1)S(1)}, bf16[128,2048]{1,0:T(8,128)(2,1)S(1)}, u32[]{:S(2)}, u32[]{:S(2)}) %collective-permute-start.66) | collective-permute-done | bytes 524320 | tf_op jit(solution)/shard_map/ppermute | solution.py:401
  323.4 10.9 %collective-permute-done.68 = bf16[64,2048]{1,0:T(8,128)(2,1)S(1)} collective-permute-done((bf16[64,2048]{1,0:T(8,128)(2,1)S(1)}, bf16[64,2048]{1,0:T(8,128)(2,1)S(1)}, u32[]{:S(2)}, u32[]{:S(2)}) %collective-permute-start.68) | collective-permute-done | bytes 262176 | tf_op jit(solution)/shard_map/ppermute | solution.py:364
  348.4 11.0 %collective-permute-done.73 = bf16[64,2048]{1,0:T(8,128)(2,1)S(1)} collective-permute-done((bf16[64,2048]{1,0:T(8,128)(2,1)S(1)}, bf16[64,2048]{1,0:T(8,128)(2,1)S(1)}, u32[]{:S(2)}, u32[]{:S(2)}) %collective-permute-start.73) | collective-permute-done | bytes 262176 | tf_op jit(solution)/shard_map/ppermute | solution.py:364
  363.1 7.0 %collective-permute-done.71 = bf16[64,2048]{1,0:T(8,128)(2,1)S(1)} collective-permute-done((bf16[64,2048]{1,0:T(8,128)(2,1)S(1)}, bf16[64,2048]{1,0:T(8,128)(2,1)S(1)}, u32[]{:S(2)}, u32[]{:S(2)}) %collective-permute-start.71) | collective-permute-done | bytes 262176 | tf_op jit(solution)/shard_map/ppermute | solution.py:401
  370.0 4.9 collective-permute-done.72
  380.3 10.4 %collective-permute-done.83 = bf16[128,2048]{1,0:T(8,128)(2,1)S(1)} collective-permute-done((bf16[128,2048]{1,0:T(8,128)(2,1)S(1)}, bf16[128,2048]{1,0:T(8,128)(2,1)S(1)}, u32[]{:S(2)}, u32[]{:S(2)}) %collective-permute-start.83) | collective-permute-done | bytes 524320 | tf_op jit(solution)/shard_map/ppermute | solution.py:401
  403.3 5.0 all-to-all-start.2
  411.4 7.6 %shard_map.209 = (f32[1024,128]{1,0:T(8,128)S(1)}, f32[1024,256]{1,0:T(8,128)S(1)}, bf16[1024,256]{1,0:T(8,128)(2,1)S(1)}) custom-call(s32[3]{0:T(128)S(1)} %pad_add_fusion.1.at, bf16[1024,128]{1,0:T(8,128)(2,1)S(1)} %copy-done.21, s32[1024,1]{1,0:T(8,128)S(1)} %copy-done.17, s32[2,1024]{1,0:T(2,128)S(1)} %pad_add_fusion.key_doc_ref, ...), custom_call_target="tpu_custom_call" | custom-call | flops 1342177280 | bytes 3682304 | tf_op jit(solution)/shard_map/pallas_call | solution.py:91
  421.4 11.7 %collective-permute-done.95.refs_1_ = bf16[1024,256]{1,0:T(8,128)(2,1)S(1)} collective-permute-done((bf16[1024,256]{1,0:T(8,128)(2,1)S(1)}, bf16[1024,256]{1,0:T(8,128)(2,1)S(1)}, u32[]{:S(2)}, u32[]{:S(2)}) %collective-permute-start.95) | collective-permute-done | bytes 524320 | tf_op jit(solution)/shard_map/ppermute | solution.py:390
  456.1 8.9 %collective-permute-done.104 = bf16[128,2048]{1,0:T(8,128)(2,1)S(1)} collective-permute-done((bf16[128,2048]{1,0:T(8,128)(2,1)S(1)}, bf16[128,2048]{1,0:T(8,128)(2,1)S(1)}, u32[]{:S(2)}, u32[]{:S(2)}) %collective-permute-start.104) | collective-permute-done | bytes 524320 | tf_op jit(solution)/shard_map/ppermute | solution.py:401
  465.2 14.2 %all-to-all-done.2.piece_ref = bf16[4,256,1536]{2,1,0:T(8,128)(2,1)} async-done(((bf16[4,256,1536]{2,1,0:T(8,128)(2,1)}), bf16[4,256,1536]{2,1,0:T(8,128)(2,1)}, u32[]{:S(2)}, u32[]{:S(2)}) %all-to-all-start.2) | async-done | bytes 3145760 | tf_op jit(solution)/shard_map/all_to_all | solution.py:380
  485.1 7.5 %collective-permute-done.105 = bf16[128,2048]{1,0:T(8,128)(2,1)S(1)} collective-permute-done((bf16[128,2048]{1,0:T(8,128)(2,1)}, bf16[128,2048]{1,0:T(8,128)(2,1)S(1)}, u32[]{:S(2)}, u32[]{:S(2)}) %collective-permute-start.105) | collective-permute-done | bytes 524320 | tf_op jit(solution)/shard_map/ppermute | solution.py:401
  501.8 17.3 %collective-permute-done.108 = bf16[64,2048]{1,0:T(8,128)(2,1)} collective-permute-done((bf16[64,2048]{1,0:T(8,128)(2,1)}, bf16[64,2048]{1,0:T(8,128)(2,1)}, u32[]{:S(2)}, u32[]{:S(2)}) %collective-permute-start.108) | collective-permute-done | bytes 262176 | tf_op jit(solution)/shard_map/ppermute | solution.py:364
  530.7 5.2 shard_map.214
  538.1 13.0 %collective-permute-done.114 = bf16[64,2048]{1,0:T(8,128)(2,1)} collective-permute-done((bf16[64,2048]{1,0:T(8,128)(2,1)}, bf16[64,2048]{1,0:T(8,128)(2,1)}, u32[]{:S(2)}, u32[]{:S(2)}) %collective-permute-start.114) | collective-permute-done | bytes 262176 | tf_op jit(solution)/shard_map/ppermute | solution.py:364
  (583 shorter events, 249.8 us)
Async XLA Ops:
  3.5 24.9 %collective-permute-start.4 = (bf16[64,2048]{1,0:T(8,128)(2,1)}, bf16[64,2048]{1,0:T(8,128)(2,1)}, u32[]{:S(2)}, u32[]{:S(2)}) collective-permute-start(bf16[64,2048]{1,0:T(8,128)(2,1)} %fusion.13), channel_id=1, source_target_pairs={{0,24},{4,28},{8,16},{12,20},{16,8},{20,12},{24,0},{28,4},{1,25},{... | collective-permute-start | bytes 786440 | tf_op jit(solution)/shard_map/ppermute | solution.py:364
  8.6 30.0 %collective-permute-start.3 = (bf16[64,2048]{1,0:T(8,128)(2,1)}, bf16[64,2048]{1,0:T(8,128)(2,1)}, u32[]{:S(2)}, u32[]{:S(2)}) collective-permute-start(bf16[64,2048]{1,0:T(8,128)(2,1)} %fusion.13), channel_id=1, source_target_pairs={{0,16},{4,20},{8,24},{12,28},{16,0},{20,4},{24,8},{28,12},{1,17},{... | collective-permute-start | bytes 786440 | tf_op jit(solution)/shard_map/ppermute | solution.py:364
  8.6 31.9 %collective-permute-start.1 = (bf16[64,2048]{1,0:T(8,128)(2,1)}, bf16[64,2048]{1,0:T(8,128)(2,1)}, u32[]{:S(2)}, u32[]{:S(2)}) collective-permute-start(bf16[64,2048]{1,0:T(8,128)(2,1)} %fusion.13), channel_id=1, source_target_pairs={{0,2},{1,3},{2,0},{3,1},{4,6},{5,7},{6,4},{7,5},{8,10},{9,11},{10,... | collective-permute-start | bytes 786440 | tf_op jit(solution)/shard_map/ppermute | solution.py:401
  10.1 16.8 %collective-permute-start = (bf16[64,2048]{1,0:T(8,128)(2,1)}, bf16[64,2048]{1,0:T(8,128)(2,1)}, u32[]{:S(2)}, u32[]{:S(2)}) collective-permute-start(bf16[64,2048]{1,0:T(8,128)(2,1)} %fusion.13), channel_id=1, source_target_pairs={{0,8},{4,12},{8,0},{12,4},{16,24},{20,28},{24,16},{28,20},{1,9},{5... | collective-permute-start | bytes 786440 | tf_op jit(solution)/shard_map/ppermute | solution.py:364
  15.3 38.4 %all-to-all-start = ((bf16[4,256,512]{2,1,0:T(8,128)(2,1)}), bf16[4,256,512]{2,1,0:T(8,128)(2,1)}, u32[]{:S(2)}, u32[]{:S(2)}) async-start(bf16[4,256,512]{2,1,0:T(8,128)(2,1)} %pad_maximum_fusion.6), calls=%async_computation | async-start | bytes 2097152 | tf_op jit(solution)/shard_map/all_to_all | solution.py:380
  54.7 25.9 %collective-permute-start.10 = (bf16[4,256,512]{2,1,0:T(8,128)(2,1)}, bf16[4,256,512]{2,1,0:T(8,128)(2,1)}, u32[]{:S(2)}, u32[]{:S(2)}) collective-permute-start(bf16[4,256,512]{2,1,0:T(8,128)(2,1)} %all-to-all-done), channel_id=1, source_target_pairs={{0,4},{4,0},{8,12},{12,8},{16,20},{20,16},{24,28},{28,24},{1,5},{5... | collective-permute-start | bytes 3145736 | tf_op jit(solution)/shard_map/ppermute | solution.py:390
  61.6 75.5 %all-to-all-start.1 = ((bf16[4,256,1536]{2,1,0:T(8,128)(2,1)}), bf16[4,256,1536]{2,1,0:T(8,128)(2,1)S(1)}, u32[]{:S(2)}, u32[]{:S(2)}) async-start(bf16[4,256,1536]{2,1,0:T(8,128)(2,1)} %pad_maximum_fusion), calls=%async_computation.1 | async-start | bytes 6291456 | tf_op jit(solution)/shard_map/all_to_all | solution.py:380
  144.7 70.2 %collective-permute-start.32 = (bf16[4,256,1536]{2,1,0:T(8,128)(2,1)S(1)}, bf16[4,256,1536]{2,1,0:T(8,128)(2,1)}, u32[]{:S(2)}, u32[]{:S(2)}) collective-permute-start(bf16[4,256,1536]{2,1,0:T(8,128)(2,1)S(1)} %all-to-all-done.1), channel_id=1, source_target_pairs={{0,4},{4,0},{8,12},{12,8},{16,20},{20,16},{24,28},{28,24},{1,5},{5... | collective-permute-start | bytes 9437192 | tf_op jit(solution)/shard_map/ppermute | solution.py:390
  145.2 20.4 %collective-permute-start.27 = (bf16[64,2048]{1,0:T(8,128)(2,1)S(1)}, bf16[64,2048]{1,0:T(8,128)(2,1)S(1)}, u32[]{:S(2)}, u32[]{:S(2)}) collective-permute-start(bf16[64,2048]{1,0:T(8,128)(2,1)S(1)} %constant_dynamic-slice_fusion), channel_id=1, source_target_pairs={{0,24},{4,28},{8,16},{12,20},{16,8},{20,12},{24,0},{28,4},{1,25},{... | collective-permute-start | bytes 786440 | tf_op jit(solution)/shard_map/ppermute | solution.py:364
  146.7 21.9 %collective-permute-start.26 = (bf16[64,2048]{1,0:T(8,128)(2,1)S(1)}, bf16[64,2048]{1,0:T(8,128)(2,1)S(1)}, u32[]{:S(2)}, u32[]{:S(2)}) collective-permute-start(bf16[64,2048]{1,0:T(8,128)(2,1)S(1)} %constant_dynamic-slice_fusion), channel_id=1, source_target_pairs={{0,16},{4,20},{8,24},{12,28},{16,0},{20,4},{24,8},{28,12},{1,17},{... | collective-permute-start | bytes 786440 | tf_op jit(solution)/shard_map/ppermute | solution.py:364
  146.7 17.2 %collective-permute-start.25 = (bf16[64,2048]{1,0:T(8,128)(2,1)S(1)}, bf16[64,2048]{1,0:T(8,128)(2,1)S(1)}, u32[]{:S(2)}, u32[]{:S(2)}) collective-permute-start(bf16[64,2048]{1,0:T(8,128)(2,1)S(1)} %constant_dynamic-slice_fusion), channel_id=1, source_target_pairs={{0,8},{4,12},{8,0},{12,4},{16,24},{20,28},{24,16},{28,20},{1,9},{5... | collective-permute-start | bytes 786440 | tf_op jit(solution)/shard_map/ppermute | solution.py:364
  169.8 46.7 %collective-permute-start.49 = (bf16[64,2048]{1,0:T(8,128)(2,1)}, bf16[64,2048]{1,0:T(8,128)(2,1)S(1)}, u32[]{:S(2)}, u32[]{:S(2)}) collective-permute-start(bf16[64,2048]{1,0:T(8,128)(2,1)} %copy-done.44), channel_id=1, source_target_pairs={{0,1},{1,0},{2,3},{3,2},{4,5},{5,4},{6,7},{7,6},{8,9},{9,8},{10,11... | collective-permute-start | bytes 786440 | tf_op jit(solution)/shard_map/ppermute | solution.py:401
  173.4 23.0 %collective-permute-start.30 = (bf16[64,2048]{1,0:T(8,128)(2,1)S(1)}, bf16[64,2048]{1,0:T(8,128)(2,1)S(1)}, u32[]{:S(2)}, u32[]{:S(2)}) collective-permute-start(bf16[64,2048]{1,0:T(8,128)(2,1)S(1)} %get-tuple-element.409), channel_id=1, source_target_pairs={{0,16},{4,20},{8,24},{12,28},{16,0},{20,4},{24,8},{28,12},{1,17},{... | collective-permute-start | bytes 786440 | tf_op jit(solution)/shard_map/ppermute | solution.py:364
  184.8 33.7 %collective-permute-start.50 = (bf16[64,2048]{1,0:T(8,128)(2,1)S(1)}, bf16[64,2048]{1,0:T(8,128)(2,1)S(1)}, u32[]{:S(2)}, u32[]{:S(2)}) collective-permute-start(bf16[64,2048]{1,0:T(8,128)(2,1)S(1)} %copy-done.61), channel_id=1, source_target_pairs={{0,1},{1,0},{2,3},{3,2},{4,5},{5,4},{6,7},{7,6},{8,9},{9,8},{10,11... | collective-permute-start | bytes 786440 | tf_op jit(solution)/shard_map/ppermute | solution.py:401
  196.4 44.4 %collective-permute-start.38 = (bf16[128,2048]{1,0:T(8,128)(2,1)S(1)}, bf16[128,2048]{1,0:T(8,128)(2,1)S(1)}, u32[]{:S(2)}, u32[]{:S(2)}) collective-permute-start(bf16[128,2048]{1,0:T(8,128)(2,1)S(1)} %copy-done.64), channel_id=1, source_target_pairs={{0,2},{1,3},{2,0},{3,1},{4,6},{5,7},{6,4},{7,5},{8,10},{9,11},{10,... | collective-permute-start | bytes 1572872 | tf_op jit(solution)/shard_map/ppermute | solution.py:401
  215.0 17.4 %collective-permute-start.37 = (bf16[64,2048]{1,0:T(8,128)(2,1)S(1)}, bf16[64,2048]{1,0:T(8,128)(2,1)S(1)}, u32[]{:S(2)}, u32[]{:S(2)}) collective-permute-start(bf16[64,2048]{1,0:T(8,128)(2,1)S(1)} %multiply_convert_fusion.14), channel_id=1, source_target_pairs={{0,24},{4,28},{8,16},{12,20},{16,8},{20,12},{24,0},{28,4},{1,25},{... | collective-permute-start | bytes 786440 | tf_op jit(solution)/shard_map/ppermute | solution.py:364
  216.5 24.1 %collective-permute-start.36 = (bf16[64,2048]{1,0:T(8,128)(2,1)S(1)}, bf16[64,2048]{1,0:T(8,128)(2,1)S(1)}, u32[]{:S(2)}, u32[]{:S(2)}) collective-permute-start(bf16[64,2048]{1,0:T(8,128)(2,1)S(1)} %multiply_convert_fusion.14), channel_id=1, source_target_pairs={{0,16},{4,20},{8,24},{12,28},{16,0},{20,4},{24,8},{28,12},{1,17},{... | collective-permute-start | bytes 786440 | tf_op jit(solution)/shard_map/ppermute | solution.py:364
  218.5 22.1 %collective-permute-start.34 = (bf16[64,2048]{1,0:T(8,128)(2,1)S(1)}, bf16[64,2048]{1,0:T(8,128)(2,1)S(1)}, u32[]{:S(2)}, u32[]{:S(2)}) collective-permute-start(bf16[64,2048]{1,0:T(8,128)(2,1)S(1)} %multiply_convert_fusion.14), channel_id=1, source_target_pairs={{0,2},{1,3},{2,0},{3,1},{4,6},{5,7},{6,4},{7,5},{8,10},{9,11},{10,... | collective-permute-start | bytes 786440 | tf_op jit(solution)/shard_map/ppermute | solution.py:401
  244.5 22.7 %collective-permute-start.44 = (bf16[128,2048]{1,0:T(8,128)(2,1)S(1)}, bf16[128,2048]{1,0:T(8,128)(2,1)S(1)}, u32[]{:S(2)}, u32[]{:S(2)}) collective-permute-start(bf16[128,2048]{1,0:T(8,128)(2,1)S(1)} %pad_maximum_fusion.24), channel_id=1, source_target_pairs={{0,2},{1,3},{2,0},{3,1},{4,6},{5,7},{6,4},{7,5},{8,10},{9,11},{10,... | collective-permute-start | bytes 1572872 | tf_op jit(solution)/shard_map/ppermute | solution.py:401
  312.8 21.5 %collective-permute-start.68 = (bf16[64,2048]{1,0:T(8,128)(2,1)S(1)}, bf16[64,2048]{1,0:T(8,128)(2,1)S(1)}, u32[]{:S(2)}, u32[]{:S(2)}) collective-permute-start(bf16[64,2048]{1,0:T(8,128)(2,1)S(1)} %get-tuple-element.403), channel_id=1, source_target_pairs={{0,16},{4,20},{8,24},{12,28},{16,0},{20,4},{24,8},{28,12},{1,17},{... | collective-permute-start | bytes 786440 | tf_op jit(solution)/shard_map/ppermute | solution.py:364
  322.8 69.6 %collective-permute-start.88 = (bf16[4,256,1536]{2,1,0:T(8,128)(2,1)}, bf16[4,256,1536]{2,1,0:T(8,128)(2,1)S(1)}, u32[]{:S(2)}, u32[]{:S(2)}) collective-permute-start(bf16[4,256,1536]{2,1,0:T(8,128)(2,1)} %pad_maximum_fusion.1), channel_id=1, source_target_pairs={{0,4},{4,0},{8,12},{12,8},{16,20},{20,16},{24,28},{28,24},{1,5},{5... | collective-permute-start | bytes 9437192 | tf_op jit(solution)/shard_map/ppermute | solution.py:390
  339.5 20.0 %collective-permute-start.73 = (bf16[64,2048]{1,0:T(8,128)(2,1)S(1)}, bf16[64,2048]{1,0:T(8,128)(2,1)S(1)}, u32[]{:S(2)}, u32[]{:S(2)}) collective-permute-start(bf16[64,2048]{1,0:T(8,128)(2,1)S(1)} %get-tuple-element.231), channel_id=1, source_target_pairs={{0,16},{4,20},{8,24},{12,28},{16,0},{20,4},{24,8},{28,12},{1,17},{... | collective-permute-start | bytes 786440 | tf_op jit(solution)/shard_map/ppermute | solution.py:364
  379.8 39.2 %collective-permute-start.93 = (bf16[128,2048]{1,0:T(8,128)(2,1)}, bf16[128,2048]{1,0:T(8,128)(2,1)S(1)}, u32[]{:S(2)}, u32[]{:S(2)}) collective-permute-start(bf16[128,2048]{1,0:T(8,128)(2,1)} %fusion.7), channel_id=1, source_target_pairs={{0,2},{1,3},{2,0},{3,1},{4,6},{5,7},{6,4},{7,5},{8,10},{9,11},{10,... | collective-permute-start | bytes 1572872 | tf_op jit(solution)/shard_map/ppermute | solution.py:401
  392.3 26.7 %collective-permute-start.94 = (bf16[128,2048]{1,0:T(8,128)(2,1)}, bf16[128,2048]{1,0:T(8,128)(2,1)}, u32[]{:S(2)}, u32[]{:S(2)}) collective-permute-start(bf16[128,2048]{1,0:T(8,128)(2,1)} %slice.716), channel_id=1, source_target_pairs={{0,2},{1,3},{2,0},{3,1},{4,6},{5,7},{6,4},{7,5},{8,10},{9,11},{10,... | collective-permute-start | bytes 1572872 | tf_op jit(solution)/shard_map/ppermute | solution.py:401
  403.3 76.0 %all-to-all-start.2 = ((bf16[4,256,1536]{2,1,0:T(8,128)(2,1)}), bf16[4,256,1536]{2,1,0:T(8,128)(2,1)}, u32[]{:S(2)}, u32[]{:S(2)}) async-start(bf16[4,256,1536]{2,1,0:T(8,128)(2,1)} %fusion), calls=%async_computation.2 | async-start | bytes 6291456 | tf_op jit(solution)/shard_map/all_to_all | solution.py:380
  450.6 29.5 %collective-permute-start.106 = (bf16[4,256,512]{2,1,0:T(8,128)(2,1)}, bf16[4,256,512]{2,1,0:T(8,128)(2,1)}, u32[]{:S(2)}, u32[]{:S(2)}) collective-permute-start(bf16[4,256,512]{2,1,0:T(8,128)(2,1)} %pad_maximum_fusion.18), channel_id=1, source_target_pairs={{0,4},{4,0},{8,12},{12,8},{16,20},{20,16},{24,28},{28,24},{1,5},{5... | collective-permute-start | bytes 3145736 | tf_op jit(solution)/shard_map/ppermute | solution.py:390
  483.6 18.2 %collective-permute-start.107 = (bf16[64,2048]{1,0:T(8,128)(2,1)}, bf16[64,2048]{1,0:T(8,128)(2,1)S(1)}, u32[]{:S(2)}, u32[]{:S(2)}) collective-permute-start(bf16[64,2048]{1,0:T(8,128)(2,1)} %get-tuple-element.396), channel_id=1, source_target_pairs={{0,24},{4,28},{8,16},{12,20},{16,8},{20,12},{24,0},{28,4},{1,25},{... | collective-permute-start | bytes 786440 | tf_op jit(solution)/shard_map/ppermute | solution.py:364
  485.1 34.0 %collective-permute-start.108 = (bf16[64,2048]{1,0:T(8,128)(2,1)}, bf16[64,2048]{1,0:T(8,128)(2,1)}, u32[]{:S(2)}, u32[]{:S(2)}) collective-permute-start(bf16[64,2048]{1,0:T(8,128)(2,1)} %get-tuple-element.397), channel_id=1, source_target_pairs={{0,16},{4,20},{8,24},{12,28},{16,0},{20,4},{24,8},{28,12},{1,17},{... | collective-permute-start | bytes 786440 | tf_op jit(solution)/shard_map/ppermute | solution.py:364
  492.8 60.4 %all-to-all-start.3 = ((bf16[4,256,512]{2,1,0:T(8,128)(2,1)}), bf16[4,256,512]{2,1,0:T(8,128)(2,1)S(1)}, u32[]{:S(2)}, u32[]{:S(2)}) async-start(bf16[4,256,512]{2,1,0:T(8,128)(2,1)} %fusion.2), calls=%async_computation.3 | async-start | bytes 2097152 | tf_op jit(solution)/shard_map/all_to_all | solution.py:380
  496.4 24.3 %collective-permute-start.109 = (bf16[64,2048]{1,0:T(8,128)(2,1)S(1)}, bf16[64,2048]{1,0:T(8,128)(2,1)S(1)}, u32[]{:S(2)}, u32[]{:S(2)}) collective-permute-start(bf16[64,2048]{1,0:T(8,128)(2,1)S(1)} %slice.721), channel_id=1, source_target_pairs={{0,8},{4,12},{8,0},{12,4},{16,24},{20,28},{24,16},{28,20},{1,9},{5... | collective-permute-start | bytes 786440 | tf_op jit(solution)/shard_map/ppermute | solution.py:364
  499.4 38.8 %collective-permute-start.113 = (bf16[64,2048]{1,0:T(8,128)(2,1)}, bf16[64,2048]{1,0:T(8,128)(2,1)}, u32[]{:S(2)}, u32[]{:S(2)}) collective-permute-start(bf16[64,2048]{1,0:T(8,128)(2,1)} %get-tuple-element.333), channel_id=1, source_target_pairs={{0,24},{4,28},{8,16},{12,20},{16,8},{20,12},{24,0},{28,4},{1,25},{... | collective-permute-start | bytes 786440 | tf_op jit(solution)/shard_map/ppermute | solution.py:364
  526.5 24.6 %collective-permute-start.114 = (bf16[64,2048]{1,0:T(8,128)(2,1)}, bf16[64,2048]{1,0:T(8,128)(2,1)}, u32[]{:S(2)}, u32[]{:S(2)}) collective-permute-start(bf16[64,2048]{1,0:T(8,128)(2,1)} %get-tuple-element.335), channel_id=1, source_target_pairs={{0,16},{4,20},{8,24},{12,28},{16,0},{20,4},{24,8},{28,12},{1,17},{... | collective-permute-start | bytes 786440 | tf_op jit(solution)/shard_map/ppermute | solution.py:364
  (174 other events, 1648.9 us)

commit v4 on v3

--- a/solution.py
+++ b/solution.py
@@ -14,10 +14,10 @@
 LOG_BIAS = math.log(4096.0)
 LOW = jnp.bfloat16
 F32 = jnp.float32
-G_ATTN = (("start", "x1"), ("x1", "x2"))
-G_TOP = (("z1", "z2"), ("z2", "h1"), ("h0", "h2"))
-G_MLP = (("x1", "z0"), ("z0", "h0"))
-G_GRAD_MLP = (("g1n", "m2"), ("back", "r2"))
+G_ATTN = (("start", "x1"), [("x1", "x2")])
+G_TOP = (("z1n", "z2n"), ("z2n", "h0"), ("z2n", "h1"))
+G_MLP = (("x1", "z1"), [("z1", "z2n"), ("z2n", "h1")])
+G_GRAD_MLP = (("g2", "m2"), ("back", "r2"))
 G_OUT = (("m0", "m1"), ("m1", "kvb"), ("m2", "kvb"), ("r2n", "end"))
 G_GRAD_ATTN = (("r1n", "r2n"), ("r2n", "end"))
 VMEM_ASK = 40 * 1024 * 1024
@@ -49,6 +49,10 @@
     return inv_root * (
         grad_normed - normed * jnp.mean(grad_normed * normed, axis=-1, keepdims=True)
     )
+
+
+def pick(stacked, index):
+    return lax.dynamic_index_in_dim(stacked, index, 0, keepdims=False)
 
 
 class Flow:
@@ -99,19 +103,19 @@
     )(scalars, *arrays)
 
 
-def place(scalars, pieces, rows, height, breadth):
-    count = len(pieces)
-    blocks = pieces[0][0].shape[0] // height
+def place(scalars, entries, rows, height, breadth):
+    number = len(entries)
+    blocks = entries[0][0].shape[0] // height
 
     def body(at, *refs):
-        ins, out, sems = refs[:count], refs[count], refs[count + 1]
+        ins, out, sems = refs[:number], refs[number], refs[number + 1]
         copies = []
-        for n, (_, first, spot) in enumerate(pieces):
+        for n, (_, first, target, count, spot) in enumerate(entries):
             for i in range(blocks):
                 copies.append(
                     pltpu.make_async_copy(
-                        ins[n].at[i * height : (i + 1) * height, first : first + breadth],
-                        out.at[at_rows(spot(at, i), height), :],
+                        ins[n].at[i * height : (i + 1) * height, first : first + count],
+                        out.at[at_rows(spot(at, i), height), target : target + count],
                         sems.at[n * blocks + i],
                     )
                 )
@@ -124,8 +128,8 @@
         body,
         [shape_of(rows, breadth, LOW)],
         scalars,
-        [piece[0] for piece in pieces],
-        [pltpu.SemaphoreType.DMA((count * blocks,))],
+        [entry[0] for entry in entries],
+        [pltpu.SemaphoreType.DMA((number * blocks,))],
         ANY_SPEC,
     )[0]
 
@@ -513,10 +517,17 @@
     def row_blocks(weight):
         return weight.reshape(far, weight.shape[0] // far, weight.shape[1]).transpose(0, 2, 1)
 
-    def plan_weight(name, make, far_gates, group_gates):
+    def plan_weight(name, make, breadth, far_gates, group_gates):
         plan(name, *far_gates, make, far_exchange)
-        for g in range(1, groups):
-            plan((name, g), *group_gates, lambda: got[name], lambda v, g=g: group_shift(v, g))
+        step = breadth // len(group_gates)
+        for n, gates in enumerate(group_gates):
+            for g in range(1, groups):
+                plan(
+                    (name, n, g),
+                    *gates,
+                    lambda n=n: got[name][:, :, n * step : (n + 1) * step],
+                    lambda v, g=g: group_shift(v, g),
+                )
 
     def place_weight(name, first, breadth):
         def flat(value):
@@ -525,9 +536,17 @@
         def spot(g):
             return lambda at, i: i * groups + lax.rem(at[2] + groups - g, groups)
 
-        pieces = [(flat(got[name]), first, spot(0))]
-        pieces += [(flat(got[name, g]), first, spot(g)) for g in range(1, groups)]
-        return place(scalars, pieces, width, rows_s, breadth)
+        entries = [(flat(got[name]), first, 0, breadth, spot(0))]
+        for g in range(1, groups):
+            n, start = 0, 0
+            while (name, n, g) in got:
+                piece = flat(got[name, n, g])
+                stop = start + piece.shape[1]
+                begin, end = max(first, start), min(first + breadth, stop)
+                if begin < end:
+                    entries.append((piece, begin - start, begin - first, end - begin, spot(g)))
+                n, start = n + 1, stop
+        return place(scalars, entries, width, rows_s, breadth)
 
     def plan_grad(name, make, group_gates, far_gates):
         made = []
@@ -578,6 +597,7 @@
             + [row_blocks(proj_weight)],
             axis=2,
         ),
+        4 * HD,
         *G_ATTN,
     )
     plan_weight(
@@ -586,13 +606,11 @@
             [column_blocks(w, gain_b) for w in (gate_weight, up_weight)] + [row_blocks(down_weight)],
             axis=2,
         ),
+        3 * hidden,
         *G_MLP,
     )
     finish_top = plan_gather("top", own_grad, *G_TOP)
     gate("start", [])
-    hidden_a = gather_rows(("x0", "x1", "x2"), normed_a.astype(LOW))
-    qkv_full, proj_turned = place_weight("attn", 0, 3 * HD), place_weight("attn", 3 * HD, HD)
-
     far_ids = jnp.arange(far, dtype=jnp.int32)
     positions = (far_ids * groups + group_at)[:, None] * tok + jnp.arange(tok, dtype=jnp.int32)
     frequency = ROPE_BASE ** (-jnp.arange(HD // 2, dtype=F32) * 2.0 / HD)
@@ -610,6 +628,11 @@
             for g in range(groups)
         ]
     )
+    keep("tables", (cosine, signed, query_doc, key_doc), "x0n")
+    hidden_a = gather_rows(("x0", "x1", "x2"), normed_a.astype(LOW))
+    qkv_full, proj_turned = place_weight("attn", 0, 3 * HD), place_weight("attn", 3 * HD, HD)
+
+    cosine, signed, query_doc, key_doc = got["tables"]
     hidden_a = gate("qkv", hidden_a)
     query_rot, key_own = rotate_all(
         scalars, [dot(h, qkv_full) for h in hidden_a], cosine, signed, far, head_size, own
@@ -640,8 +663,6 @@
     plan_scatter(
         "out", lambda: [dot_last(a, down_turned).astype(LOW) for a in active], *G_OUT
     )
-    parts = gate("mlpb", [parts])[0]
-    parts = gate("mlpc", [parts])[0]
     grad_top = finish_top()
     grad_gu = []
     for top, (silu_val, gate_slope) in zip(grad_top, parts):
@@ -656,7 +677,7 @@
     def over_tokens(left_mats, right_mats):
         return sum(dot_first(a, b) for a, b in zip(left_mats, right_mats))
 
-    keep("mlp kept", (hidden_b, grad_gu, grad_top, active), "g1")
+    keep("mlp kept", (hidden_b, grad_gu, grad_top, active), "g1n")
 
     def mlp_grads():
         hidden_b, grad_gu, grad_top, active = got["mlp kept"]

time: 572 us -> 544 us (0.951)
  waiting for transfers between devices: 304 us -> 274 us
  starting transfers between devices: 93.2 us -> 106 us
    ppermute x6 -> x7, waiting for transfers between devices: 47.5 us -> 27.3 us  [group_shift(): lax.ppermute(value, 'seq', [(i * groups + g, i * groups + (g + step) % gr...]
    all_to_all x4, waiting for transfers between devices: 50.9 us -> 44.2 us  [far_exchange(): lax.all_to_all(blocks, 'seq', 0, 0, axis_index_groups=[[i * groups + g fo...]
    unnamed x180 -> x152, local copies, waits for them, and re-layouts: 13.3 us -> 11.1 us
  transfers between devices with their start and end apart: 125 -> 126, of which waited for: 52 -> 54; matrix products, arithmetic and copies ran while one was open for 19% -> 17% of each run, Pallas kernels for 6% -> 5%
where the time goes in v4:
time: 544 us; the launch traced here: 539 us
  waiting for transfers between devices  274 us (50%)
  starting transfers between devices  106 us (19%)
  other arithmetic  47.1 us (9%)
  matrix products  39.2 us (7%)
  local copies, waits for them, and re-layouts  38.5 us (7%)
  Pallas kernels  30.6 us (6%)
    ppermute x24, waiting for transfers between devices, far_swap(): lax.ppermute(value, 'seq', [(i * groups + g, (i ^ step) * groups + g) for...  114 us
    ppermute x91, waiting for transfers between devices, head_swap(): lax.ppermute(value, 'head', [(i, i ^ step) for i in range(head_size)])  88.7 us
    all_to_all x4, waiting for transfers between devices, far_exchange(): lax.all_to_all(blocks, 'seq', 0, 0, axis_index_groups=[[i * groups + g fo...  44.2 us
    ppermute x91, starting transfers between devices, head_swap(): lax.ppermute(value, 'head', [(i, i ^ step) for i in range(head_size)])  41.4 us
    ppermute x24, starting transfers between devices, far_swap(): lax.ppermute(value, 'seq', [(i * groups + g, (i ^ step) * groups + g) for...  36.9 us
    pallas_call x12, Pallas kernels, call(): pl.pallas_call(body, out_shape=outs, in_specs=[SMEM_SPEC] + [space] * len...  30.6 us
    ppermute x7, waiting for transfers between devices, group_shift(): lax.ppermute(value, 'seq', [(i * groups + g, i * groups + (g + step) % gr...  27.3 us
    all_to_all x4, starting transfers between devices, far_exchange(): lax.all_to_all(blocks, 'seq', 0, 0, axis_index_groups=[[i * groups + g fo...  17.6 us
  transfers between devices with their start and end apart: 126, of which 54 were waited for; matrix products, arithmetic and copies ran while one was open for 17% of the time, Pallas kernels for 5%

profile of v4, /device:TPU:0, one launch (start us, length us, event | category | flops | bytes accessed | tf_op | source)
XLA Modules:
  0.0 538.6 jit_solution(12907044526556819546)
XLA Ops:
  3.5 5.0 collective-permute-start.4
  15.2 5.0 all-to-all-start
  28.7 9.9 %collective-permute-done.3 = bf16[64,2048]{1,0:T(8,128)(2,1)} collective-permute-done((bf16[64,2048]{1,0:T(8,128)(2,1)}, bf16[64,2048]{1,0:T(8,128)(2,1)}, u32[]{:S(2)}, u32[]{:S(2)}) %collective-permute-start.3) | collective-permute-done | bytes 262176 | tf_op jit(solution)/shard_map/ppermute | solution.py:368
  41.7 12.0 %all-to-all-done = bf16[4,256,512]{2,1,0:T(8,128)(2,1)} async-done(((bf16[4,256,512]{2,1,0:T(8,128)(2,1)}), bf16[4,256,512]{2,1,0:T(8,128)(2,1)}, u32[]{:S(2)}, u32[]{:S(2)}) %all-to-all-start) | async-done | bytes 1048608 | tf_op jit(solution)/shard_map/all_to_all | solution.py:384
  63.7 7.1 %collective-permute-done.5 = bf16[128,2048]{1,0:T(8,128)(2,1)} collective-permute-done((bf16[128,2048]{1,0:T(8,128)(2,1)}, bf16[128,2048]{1,0:T(8,128)(2,1)}, u32[]{:S(2)}, u32[]{:S(2)}) %collective-permute-start.5) | collective-permute-done | bytes 524320 | tf_op jit(solution)/shard_map/ppermute | solution.py:405
  72.0 6.2 %collective-permute-done.10 = bf16[4,256,512]{2,1,0:T(8,128)(2,1)} collective-permute-done((bf16[4,256,512]{2,1,0:T(8,128)(2,1)}, bf16[4,256,512]{2,1,0:T(8,128)(2,1)}, u32[]{:S(2)}, u32[]{:S(2)}) %collective-permute-start.10) | collective-permute-done | bytes 1048608 | tf_op jit(solution)/shard_map/ppermute | solution.py:394
  91.0 10.0 %collective-permute-done.15.refs_1_ = bf16[1024,256]{1,0:T(8,128)(2,1)} collective-permute-done((bf16[1024,256]{1,0:T(8,128)(2,1)}, bf16[1024,256]{1,0:T(8,128)(2,1)}, u32[]{:S(2)}, u32[]{:S(2)}) %collective-permute-start.15) | collective-permute-done | bytes 524320 | tf_op jit(solution)/shard_map/ppermute | solution.py:394
  114.4 19.1 %all-to-all-done.1 = bf16[4,256,1536]{2,1,0:T(8,128)(2,1)S(1)} async-done(((bf16[4,256,1536]{2,1,0:T(8,128)(2,1)}), bf16[4,256,1536]{2,1,0:T(8,128)(2,1)S(1)}, u32[]{:S(2)}, u32[]{:S(2)}) %all-to-all-start.1) | async-done | bytes 3145760 | tf_op jit(solution)/shard_map/all_to_all | solution.py:384
  146.3 6.2 %collective-permute-done.24 = bf16[128,2048]{1,0:T(8,128)(2,1)S(1)} collective-permute-done((bf16[128,2048]{1,0:T(8,128)(2,1)}, bf16[128,2048]{1,0:T(8,128)(2,1)S(1)}, u32[]{:S(2)}, u32[]{:S(2)}) %collective-permute-start.24) | collective-permute-done | bytes 524320 | tf_op jit(solution)/shard_map/ppermute | solution.py:405
  153.7 6.1 %collective-permute-done.27 = bf16[64,2048]{1,0:T(8,128)(2,1)S(1)} collective-permute-done((bf16[64,2048]{1,0:T(8,128)(2,1)S(1)}, bf16[64,2048]{1,0:T(8,128)(2,1)S(1)}, u32[]{:S(2)}, u32[]{:S(2)}) %collective-permute-start.27) | collective-permute-done | bytes 262176 | tf_op jit(solution)/shard_map/ppermute | solution.py:368
  163.9 13.5 %collective-permute-done.28 = bf16[64,2048]{1,0:T(8,128)(2,1)S(1)} collective-permute-done((bf16[64,2048]{1,0:T(8,128)(2,1)S(1)}, bf16[64,2048]{1,0:T(8,128)(2,1)S(1)}, u32[]{:S(2)}, u32[]{:S(2)}) %collective-permute-start.28) | collective-permute-done | bytes 262176 | tf_op jit(solution)/shard_map/ppermute | solution.py:368
  181.0 6.1 %collective-permute-done.31 = bf16[64,2048]{1,0:T(8,128)(2,1)S(1)} collective-permute-done((bf16[64,2048]{1,0:T(8,128)(2,1)S(1)}, bf16[64,2048]{1,0:T(8,128)(2,1)S(1)}, u32[]{:S(2)}, u32[]{:S(2)}) %collective-permute-start.31) | collective-permute-done | bytes 262176 | tf_op jit(solution)/shard_map/ppermute | solution.py:368
  201.7 5.4 collective-permute-done.38
  208.0 4.4 collective-permute-done.34
  213.5 8.9 %collective-permute-done.37 = bf16[64,2048]{1,0:T(8,128)(2,1)S(1)} collective-permute-done((bf16[64,2048]{1,0:T(8,128)(2,1)S(1)}, bf16[64,2048]{1,0:T(8,128)(2,1)S(1)}, u32[]{:S(2)}, u32[]{:S(2)}) %collective-permute-start.37) | collective-permute-done | bytes 262176 | tf_op jit(solution)/shard_map/ppermute | solution.py:368
  231.9 8.2 %collective-permute-done.41 = bf16[128,2048]{1,0:T(8,128)(2,1)S(1)} collective-permute-done((bf16[128,2048]{1,0:T(8,128)(2,1)S(1)}, bf16[128,2048]{1,0:T(8,128)(2,1)S(1)}, u32[]{:S(2)}, u32[]{:S(2)}) %collective-permute-start.41) | collective-permute-done | bytes 524320 | tf_op jit(solution)/shard_map/ppermute | solution.py:405
  284.7 8.6 %collective-permute-done.67 = bf16[128,2048]{1,0:T(8,128)(2,1)S(1)} collective-permute-done((bf16[128,2048]{1,0:T(8,128)(2,1)S(1)}, bf16[128,2048]{1,0:T(8,128)(2,1)S(1)}, u32[]{:S(2)}, u32[]{:S(2)}) %collective-permute-start.67) | collective-permute-done | bytes 524320 | tf_op jit(solution)/shard_map/ppermute | solution.py:405
  296.2 10.8 %collective-permute-done.69 = bf16[64,2048]{1,0:T(8,128)(2,1)S(1)} collective-permute-done((bf16[64,2048]{1,0:T(8,128)(2,1)S(1)}, bf16[64,2048]{1,0:T(8,128)(2,1)S(1)}, u32[]{:S(2)}, u32[]{:S(2)}) %collective-permute-start.69) | collective-permute-done | bytes 262176 | tf_op jit(solution)/shard_map/ppermute | solution.py:368
  320.4 11.4 %collective-permute-done.74 = bf16[64,2048]{1,0:T(8,128)(2,1)S(1)} collective-permute-done((bf16[64,2048]{1,0:T(8,128)(2,1)S(1)}, bf16[64,2048]{1,0:T(8,128)(2,1)S(1)}, u32[]{:S(2)}, u32[]{:S(2)}) %collective-permute-start.74) | collective-permute-done | bytes 262176 | tf_op jit(solution)/shard_map/ppermute | solution.py:368
  335.5 7.0 %collective-permute-done.72 = bf16[64,2048]{1,0:T(8,128)(2,1)S(1)} collective-permute-done((bf16[64,2048]{1,0:T(8,128)(2,1)S(1)}, bf16[64,2048]{1,0:T(8,128)(2,1)S(1)}, u32[]{:S(2)}, u32[]{:S(2)}) %collective-permute-start.72) | collective-permute-done | bytes 262176 | tf_op jit(solution)/shard_map/ppermute | solution.py:405
  342.4 4.7 collective-permute-done.73
  352.4 10.5 %collective-permute-done.84 = bf16[128,2048]{1,0:T(8,128)(2,1)S(1)} collective-permute-done((bf16[128,2048]{1,0:T(8,128)(2,1)S(1)}, bf16[128,2048]{1,0:T(8,128)(2,1)S(1)}, u32[]{:S(2)}, u32[]{:S(2)}) %collective-permute-start.84) | collective-permute-done | bytes 524320 | tf_op jit(solution)/shard_map/ppermute | solution.py:405
  366.0 4.6 fusion
  375.8 5.2 all-to-all-start.2
  384.0 7.6 %shard_map.209 = (f32[1024,128]{1,0:T(8,128)S(1)}, f32[1024,256]{1,0:T(8,128)S(1)}, bf16[1024,256]{1,0:T(8,128)(2,1)S(1)}) custom-call(s32[3]{0:T(128)S(1)} %pad_add_fusion.1.at, bf16[1024,128]{1,0:T(8,128)(2,1)S(1)} %copy-done.21, s32[1024,1]{1,0:T(8,128)S(1)} %copy-done.17, s32[2,1024]{1,0:T(2,128)S(1)} %pad_add_fusion.key_doc_ref, ...), custom_call_target="tpu_custom_call" | custom-call | flops 1342177280 | bytes 3682304 | tf_op jit(solution)/shard_map/pallas_call | solution.py:95
  394.7 11.0 %collective-permute-done.96.refs_1_ = bf16[1024,256]{1,0:T(8,128)(2,1)S(1)} collective-permute-done((bf16[1024,256]{1,0:T(8,128)(2,1)S(1)}, bf16[1024,256]{1,0:T(8,128)(2,1)S(1)}, u32[]{:S(2)}, u32[]{:S(2)}) %collective-permute-start.96) | collective-permute-done | bytes 524320 | tf_op jit(solution)/shard_map/ppermute | solution.py:394
  429.9 8.6 %collective-permute-done.105 = bf16[128,2048]{1,0:T(8,128)(2,1)S(1)} collective-permute-done((bf16[128,2048]{1,0:T(8,128)(2,1)S(1)}, bf16[128,2048]{1,0:T(8,128)(2,1)S(1)}, u32[]{:S(2)}, u32[]{:S(2)}) %collective-permute-start.105) | collective-permute-done | bytes 524320 | tf_op jit(solution)/shard_map/ppermute | solution.py:405
  438.7 13.1 %all-to-all-done.2.piece_ref = bf16[4,256,1536]{2,1,0:T(8,128)(2,1)} async-done(((bf16[4,256,1536]{2,1,0:T(8,128)(2,1)}), bf16[4,256,1536]{2,1,0:T(8,128)(2,1)}, u32[]{:S(2)}, u32[]{:S(2)}) %all-to-all-start.2) | async-done | bytes 3145760 | tf_op jit(solution)/shard_map/all_to_all | solution.py:384
  457.8 7.3 %collective-permute-done.106 = bf16[128,2048]{1,0:T(8,128)(2,1)S(1)} collective-permute-done((bf16[128,2048]{1,0:T(8,128)(2,1)}, bf16[128,2048]{1,0:T(8,128)(2,1)S(1)}, u32[]{:S(2)}, u32[]{:S(2)}) %collective-permute-start.106) | collective-permute-done | bytes 524320 | tf_op jit(solution)/shard_map/ppermute | solution.py:405
  474.2 17.6 %collective-permute-done.109 = bf16[64,2048]{1,0:T(8,128)(2,1)} collective-permute-done((bf16[64,2048]{1,0:T(8,128)(2,1)}, bf16[64,2048]{1,0:T(8,128)(2,1)}, u32[]{:S(2)}, u32[]{:S(2)}) %collective-permute-start.109) | collective-permute-done | bytes 262176 | tf_op jit(solution)/shard_map/ppermute | solution.py:368
  503.4 5.2 shard_map.214
  510.8 12.9 %collective-permute-done.115 = bf16[64,2048]{1,0:T(8,128)(2,1)} collective-permute-done((bf16[64,2048]{1,0:T(8,128)(2,1)}, bf16[64,2048]{1,0:T(8,128)(2,1)}, u32[]{:S(2)}, u32[]{:S(2)}) %collective-permute-start.115) | collective-permute-done | bytes 262176 | tf_op jit(solution)/shard_map/ppermute | solution.py:368
  (557 shorter events, 256.4 us)
Async XLA Ops:
  3.5 25.2 %collective-permute-start.4 = (bf16[64,2048]{1,0:T(8,128)(2,1)}, bf16[64,2048]{1,0:T(8,128)(2,1)}, u32[]{:S(2)}, u32[]{:S(2)}) collective-permute-start(bf16[64,2048]{1,0:T(8,128)(2,1)} %fusion.13), channel_id=1, source_target_pairs={{0,24},{4,28},{8,16},{12,20},{16,8},{20,12},{24,0},{28,4},{1,25},{... | collective-permute-start | bytes 786440 | tf_op jit(solution)/shard_map/ppermute | solution.py:368
  8.6 30.0 %collective-permute-start.3 = (bf16[64,2048]{1,0:T(8,128)(2,1)}, bf16[64,2048]{1,0:T(8,128)(2,1)}, u32[]{:S(2)}, u32[]{:S(2)}) collective-permute-start(bf16[64,2048]{1,0:T(8,128)(2,1)} %fusion.13), channel_id=1, source_target_pairs={{0,16},{4,20},{8,24},{12,28},{16,0},{20,4},{24,8},{28,12},{1,17},{... | collective-permute-start | bytes 786440 | tf_op jit(solution)/shard_map/ppermute | solution.py:368
  8.6 31.9 %collective-permute-start.1 = (bf16[64,2048]{1,0:T(8,128)(2,1)}, bf16[64,2048]{1,0:T(8,128)(2,1)}, u32[]{:S(2)}, u32[]{:S(2)}) collective-permute-start(bf16[64,2048]{1,0:T(8,128)(2,1)} %fusion.13), channel_id=1, source_target_pairs={{0,2},{1,3},{2,0},{3,1},{4,6},{5,7},{6,4},{7,5},{8,10},{9,11},{10,... | collective-permute-start | bytes 786440 | tf_op jit(solution)/shard_map/ppermute | solution.py:405
  10.1 18.1 %collective-permute-start = (bf16[64,2048]{1,0:T(8,128)(2,1)}, bf16[64,2048]{1,0:T(8,128)(2,1)}, u32[]{:S(2)}, u32[]{:S(2)}) collective-permute-start(bf16[64,2048]{1,0:T(8,128)(2,1)} %fusion.13), channel_id=1, source_target_pairs={{0,8},{4,12},{8,0},{12,4},{16,24},{20,28},{24,16},{28,20},{1,9},{5... | collective-permute-start | bytes 786440 | tf_op jit(solution)/shard_map/ppermute | solution.py:368
  15.2 38.5 %all-to-all-start = ((bf16[4,256,512]{2,1,0:T(8,128)(2,1)}), bf16[4,256,512]{2,1,0:T(8,128)(2,1)}, u32[]{:S(2)}, u32[]{:S(2)}) async-start(bf16[4,256,512]{2,1,0:T(8,128)(2,1)} %pad_maximum_fusion.6), calls=%async_computation | async-start | bytes 2097152 | tf_op jit(solution)/shard_map/all_to_all | solution.py:384
  53.7 24.5 %collective-permute-start.10 = (bf16[4,256,512]{2,1,0:T(8,128)(2,1)}, bf16[4,256,512]{2,1,0:T(8,128)(2,1)}, u32[]{:S(2)}, u32[]{:S(2)}) collective-permute-start(bf16[4,256,512]{2,1,0:T(8,128)(2,1)} %all-to-all-done), channel_id=1, source_target_pairs={{0,4},{4,0},{8,12},{12,8},{16,20},{20,16},{24,28},{28,24},{1,5},{5... | collective-permute-start | bytes 3145736 | tf_op jit(solution)/shard_map/ppermute | solution.py:394
  58.4 75.1 %all-to-all-start.1 = ((bf16[4,256,1536]{2,1,0:T(8,128)(2,1)}), bf16[4,256,1536]{2,1,0:T(8,128)(2,1)S(1)}, u32[]{:S(2)}, u32[]{:S(2)}) async-start(bf16[4,256,1536]{2,1,0:T(8,128)(2,1)} %pad_maximum_fusion), calls=%async_computation.1 | async-start | bytes 6291456 | tf_op jit(solution)/shard_map/all_to_all | solution.py:384
  139.6 38.0 %collective-permute-start.26 = (bf16[4,256,768]{2,1,0:T(8,128)(2,1)S(1)}, bf16[4,256,768]{2,1,0:T(8,128)(2,1)S(1)}, u32[]{:S(2)}, u32[]{:S(2)}) collective-permute-start(bf16[4,256,768]{2,1,0:T(8,128)(2,1)S(1)} %copy-done.50), channel_id=1, source_target_pairs={{0,4},{4,0},{8,12},{12,8},{16,20},{20,16},{24,28},{28,24},{1,5},{5... | collective-permute-start | bytes 4718600 | tf_op jit(solution)/shard_map/ppermute | solution.py:394
  141.8 20.4 %collective-permute-start.29 = (bf16[64,2048]{1,0:T(8,128)(2,1)S(1)}, bf16[64,2048]{1,0:T(8,128)(2,1)S(1)}, u32[]{:S(2)}, u32[]{:S(2)}) collective-permute-start(bf16[64,2048]{1,0:T(8,128)(2,1)S(1)} %constant_dynamic-slice_fusion), channel_id=1, source_target_pairs={{0,24},{4,28},{8,16},{12,20},{16,8},{20,12},{24,0},{28,4},{1,25},{... | collective-permute-start | bytes 786440 | tf_op jit(solution)/shard_map/ppermute | solution.py:368
  143.3 34.1 %collective-permute-start.28 = (bf16[64,2048]{1,0:T(8,128)(2,1)S(1)}, bf16[64,2048]{1,0:T(8,128)(2,1)S(1)}, u32[]{:S(2)}, u32[]{:S(2)}) collective-permute-start(bf16[64,2048]{1,0:T(8,128)(2,1)S(1)} %constant_dynamic-slice_fusion), channel_id=1, source_target_pairs={{0,16},{4,20},{8,24},{12,28},{16,0},{20,4},{24,8},{28,12},{1,17},{... | collective-permute-start | bytes 786440 | tf_op jit(solution)/shard_map/ppermute | solution.py:368
  152.6 24.8 %collective-permute-start.25 = (bf16[128,2048]{1,0:T(8,128)(2,1)S(1)}, bf16[128,2048]{1,0:T(8,128)(2,1)S(1)}, u32[]{:S(2)}, u32[]{:S(2)}) collective-permute-start(bf16[128,2048]{1,0:T(8,128)(2,1)S(1)} %slice.724), channel_id=1, source_target_pairs={{0,2},{1,3},{2,0},{3,1},{4,6},{5,7},{6,4},{7,5},{8,10},{9,11},{10,... | collective-permute-start | bytes 1572872 | tf_op jit(solution)/shard_map/ppermute | solution.py:405
  159.8 20.1 %collective-permute-start.30 = (bf16[64,2048]{1,0:T(8,128)(2,1)S(1)}, bf16[64,2048]{1,0:T(8,128)(2,1)S(1)}, u32[]{:S(2)}, u32[]{:S(2)}) collective-permute-start(bf16[64,2048]{1,0:T(8,128)(2,1)S(1)} %get-tuple-element.414), channel_id=1, source_target_pairs={{0,24},{4,28},{8,16},{12,20},{16,8},{20,12},{24,0},{28,4},{1,25},{... | collective-permute-start | bytes 786440 | tf_op jit(solution)/shard_map/ppermute | solution.py:368
  162.2 24.9 %collective-permute-start.31 = (bf16[64,2048]{1,0:T(8,128)(2,1)S(1)}, bf16[64,2048]{1,0:T(8,128)(2,1)S(1)}, u32[]{:S(2)}, u32[]{:S(2)}) collective-permute-start(bf16[64,2048]{1,0:T(8,128)(2,1)S(1)} %get-tuple-element.415), channel_id=1, source_target_pairs={{0,16},{4,20},{8,24},{12,28},{16,0},{20,4},{24,8},{28,12},{1,17},{... | collective-permute-start | bytes 786440 | tf_op jit(solution)/shard_map/ppermute | solution.py:368
  179.1 20.2 %collective-permute-start.54 = (bf16[64,2048]{1,0:T(8,128)(2,1)S(1)}, bf16[64,2048]{1,0:T(8,128)(2,1)S(1)}, u32[]{:S(2)}, u32[]{:S(2)}) collective-permute-start(bf16[64,2048]{1,0:T(8,128)(2,1)S(1)} %collective-permute-done.28), channel_id=1, source_target_pairs={{0,1},{1,0},{2,3},{3,2},{4,5},{5,4},{6,7},{7,6},{8,9},{9,8},{10,11... | collective-permute-start | bytes 786440 | tf_op jit(solution)/shard_map/ppermute | solution.py:405
  179.5 21.1 %collective-permute-start.55 = (bf16[64,2048]{1,0:T(8,128)(2,1)S(1)}, bf16[64,2048]{1,0:T(8,128)(2,1)S(1)}, u32[]{:S(2)}, u32[]{:S(2)}) collective-permute-start(bf16[64,2048]{1,0:T(8,128)(2,1)S(1)} %collective-permute-done.29), channel_id=1, source_target_pairs={{0,1},{1,0},{2,3},{3,2},{4,5},{5,4},{6,7},{7,6},{8,9},{9,8},{10,11... | collective-permute-start | bytes 786440 | tf_op jit(solution)/shard_map/ppermute | solution.py:405
  187.1 38.0 %collective-permute-start.39 = (bf16[4,256,768]{2,1,0:T(8,128)(2,1)S(1)}, bf16[4,256,768]{2,1,0:T(8,128)(2,1)S(1)}, u32[]{:S(2)}, u32[]{:S(2)}) collective-permute-start(bf16[4,256,768]{2,1,0:T(8,128)(2,1)S(1)} %slice.488), channel_id=1, source_target_pairs={{0,4},{4,0},{8,12},{12,8},{16,20},{20,16},{24,28},{28,24},{1,5},{5... | collective-permute-start | bytes 4718600 | tf_op jit(solution)/shard_map/ppermute | solution.py:394
  199.4 23.0 %collective-permute-start.37 = (bf16[64,2048]{1,0:T(8,128)(2,1)S(1)}, bf16[64,2048]{1,0:T(8,128)(2,1)S(1)}, u32[]{:S(2)}, u32[]{:S(2)}) collective-permute-start(bf16[64,2048]{1,0:T(8,128)(2,1)S(1)} %multiply_convert_fusion.14), channel_id=1, source_target_pairs={{0,16},{4,20},{8,24},{12,28},{16,0},{20,4},{24,8},{28,12},{1,17},{... | collective-permute-start | bytes 786440 | tf_op jit(solution)/shard_map/ppermute | solution.py:368
  200.6 24.5 %collective-permute-start.40 = (bf16[128,2048]{1,0:T(8,128)(2,1)S(1)}, bf16[128,2048]{1,0:T(8,128)(2,1)S(1)}, u32[]{:S(2)}, u32[]{:S(2)}) collective-permute-start(bf16[128,2048]{1,0:T(8,128)(2,1)S(1)} %pad_maximum_fusion.24), channel_id=1, source_target_pairs={{0,2},{1,3},{2,0},{3,1},{4,6},{5,7},{6,4},{7,5},{8,10},{9,11},{10,... | collective-permute-start | bytes 1572872 | tf_op jit(solution)/shard_map/ppermute | solution.py:405
  284.7 22.3 %collective-permute-start.69 = (bf16[64,2048]{1,0:T(8,128)(2,1)S(1)}, bf16[64,2048]{1,0:T(8,128)(2,1)S(1)}, u32[]{:S(2)}, u32[]{:S(2)}) collective-permute-start(bf16[64,2048]{1,0:T(8,128)(2,1)S(1)} %get-tuple-element.409), channel_id=1, source_target_pairs={{0,16},{4,20},{8,24},{12,28},{16,0},{20,4},{24,8},{28,12},{1,17},{... | collective-permute-start | bytes 786440 | tf_op jit(solution)/shard_map/ppermute | solution.py:368
  294.7 68.4 %collective-permute-start.89 = (bf16[4,256,1536]{2,1,0:T(8,128)(2,1)S(1)}, bf16[4,256,1536]{2,1,0:T(8,128)(2,1)S(1)}, u32[]{:S(2)}, u32[]{:S(2)}) collective-permute-start(bf16[4,256,1536]{2,1,0:T(8,128)(2,1)S(1)} %pad_maximum_fusion.1), channel_id=1, source_target_pairs={{0,4},{4,0},{8,12},{12,8},{16,20},{20,16},{24,28},{28,24},{1,5},{5... | collective-permute-start | bytes 9437192 | tf_op jit(solution)/shard_map/ppermute | solution.py:394
  311.7 20.2 %collective-permute-start.74 = (bf16[64,2048]{1,0:T(8,128)(2,1)S(1)}, bf16[64,2048]{1,0:T(8,128)(2,1)S(1)}, u32[]{:S(2)}, u32[]{:S(2)}) collective-permute-start(bf16[64,2048]{1,0:T(8,128)(2,1)S(1)} %get-tuple-element.241), channel_id=1, source_target_pairs={{0,16},{4,20},{8,24},{12,28},{16,0},{20,4},{24,8},{28,12},{1,17},{... | collective-permute-start | bytes 786440 | tf_op jit(solution)/shard_map/ppermute | solution.py:368
  315.3 16.6 %collective-permute-start.71 = (bf16[64,2048]{1,0:T(8,128)(2,1)S(1)}, bf16[64,2048]{1,0:T(8,128)(2,1)S(1)}, u32[]{:S(2)}, u32[]{:S(2)}) collective-permute-start(bf16[64,2048]{1,0:T(8,128)(2,1)S(1)} %get-tuple-element.241), channel_id=1, source_target_pairs={{0,8},{4,12},{8,0},{12,4},{16,24},{20,28},{24,16},{28,20},{1,9},{5... | collective-permute-start | bytes 786440 | tf_op jit(solution)/shard_map/ppermute | solution.py:368
  351.3 40.4 %collective-permute-start.94 = (bf16[128,2048]{1,0:T(8,128)(2,1)}, bf16[128,2048]{1,0:T(8,128)(2,1)S(1)}, u32[]{:S(2)}, u32[]{:S(2)}) collective-permute-start(bf16[128,2048]{1,0:T(8,128)(2,1)} %fusion.7), channel_id=1, source_target_pairs={{0,2},{1,3},{2,0},{3,1},{4,6},{5,7},{6,4},{7,5},{8,10},{9,11},{10,... | collective-permute-start | bytes 1572872 | tf_op jit(solution)/shard_map/ppermute | solution.py:405
  364.8 26.9 %collective-permute-start.95 = (bf16[128,2048]{1,0:T(8,128)(2,1)}, bf16[128,2048]{1,0:T(8,128)(2,1)}, u32[]{:S(2)}, u32[]{:S(2)}) collective-permute-start(bf16[128,2048]{1,0:T(8,128)(2,1)} %slice.721), channel_id=1, source_target_pairs={{0,2},{1,3},{2,0},{3,1},{4,6},{5,7},{6,4},{7,5},{8,10},{9,11},{10,... | collective-permute-start | bytes 1572872 | tf_op jit(solution)/shard_map/ppermute | solution.py:405
  375.8 76.0 %all-to-all-start.2 = ((bf16[4,256,1536]{2,1,0:T(8,128)(2,1)}), bf16[4,256,1536]{2,1,0:T(8,128)(2,1)}, u32[]{:S(2)}, u32[]{:S(2)}) async-start(bf16[4,256,1536]{2,1,0:T(8,128)(2,1)} %fusion), calls=%async_computation.2 | async-start | bytes 6291456 | tf_op jit(solution)/shard_map/all_to_all | solution.py:384
  423.1 29.7 %collective-permute-start.107 = (bf16[4,256,512]{2,1,0:T(8,128)(2,1)}, bf16[4,256,512]{2,1,0:T(8,128)(2,1)}, u32[]{:S(2)}, u32[]{:S(2)}) collective-permute-start(bf16[4,256,512]{2,1,0:T(8,128)(2,1)} %pad_maximum_fusion.18), channel_id=1, source_target_pairs={{0,4},{4,0},{8,12},{12,8},{16,20},{20,16},{24,28},{28,24},{1,5},{5... | collective-permute-start | bytes 3145736 | tf_op jit(solution)/shard_map/ppermute | solution.py:394
  456.3 17.9 %collective-permute-start.108 = (bf16[64,2048]{1,0:T(8,128)(2,1)}, bf16[64,2048]{1,0:T(8,128)(2,1)S(1)}, u32[]{:S(2)}, u32[]{:S(2)}) collective-permute-start(bf16[64,2048]{1,0:T(8,128)(2,1)} %get-tuple-element.402), channel_id=1, source_target_pairs={{0,24},{4,28},{8,16},{12,20},{16,8},{20,12},{24,0},{28,4},{1,25},{... | collective-permute-start | bytes 786440 | tf_op jit(solution)/shard_map/ppermute | solution.py:368
  457.8 34.0 %collective-permute-start.109 = (bf16[64,2048]{1,0:T(8,128)(2,1)}, bf16[64,2048]{1,0:T(8,128)(2,1)}, u32[]{:S(2)}, u32[]{:S(2)}) collective-permute-start(bf16[64,2048]{1,0:T(8,128)(2,1)} %get-tuple-element.403), channel_id=1, source_target_pairs={{0,16},{4,20},{8,24},{12,28},{16,0},{20,4},{24,8},{28,12},{1,17},{... | collective-permute-start | bytes 786440 | tf_op jit(solution)/shard_map/ppermute | solution.py:368
  465.2 60.6 %all-to-all-start.3 = ((bf16[4,256,512]{2,1,0:T(8,128)(2,1)}), bf16[4,256,512]{2,1,0:T(8,128)(2,1)S(1)}, u32[]{:S(2)}, u32[]{:S(2)}) async-start(bf16[4,256,512]{2,1,0:T(8,128)(2,1)} %fusion.2), calls=%async_computation.3 | async-start | bytes 2097152 | tf_op jit(solution)/shard_map/all_to_all | solution.py:384
  468.8 24.3 %collective-permute-start.110 = (bf16[64,2048]{1,0:T(8,128)(2,1)S(1)}, bf16[64,2048]{1,0:T(8,128)(2,1)S(1)}, u32[]{:S(2)}, u32[]{:S(2)}) collective-permute-start(bf16[64,2048]{1,0:T(8,128)(2,1)S(1)} %slice.726), channel_id=1, source_target_pairs={{0,8},{4,12},{8,0},{12,4},{16,24},{20,28},{24,16},{28,20},{1,9},{5... | collective-permute-start | bytes 786440 | tf_op jit(solution)/shard_map/ppermute | solution.py:368
  471.8 39.0 %collective-permute-start.114 = (bf16[64,2048]{1,0:T(8,128)(2,1)}, bf16[64,2048]{1,0:T(8,128)(2,1)}, u32[]{:S(2)}, u32[]{:S(2)}) collective-permute-start(bf16[64,2048]{1,0:T(8,128)(2,1)} %get-tuple-element.343), channel_id=1, source_target_pairs={{0,24},{4,28},{8,16},{12,20},{16,8},{20,12},{24,0},{28,4},{1,25},{... | collective-permute-start | bytes 786440 | tf_op jit(solution)/shard_map/ppermute | solution.py:368
  499.2 24.5 %collective-permute-start.115 = (bf16[64,2048]{1,0:T(8,128)(2,1)}, bf16[64,2048]{1,0:T(8,128)(2,1)}, u32[]{:S(2)}, u32[]{:S(2)}) collective-permute-start(bf16[64,2048]{1,0:T(8,128)(2,1)} %get-tuple-element.345), channel_id=1, source_target_pairs={{0,16},{4,20},{8,24},{12,28},{16,0},{20,4},{24,8},{28,12},{1,17},{... | collective-permute-start | bytes 786440 | tf_op jit(solution)/shard_map/ppermute | solution.py:368
  (161 other events, 1457.6 us)

commit v5 on v4

--- a/solution.py
+++ b/solution.py
@@ -17,7 +17,7 @@
 G_ATTN = (("start", "x1"), [("x1", "x2")])
 G_TOP = (("z1n", "z2n"), ("z2n", "h0"), ("z2n", "h1"))
 G_MLP = (("x1", "z1"), [("z1", "z2n"), ("z2n", "h1")])
-G_GRAD_MLP = (("g2", "m2"), ("back", "r2"))
+G_GRAD_MLP = (("g2", "m2"), ("back", "r2n"))
 G_OUT = (("m0", "m1"), ("m1", "kvb"), ("m2", "kvb"), ("r2n", "end"))
 G_GRAD_ATTN = (("r1n", "r2n"), ("r2n", "end"))
 VMEM_ASK = 40 * 1024 * 1024

time: 544 us -> 540 us (level)
    ppermute x7, waiting for transfers between devices: 27.3 us -> 35.5 us  [group_shift(): lax.ppermute(value, 'seq', [(i * groups + g, i * groups + (g + step) % gr...]
  transfers between devices with their start and end apart: 126 -> 126, of which waited for: 54 -> 55; matrix products, arithmetic and copies ran while one was open for 17% -> 16% of each run, Pallas kernels for 5% -> 5%
where the time goes in v5:
time: 540 us; the launch traced here: 534 us
  waiting for transfers between devices  275 us (51%)
  starting transfers between devices  108 us (20%)
  other arithmetic  43.8 us (8%)
  matrix products  39.2 us (7%)
  local copies, waits for them, and re-layouts  34.7 us (6%)
  Pallas kernels  30.6 us (6%)
    ppermute x24, waiting for transfers between devices, far_swap(): lax.ppermute(value, 'seq', [(i * groups + g, (i ^ step) * groups + g) for...  111 us
    ppermute x91, waiting for transfers between devices, head_swap(): lax.ppermute(value, 'head', [(i, i ^ step) for i in range(head_size)])  83.4 us
    all_to_all x4, waiting for transfers between devices, far_exchange(): lax.all_to_all(blocks, 'seq', 0, 0, axis_index_groups=[[i * groups + g fo...  44.8 us
    ppermute x91, starting transfers between devices, head_swap(): lax.ppermute(value, 'head', [(i, i ^ step) for i in range(head_size)])  41.5 us
    ppermute x24, starting transfers between devices, far_swap(): lax.ppermute(value, 'seq', [(i * groups + g, (i ^ step) * groups + g) for...  39.3 us
    ppermute x7, waiting for transfers between devices, group_shift(): lax.ppermute(value, 'seq', [(i * groups + g, i * groups + (g + step) % gr...  35.5 us
    pallas_call x12, Pallas kernels, call(): pl.pallas_call(body, out_shape=outs, in_specs=[SMEM_SPEC] + [space] * len...  30.6 us
    all_to_all x4, starting transfers between devices, far_exchange(): lax.all_to_all(blocks, 'seq', 0, 0, axis_index_groups=[[i * groups + g fo...  17.6 us
  transfers between devices with their start and end apart: 126, of which 55 were waited for; matrix products, arithmetic and copies ran while one was open for 16% of the time, Pallas kernels for 5%

profile of v5, /device:TPU:0, one launch (start us, length us, event | category | flops | bytes accessed | tf_op | source)
XLA Modules:
  0.0 534.1 jit_solution(7651919835354692131)
XLA Ops:
  3.5 5.0 collective-permute-start.4
  15.2 5.0 all-to-all-start
  28.7 9.9 %collective-permute-done.3 = bf16[64,2048]{1,0:T(8,128)(2,1)} collective-permute-done((bf16[64,2048]{1,0:T(8,128)(2,1)}, bf16[64,2048]{1,0:T(8,128)(2,1)}, u32[]{:S(2)}, u32[]{:S(2)}) %collective-permute-start.3) | collective-permute-done | bytes 262176 | tf_op jit(solution)/shard_map/ppermute | solution.py:368
  41.7 12.0 %all-to-all-done = bf16[4,256,512]{2,1,0:T(8,128)(2,1)} async-done(((bf16[4,256,512]{2,1,0:T(8,128)(2,1)}), bf16[4,256,512]{2,1,0:T(8,128)(2,1)}, u32[]{:S(2)}, u32[]{:S(2)}) %all-to-all-start) | async-done | bytes 1048608 | tf_op jit(solution)/shard_map/all_to_all | solution.py:384
  63.7 7.1 %collective-permute-done.5 = bf16[128,2048]{1,0:T(8,128)(2,1)} collective-permute-done((bf16[128,2048]{1,0:T(8,128)(2,1)}, bf16[128,2048]{1,0:T(8,128)(2,1)}, u32[]{:S(2)}, u32[]{:S(2)}) %collective-permute-start.5) | collective-permute-done | bytes 524320 | tf_op jit(solution)/shard_map/ppermute | solution.py:405
  72.0 6.2 %collective-permute-done.10 = bf16[4,256,512]{2,1,0:T(8,128)(2,1)} collective-permute-done((bf16[4,256,512]{2,1,0:T(8,128)(2,1)}, bf16[4,256,512]{2,1,0:T(8,128)(2,1)}, u32[]{:S(2)}, u32[]{:S(2)}) %collective-permute-start.10) | collective-permute-done | bytes 1048608 | tf_op jit(solution)/shard_map/ppermute | solution.py:394
  91.0 10.0 %collective-permute-done.15.refs_1_ = bf16[1024,256]{1,0:T(8,128)(2,1)} collective-permute-done((bf16[1024,256]{1,0:T(8,128)(2,1)}, bf16[1024,256]{1,0:T(8,128)(2,1)}, u32[]{:S(2)}, u32[]{:S(2)}) %collective-permute-start.15) | collective-permute-done | bytes 524320 | tf_op jit(solution)/shard_map/ppermute | solution.py:394
  114.4 19.1 %all-to-all-done.1 = bf16[4,256,1536]{2,1,0:T(8,128)(2,1)S(1)} async-done(((bf16[4,256,1536]{2,1,0:T(8,128)(2,1)}), bf16[4,256,1536]{2,1,0:T(8,128)(2,1)S(1)}, u32[]{:S(2)}, u32[]{:S(2)}) %all-to-all-start.1) | async-done | bytes 3145760 | tf_op jit(solution)/shard_map/all_to_all | solution.py:384
  146.3 6.2 %collective-permute-done.24 = bf16[128,2048]{1,0:T(8,128)(2,1)S(1)} collective-permute-done((bf16[128,2048]{1,0:T(8,128)(2,1)}, bf16[128,2048]{1,0:T(8,128)(2,1)S(1)}, u32[]{:S(2)}, u32[]{:S(2)}) %collective-permute-start.24) | collective-permute-done | bytes 524320 | tf_op jit(solution)/shard_map/ppermute | solution.py:405
  153.7 6.1 %collective-permute-done.27 = bf16[64,2048]{1,0:T(8,128)(2,1)S(1)} collective-permute-done((bf16[64,2048]{1,0:T(8,128)(2,1)S(1)}, bf16[64,2048]{1,0:T(8,128)(2,1)S(1)}, u32[]{:S(2)}, u32[]{:S(2)}) %collective-permute-start.27) | collective-permute-done | bytes 262176 | tf_op jit(solution)/shard_map/ppermute | solution.py:368
  163.9 13.5 %collective-permute-done.28 = bf16[64,2048]{1,0:T(8,128)(2,1)S(1)} collective-permute-done((bf16[64,2048]{1,0:T(8,128)(2,1)S(1)}, bf16[64,2048]{1,0:T(8,128)(2,1)S(1)}, u32[]{:S(2)}, u32[]{:S(2)}) %collective-permute-start.28) | collective-permute-done | bytes 262176 | tf_op jit(solution)/shard_map/ppermute | solution.py:368
  181.0 6.1 %collective-permute-done.31 = bf16[64,2048]{1,0:T(8,128)(2,1)S(1)} collective-permute-done((bf16[64,2048]{1,0:T(8,128)(2,1)S(1)}, bf16[64,2048]{1,0:T(8,128)(2,1)S(1)}, u32[]{:S(2)}, u32[]{:S(2)}) %collective-permute-start.31) | collective-permute-done | bytes 262176 | tf_op jit(solution)/shard_map/ppermute | solution.py:368
  201.7 5.4 %collective-permute-done.38 = bf16[64,2048]{1,0:T(8,128)(2,1)S(1)} collective-permute-done((bf16[64,2048]{1,0:T(8,128)(2,1)S(1)}, bf16[64,2048]{1,0:T(8,128)(2,1)S(1)}, u32[]{:S(2)}, u32[]{:S(2)}) %collective-permute-start.38) | collective-permute-done | bytes 262176 | tf_op jit(solution)/shard_map/ppermute | solution.py:368
  213.5 8.9 %collective-permute-done.37 = bf16[64,2048]{1,0:T(8,128)(2,1)S(1)} collective-permute-done((bf16[64,2048]{1,0:T(8,128)(2,1)S(1)}, bf16[64,2048]{1,0:T(8,128)(2,1)S(1)}, u32[]{:S(2)}, u32[]{:S(2)}) %collective-permute-start.37) | collective-permute-done | bytes 262176 | tf_op jit(solution)/shard_map/ppermute | solution.py:368
  231.9 8.2 %collective-permute-done.41 = bf16[128,2048]{1,0:T(8,128)(2,1)S(1)} collective-permute-done((bf16[128,2048]{1,0:T(8,128)(2,1)S(1)}, bf16[128,2048]{1,0:T(8,128)(2,1)S(1)}, u32[]{:S(2)}, u32[]{:S(2)}) %collective-permute-start.41) | collective-permute-done | bytes 524320 | tf_op jit(solution)/shard_map/ppermute | solution.py:405
  284.7 8.6 %collective-permute-done.67 = bf16[128,2048]{1,0:T(8,128)(2,1)S(1)} collective-permute-done((bf16[128,2048]{1,0:T(8,128)(2,1)S(1)}, bf16[128,2048]{1,0:T(8,128)(2,1)S(1)}, u32[]{:S(2)}, u32[]{:S(2)}) %collective-permute-start.67) | collective-permute-done | bytes 524320 | tf_op jit(solution)/shard_map/ppermute | solution.py:405
  296.2 10.8 %collective-permute-done.69 = bf16[64,2048]{1,0:T(8,128)(2,1)S(1)} collective-permute-done((bf16[64,2048]{1,0:T(8,128)(2,1)S(1)}, bf16[64,2048]{1,0:T(8,128)(2,1)S(1)}, u32[]{:S(2)}, u32[]{:S(2)}) %collective-permute-start.69) | collective-permute-done | bytes 262176 | tf_op jit(solution)/shard_map/ppermute | solution.py:368
  320.4 11.4 %collective-permute-done.74 = bf16[64,2048]{1,0:T(8,128)(2,1)S(1)} collective-permute-done((bf16[64,2048]{1,0:T(8,128)(2,1)S(1)}, bf16[64,2048]{1,0:T(8,128)(2,1)S(1)}, u32[]{:S(2)}, u32[]{:S(2)}) %collective-permute-start.74) | collective-permute-done | bytes 262176 | tf_op jit(solution)/shard_map/ppermute | solution.py:368
  335.5 7.0 %collective-permute-done.72 = bf16[64,2048]{1,0:T(8,128)(2,1)S(1)} collective-permute-done((bf16[64,2048]{1,0:T(8,128)(2,1)S(1)}, bf16[64,2048]{1,0:T(8,128)(2,1)S(1)}, u32[]{:S(2)}, u32[]{:S(2)}) %collective-permute-start.72) | collective-permute-done | bytes 262176 | tf_op jit(solution)/shard_map/ppermute | solution.py:405
  342.4 4.7 collective-permute-done.73
  352.4 10.5 %collective-permute-done.84 = bf16[128,2048]{1,0:T(8,128)(2,1)S(1)} collective-permute-done((bf16[128,2048]{1,0:T(8,128)(2,1)S(1)}, bf16[128,2048]{1,0:T(8,128)(2,1)S(1)}, u32[]{:S(2)}, u32[]{:S(2)}) %collective-permute-start.84) | collective-permute-done | bytes 524320 | tf_op jit(solution)/shard_map/ppermute | solution.py:405
  366.0 4.6 fusion
  375.8 5.2 all-to-all-start.2
  384.0 7.6 %shard_map.209 = (f32[1024,128]{1,0:T(8,128)S(1)}, f32[1024,256]{1,0:T(8,128)S(1)}, bf16[1024,256]{1,0:T(8,128)(2,1)S(1)}) custom-call(s32[3]{0:T(128)S(1)} %pad_add_fusion.1.at, bf16[1024,128]{1,0:T(8,128)(2,1)S(1)} %copy-done.21, s32[1024,1]{1,0:T(8,128)S(1)} %copy-done.17, s32[2,1024]{1,0:T(2,128)S(1)} %pad_add_fusion.key_doc_ref, ...), custom_call_target="tpu_custom_call" | custom-call | flops 1342177280 | bytes 3682304 | tf_op jit(solution)/shard_map/pallas_call | solution.py:95
  394.9 12.1 %collective-permute-done.96.refs_1_ = bf16[1024,256]{1,0:T(8,128)(2,1)S(1)} collective-permute-done((bf16[1024,256]{1,0:T(8,128)(2,1)S(1)}, bf16[1024,256]{1,0:T(8,128)(2,1)S(1)}, u32[]{:S(2)}, u32[]{:S(2)}) %collective-permute-start.96) | collective-permute-done | bytes 524320 | tf_op jit(solution)/shard_map/ppermute | solution.py:394
  433.8 7.9 %collective-permute-done.106 = bf16[128,2048]{1,0:T(8,128)(2,1)S(1)} collective-permute-done((bf16[128,2048]{1,0:T(8,128)(2,1)S(1)}, bf16[128,2048]{1,0:T(8,128)(2,1)S(1)}, u32[]{:S(2)}, u32[]{:S(2)}) %collective-permute-start.106) | collective-permute-done | bytes 524320 | tf_op jit(solution)/shard_map/ppermute | solution.py:405
  441.8 7.1 %collective-permute-done.107 = bf16[4,256,512]{2,1,0:T(8,128)(2,1)S(1)} collective-permute-done((bf16[4,256,512]{2,1,0:T(8,128)(2,1)S(1)}, bf16[4,256,512]{2,1,0:T(8,128)(2,1)S(1)}, u32[]{:S(2)}, u32[]{:S(2)}) %collective-permute-start.107) | collective-permute-done | bytes 1048608 | tf_op jit(solution)/shard_map/ppermute | solution.py:394
  450.2 13.7 %all-to-all-done.2.piece_ref = bf16[4,256,1536]{2,1,0:T(8,128)(2,1)} async-done(((bf16[4,256,1536]{2,1,0:T(8,128)(2,1)}), bf16[4,256,1536]{2,1,0:T(8,128)(2,1)}, u32[]{:S(2)}, u32[]{:S(2)}) %all-to-all-start.2) | async-done | bytes 3145760 | tf_op jit(solution)/shard_map/all_to_all | solution.py:384
  472.9 9.5 %collective-permute-done.109 = bf16[64,2048]{1,0:T(8,128)(2,1)} collective-permute-done((bf16[64,2048]{1,0:T(8,128)(2,1)}, bf16[64,2048]{1,0:T(8,128)(2,1)}, u32[]{:S(2)}, u32[]{:S(2)}) %collective-permute-start.109) | collective-permute-done | bytes 262176 | tf_op jit(solution)/shard_map/ppermute | solution.py:368
  482.3 9.3 %collective-permute-done.110 = bf16[64,2048]{1,0:T(8,128)(2,1)S(1)} collective-permute-done((bf16[64,2048]{1,0:T(8,128)(2,1)S(1)}, bf16[64,2048]{1,0:T(8,128)(2,1)S(1)}, u32[]{:S(2)}, u32[]{:S(2)}) %collective-permute-start.110) | collective-permute-done | bytes 262176 | tf_op jit(solution)/shard_map/ppermute | solution.py:368
  502.0 5.2 shard_map.214
  509.5 9.8 %collective-permute-done.115 = bf16[64,2048]{1,0:T(8,128)(2,1)} collective-permute-done((bf16[64,2048]{1,0:T(8,128)(2,1)}, bf16[64,2048]{1,0:T(8,128)(2,1)}, u32[]{:S(2)}, u32[]{:S(2)}) %collective-permute-start.115) | collective-permute-done | bytes 262176 | tf_op jit(solution)/shard_map/ppermute | solution.py:368
  (557 shorter events, 257.6 us)
Async XLA Ops:
  3.5 25.2 %collective-permute-start.4 = (bf16[64,2048]{1,0:T(8,128)(2,1)}, bf16[64,2048]{1,0:T(8,128)(2,1)}, u32[]{:S(2)}, u32[]{:S(2)}) collective-permute-start(bf16[64,2048]{1,0:T(8,128)(2,1)} %fusion.13), channel_id=1, source_target_pairs={{0,24},{4,28},{8,16},{12,20},{16,8},{20,12},{24,0},{28,4},{1,25},{... | collective-permute-start | bytes 786440 | tf_op jit(solution)/shard_map/ppermute | solution.py:368
  8.6 30.0 %collective-permute-start.3 = (bf16[64,2048]{1,0:T(8,128)(2,1)}, bf16[64,2048]{1,0:T(8,128)(2,1)}, u32[]{:S(2)}, u32[]{:S(2)}) collective-permute-start(bf16[64,2048]{1,0:T(8,128)(2,1)} %fusion.13), channel_id=1, source_target_pairs={{0,16},{4,20},{8,24},{12,28},{16,0},{20,4},{24,8},{28,12},{1,17},{... | collective-permute-start | bytes 786440 | tf_op jit(solution)/shard_map/ppermute | solution.py:368
  8.6 31.9 %collective-permute-start.1 = (bf16[64,2048]{1,0:T(8,128)(2,1)}, bf16[64,2048]{1,0:T(8,128)(2,1)}, u32[]{:S(2)}, u32[]{:S(2)}) collective-permute-start(bf16[64,2048]{1,0:T(8,128)(2,1)} %fusion.13), channel_id=1, source_target_pairs={{0,2},{1,3},{2,0},{3,1},{4,6},{5,7},{6,4},{7,5},{8,10},{9,11},{10,... | collective-permute-start | bytes 786440 | tf_op jit(solution)/shard_map/ppermute | solution.py:405
  10.1 18.1 %collective-permute-start = (bf16[64,2048]{1,0:T(8,128)(2,1)}, bf16[64,2048]{1,0:T(8,128)(2,1)}, u32[]{:S(2)}, u32[]{:S(2)}) collective-permute-start(bf16[64,2048]{1,0:T(8,128)(2,1)} %fusion.13), channel_id=1, source_target_pairs={{0,8},{4,12},{8,0},{12,4},{16,24},{20,28},{24,16},{28,20},{1,9},{5... | collective-permute-start | bytes 786440 | tf_op jit(solution)/shard_map/ppermute | solution.py:368
  15.2 38.5 %all-to-all-start = ((bf16[4,256,512]{2,1,0:T(8,128)(2,1)}), bf16[4,256,512]{2,1,0:T(8,128)(2,1)}, u32[]{:S(2)}, u32[]{:S(2)}) async-start(bf16[4,256,512]{2,1,0:T(8,128)(2,1)} %pad_maximum_fusion.6), calls=%async_computation | async-start | bytes 2097152 | tf_op jit(solution)/shard_map/all_to_all | solution.py:384
  53.7 24.5 %collective-permute-start.10 = (bf16[4,256,512]{2,1,0:T(8,128)(2,1)}, bf16[4,256,512]{2,1,0:T(8,128)(2,1)}, u32[]{:S(2)}, u32[]{:S(2)}) collective-permute-start(bf16[4,256,512]{2,1,0:T(8,128)(2,1)} %all-to-all-done), channel_id=1, source_target_pairs={{0,4},{4,0},{8,12},{12,8},{16,20},{20,16},{24,28},{28,24},{1,5},{5... | collective-permute-start | bytes 3145736 | tf_op jit(solution)/shard_map/ppermute | solution.py:394
  58.4 75.1 %all-to-all-start.1 = ((bf16[4,256,1536]{2,1,0:T(8,128)(2,1)}), bf16[4,256,1536]{2,1,0:T(8,128)(2,1)S(1)}, u32[]{:S(2)}, u32[]{:S(2)}) async-start(bf16[4,256,1536]{2,1,0:T(8,128)(2,1)} %pad_maximum_fusion), calls=%async_computation.1 | async-start | bytes 6291456 | tf_op jit(solution)/shard_map/all_to_all | solution.py:384
  139.6 38.0 %collective-permute-start.26 = (bf16[4,256,768]{2,1,0:T(8,128)(2,1)S(1)}, bf16[4,256,768]{2,1,0:T(8,128)(2,1)S(1)}, u32[]{:S(2)}, u32[]{:S(2)}) collective-permute-start(bf16[4,256,768]{2,1,0:T(8,128)(2,1)S(1)} %copy-done.50), channel_id=1, source_target_pairs={{0,4},{4,0},{8,12},{12,8},{16,20},{20,16},{24,28},{28,24},{1,5},{5... | collective-permute-start | bytes 4718600 | tf_op jit(solution)/shard_map/ppermute | solution.py:394
  141.8 20.4 %collective-permute-start.29 = (bf16[64,2048]{1,0:T(8,128)(2,1)S(1)}, bf16[64,2048]{1,0:T(8,128)(2,1)S(1)}, u32[]{:S(2)}, u32[]{:S(2)}) collective-permute-start(bf16[64,2048]{1,0:T(8,128)(2,1)S(1)} %constant_dynamic-slice_fusion), channel_id=1, source_target_pairs={{0,24},{4,28},{8,16},{12,20},{16,8},{20,12},{24,0},{28,4},{1,25},{... | collective-permute-start | bytes 786440 | tf_op jit(solution)/shard_map/ppermute | solution.py:368
  143.3 34.1 %collective-permute-start.28 = (bf16[64,2048]{1,0:T(8,128)(2,1)S(1)}, bf16[64,2048]{1,0:T(8,128)(2,1)S(1)}, u32[]{:S(2)}, u32[]{:S(2)}) collective-permute-start(bf16[64,2048]{1,0:T(8,128)(2,1)S(1)} %constant_dynamic-slice_fusion), channel_id=1, source_target_pairs={{0,16},{4,20},{8,24},{12,28},{16,0},{20,4},{24,8},{28,12},{1,17},{... | collective-permute-start | bytes 786440 | tf_op jit(solution)/shard_map/ppermute | solution.py:368
  152.6 24.8 %collective-permute-start.25 = (bf16[128,2048]{1,0:T(8,128)(2,1)S(1)}, bf16[128,2048]{1,0:T(8,128)(2,1)S(1)}, u32[]{:S(2)}, u32[]{:S(2)}) collective-permute-start(bf16[128,2048]{1,0:T(8,128)(2,1)S(1)} %slice.724), channel_id=1, source_target_pairs={{0,2},{1,3},{2,0},{3,1},{4,6},{5,7},{6,4},{7,5},{8,10},{9,11},{10,... | collective-permute-start | bytes 1572872 | tf_op jit(solution)/shard_map/ppermute | solution.py:405
  159.8 20.1 %collective-permute-start.30 = (bf16[64,2048]{1,0:T(8,128)(2,1)S(1)}, bf16[64,2048]{1,0:T(8,128)(2,1)S(1)}, u32[]{:S(2)}, u32[]{:S(2)}) collective-permute-start(bf16[64,2048]{1,0:T(8,128)(2,1)S(1)} %get-tuple-element.414), channel_id=1, source_target_pairs={{0,24},{4,28},{8,16},{12,20},{16,8},{20,12},{24,0},{28,4},{1,25},{... | collective-permute-start | bytes 786440 | tf_op jit(solution)/shard_map/ppermute | solution.py:368
  162.2 24.9 %collective-permute-start.31 = (bf16[64,2048]{1,0:T(8,128)(2,1)S(1)}, bf16[64,2048]{1,0:T(8,128)(2,1)S(1)}, u32[]{:S(2)}, u32[]{:S(2)}) collective-permute-start(bf16[64,2048]{1,0:T(8,128)(2,1)S(1)} %get-tuple-element.415), channel_id=1, source_target_pairs={{0,16},{4,20},{8,24},{12,28},{16,0},{20,4},{24,8},{28,12},{1,17},{... | collective-permute-start | bytes 786440 | tf_op jit(solution)/shard_map/ppermute | solution.py:368
  179.1 20.2 %collective-permute-start.54 = (bf16[64,2048]{1,0:T(8,128)(2,1)S(1)}, bf16[64,2048]{1,0:T(8,128)(2,1)S(1)}, u32[]{:S(2)}, u32[]{:S(2)}) collective-permute-start(bf16[64,2048]{1,0:T(8,128)(2,1)S(1)} %collective-permute-done.28), channel_id=1, source_target_pairs={{0,1},{1,0},{2,3},{3,2},{4,5},{5,4},{6,7},{7,6},{8,9},{9,8},{10,11... | collective-permute-start | bytes 786440 | tf_op jit(solution)/shard_map/ppermute | solution.py:405
  179.5 21.1 %collective-permute-start.55 = (bf16[64,2048]{1,0:T(8,128)(2,1)S(1)}, bf16[64,2048]{1,0:T(8,128)(2,1)S(1)}, u32[]{:S(2)}, u32[]{:S(2)}) collective-permute-start(bf16[64,2048]{1,0:T(8,128)(2,1)S(1)} %collective-permute-done.29), channel_id=1, source_target_pairs={{0,1},{1,0},{2,3},{3,2},{4,5},{5,4},{6,7},{7,6},{8,9},{9,8},{10,11... | collective-permute-start | bytes 786440 | tf_op jit(solution)/shard_map/ppermute | solution.py:405
  187.1 38.0 %collective-permute-start.39 = (bf16[4,256,768]{2,1,0:T(8,128)(2,1)S(1)}, bf16[4,256,768]{2,1,0:T(8,128)(2,1)S(1)}, u32[]{:S(2)}, u32[]{:S(2)}) collective-permute-start(bf16[4,256,768]{2,1,0:T(8,128)(2,1)S(1)} %slice.488), channel_id=1, source_target_pairs={{0,4},{4,0},{8,12},{12,8},{16,20},{20,16},{24,28},{28,24},{1,5},{5... | collective-permute-start | bytes 4718600 | tf_op jit(solution)/shard_map/ppermute | solution.py:394
  199.4 23.0 %collective-permute-start.37 = (bf16[64,2048]{1,0:T(8,128)(2,1)S(1)}, bf16[64,2048]{1,0:T(8,128)(2,1)S(1)}, u32[]{:S(2)}, u32[]{:S(2)}) collective-permute-start(bf16[64,2048]{1,0:T(8,128)(2,1)S(1)} %multiply_convert_fusion.14), channel_id=1, source_target_pairs={{0,16},{4,20},{8,24},{12,28},{16,0},{20,4},{24,8},{28,12},{1,17},{... | collective-permute-start | bytes 786440 | tf_op jit(solution)/shard_map/ppermute | solution.py:368
  200.6 24.5 %collective-permute-start.40 = (bf16[128,2048]{1,0:T(8,128)(2,1)S(1)}, bf16[128,2048]{1,0:T(8,128)(2,1)S(1)}, u32[]{:S(2)}, u32[]{:S(2)}) collective-permute-start(bf16[128,2048]{1,0:T(8,128)(2,1)S(1)} %pad_maximum_fusion.24), channel_id=1, source_target_pairs={{0,2},{1,3},{2,0},{3,1},{4,6},{5,7},{6,4},{7,5},{8,10},{9,11},{10,... | collective-permute-start | bytes 1572872 | tf_op jit(solution)/shard_map/ppermute | solution.py:405
  284.7 22.3 %collective-permute-start.69 = (bf16[64,2048]{1,0:T(8,128)(2,1)S(1)}, bf16[64,2048]{1,0:T(8,128)(2,1)S(1)}, u32[]{:S(2)}, u32[]{:S(2)}) collective-permute-start(bf16[64,2048]{1,0:T(8,128)(2,1)S(1)} %get-tuple-element.409), channel_id=1, source_target_pairs={{0,16},{4,20},{8,24},{12,28},{16,0},{20,4},{24,8},{28,12},{1,17},{... | collective-permute-start | bytes 786440 | tf_op jit(solution)/shard_map/ppermute | solution.py:368
  294.7 68.4 %collective-permute-start.89 = (bf16[4,256,1536]{2,1,0:T(8,128)(2,1)S(1)}, bf16[4,256,1536]{2,1,0:T(8,128)(2,1)S(1)}, u32[]{:S(2)}, u32[]{:S(2)}) collective-permute-start(bf16[4,256,1536]{2,1,0:T(8,128)(2,1)S(1)} %pad_maximum_fusion.1), channel_id=1, source_target_pairs={{0,4},{4,0},{8,12},{12,8},{16,20},{20,16},{24,28},{28,24},{1,5},{5... | collective-permute-start | bytes 9437192 | tf_op jit(solution)/shard_map/ppermute | solution.py:394
  311.7 20.2 %collective-permute-start.74 = (bf16[64,2048]{1,0:T(8,128)(2,1)S(1)}, bf16[64,2048]{1,0:T(8,128)(2,1)S(1)}, u32[]{:S(2)}, u32[]{:S(2)}) collective-permute-start(bf16[64,2048]{1,0:T(8,128)(2,1)S(1)} %get-tuple-element.241), channel_id=1, source_target_pairs={{0,16},{4,20},{8,24},{12,28},{16,0},{20,4},{24,8},{28,12},{1,17},{... | collective-permute-start | bytes 786440 | tf_op jit(solution)/shard_map/ppermute | solution.py:368
  315.3 16.6 %collective-permute-start.71 = (bf16[64,2048]{1,0:T(8,128)(2,1)S(1)}, bf16[64,2048]{1,0:T(8,128)(2,1)S(1)}, u32[]{:S(2)}, u32[]{:S(2)}) collective-permute-start(bf16[64,2048]{1,0:T(8,128)(2,1)S(1)} %get-tuple-element.241), channel_id=1, source_target_pairs={{0,8},{4,12},{8,0},{12,4},{16,24},{20,28},{24,16},{28,20},{1,9},{5... | collective-permute-start | bytes 786440 | tf_op jit(solution)/shard_map/ppermute | solution.py:368
  351.3 40.4 %collective-permute-start.94 = (bf16[128,2048]{1,0:T(8,128)(2,1)}, bf16[128,2048]{1,0:T(8,128)(2,1)S(1)}, u32[]{:S(2)}, u32[]{:S(2)}) collective-permute-start(bf16[128,2048]{1,0:T(8,128)(2,1)} %fusion.7), channel_id=1, source_target_pairs={{0,2},{1,3},{2,0},{3,1},{4,6},{5,7},{6,4},{7,5},{8,10},{9,11},{10,... | collective-permute-start | bytes 1572872 | tf_op jit(solution)/shard_map/ppermute | solution.py:405
  364.8 26.9 %collective-permute-start.95 = (bf16[128,2048]{1,0:T(8,128)(2,1)}, bf16[128,2048]{1,0:T(8,128)(2,1)}, u32[]{:S(2)}, u32[]{:S(2)}) collective-permute-start(bf16[128,2048]{1,0:T(8,128)(2,1)} %slice.721), channel_id=1, source_target_pairs={{0,2},{1,3},{2,0},{3,1},{4,6},{5,7},{6,4},{7,5},{8,10},{9,11},{10,... | collective-permute-start | bytes 1572872 | tf_op jit(solution)/shard_map/ppermute | solution.py:405
  375.8 88.1 %all-to-all-start.2 = ((bf16[4,256,1536]{2,1,0:T(8,128)(2,1)}), bf16[4,256,1536]{2,1,0:T(8,128)(2,1)}, u32[]{:S(2)}, u32[]{:S(2)}) async-start(bf16[4,256,1536]{2,1,0:T(8,128)(2,1)} %fusion), calls=%async_computation.2 | async-start | bytes 6291456 | tf_op jit(solution)/shard_map/all_to_all | solution.py:384
  423.7 25.3 %collective-permute-start.107 = (bf16[4,256,512]{2,1,0:T(8,128)(2,1)S(1)}, bf16[4,256,512]{2,1,0:T(8,128)(2,1)S(1)}, u32[]{:S(2)}, u32[]{:S(2)}) collective-permute-start(bf16[4,256,512]{2,1,0:T(8,128)(2,1)S(1)} %pad_maximum_fusion.18), channel_id=1, source_target_pairs={{0,4},{4,0},{8,12},{12,8},{16,20},{20,16},{24,28},{28,24},{1,5},{5... | collective-permute-start | bytes 3145736 | tf_op jit(solution)/shard_map/ppermute | solution.py:394
  430.3 42.5 %collective-permute-start.108 = (bf16[64,2048]{1,0:T(8,128)(2,1)}, bf16[64,2048]{1,0:T(8,128)(2,1)S(1)}, u32[]{:S(2)}, u32[]{:S(2)}) collective-permute-start(bf16[64,2048]{1,0:T(8,128)(2,1)} %get-tuple-element.402), channel_id=1, source_target_pairs={{0,24},{4,28},{8,16},{12,20},{16,8},{20,12},{24,0},{28,4},{1,25},{... | collective-permute-start | bytes 786440 | tf_op jit(solution)/shard_map/ppermute | solution.py:368
  433.8 48.5 %collective-permute-start.109 = (bf16[64,2048]{1,0:T(8,128)(2,1)}, bf16[64,2048]{1,0:T(8,128)(2,1)}, u32[]{:S(2)}, u32[]{:S(2)}) collective-permute-start(bf16[64,2048]{1,0:T(8,128)(2,1)} %get-tuple-element.403), channel_id=1, source_target_pairs={{0,16},{4,20},{8,24},{12,28},{16,0},{20,4},{24,8},{28,12},{1,17},{... | collective-permute-start | bytes 786440 | tf_op jit(solution)/shard_map/ppermute | solution.py:368
  463.9 57.5 %all-to-all-start.3 = ((bf16[4,256,512]{2,1,0:T(8,128)(2,1)}), bf16[4,256,512]{2,1,0:T(8,128)(2,1)S(1)}, u32[]{:S(2)}, u32[]{:S(2)}) async-start(bf16[4,256,512]{2,1,0:T(8,128)(2,1)} %fusion.2), calls=%async_computation.3 | async-start | bytes 2097152 | tf_op jit(solution)/shard_map/all_to_all | solution.py:384
  467.5 24.1 %collective-permute-start.110 = (bf16[64,2048]{1,0:T(8,128)(2,1)S(1)}, bf16[64,2048]{1,0:T(8,128)(2,1)S(1)}, u32[]{:S(2)}, u32[]{:S(2)}) collective-permute-start(bf16[64,2048]{1,0:T(8,128)(2,1)S(1)} %slice.726), channel_id=1, source_target_pairs={{0,8},{4,12},{8,0},{12,4},{16,24},{20,28},{24,16},{28,20},{1,9},{5... | collective-permute-start | bytes 786440 | tf_op jit(solution)/shard_map/ppermute | solution.py:368
  470.4 39.1 %collective-permute-start.114 = (bf16[64,2048]{1,0:T(8,128)(2,1)}, bf16[64,2048]{1,0:T(8,128)(2,1)}, u32[]{:S(2)}, u32[]{:S(2)}) collective-permute-start(bf16[64,2048]{1,0:T(8,128)(2,1)} %get-tuple-element.343), channel_id=1, source_target_pairs={{0,24},{4,28},{8,16},{12,20},{16,8},{20,12},{24,0},{28,4},{1,25},{... | collective-permute-start | bytes 786440 | tf_op jit(solution)/shard_map/ppermute | solution.py:368
  497.6 21.6 %collective-permute-start.115 = (bf16[64,2048]{1,0:T(8,128)(2,1)}, bf16[64,2048]{1,0:T(8,128)(2,1)}, u32[]{:S(2)}, u32[]{:S(2)}) collective-permute-start(bf16[64,2048]{1,0:T(8,128)(2,1)} %get-tuple-element.345), channel_id=1, source_target_pairs={{0,16},{4,20},{8,24},{12,28},{16,0},{20,4},{24,8},{28,12},{1,17},{... | collective-permute-start | bytes 786440 | tf_op jit(solution)/shard_map/ppermute | solution.py:368
  (161 other events, 1489.5 us)

commit v6 on v5

--- a/solution.py
+++ b/solution.py
@@ -417,9 +417,16 @@
         parts = [value[i : i + own] for i in range(0, value.shape[0], own)]
         return jnp.concatenate([head_swap(part, 1) for part in parts])
 
-    def gather_rows(labels, piece):
+    def gather_rows(labels, piece, split=True):
         (piece,) = gate(labels[0], [piece])
         parts = gather_far(piece)
+        if not split:
+            (mine,) = gate(labels[1], [jnp.concatenate(parts)])
+            other = head_swap(mine, 2)
+            near, rest = slice(0, many_rows), slice(many_rows, None)
+            mine, other = gate(labels[2], [mine, other])
+            half = [jnp.concatenate([mine[rows], other[rows]]) for rows in (near, rest)]
+            return [jnp.concatenate(half), jnp.concatenate([core_swap(part) for part in half])]
         near = jnp.concatenate(
             parts[:half_far] + [head_swap(part, 2) for part in parts[:half_far]]
         )
@@ -691,7 +698,7 @@
         ],
     )
     grad_middle = own_grad.astype(F32) + norm_back(grad_normed_b, normed_b, inv_b)
-    grad_mix = gather_rows(("m0", "m1", "m2"), grad_middle.astype(LOW))
+    grad_mix = gather_rows(("m0", "m1", "m2"), grad_middle.astype(LOW), False)
 
     grad_mix = gate("back", grad_mix)
     grad_attn = [dot(g, proj_turned).astype(LOW) for g in grad_mix]

time: 540 us -> 539 us (level)
    ppermute x91 -> x89, starting transfers between devices: 41.5 us -> 38.2 us  [head_swap(): lax.ppermute(value, 'head', [(i, i ^ step) for i in range(head_size)])]
    ppermute x91 -> x89, waiting for transfers between devices: 83.4 us -> 83.7 us  [head_swap(): lax.ppermute(value, 'head', [(i, i ^ step) for i in range(head_size)])]
  transfers between devices with their start and end apart: 126 -> 124, of which waited for: 55 -> 54; matrix products, arithmetic and copies ran while one was open for 16% -> 17% of each run, Pallas kernels for 5% -> 5%
where the time goes in v6:
time: 539 us; the launch traced here: 534 us
  waiting for transfers between devices  278 us (52%)
  starting transfers between devices  105 us (19%)
  other arithmetic  42.4 us (8%)
  matrix products  39.2 us (7%)
  local copies, waits for them, and re-layouts  35.3 us (7%)
  Pallas kernels  30.7 us (6%)
    ppermute x24, waiting for transfers between devices, far_swap(): lax.ppermute(value, 'seq', [(i * groups + g, (i ^ step) * groups + g) for...  115 us
    ppermute x89, waiting for transfers between devices, head_swap(): lax.ppermute(value, 'head', [(i, i ^ step) for i in range(head_size)])  83.7 us
    all_to_all x4, waiting for transfers between devices, far_exchange(): lax.all_to_all(blocks, 'seq', 0, 0, axis_index_groups=[[i * groups + g fo...  44.9 us
    ppermute x24, starting transfers between devices, far_swap(): lax.ppermute(value, 'seq', [(i * groups + g, (i ^ step) * groups + g) for...  39.5 us
    ppermute x89, starting transfers between devices, head_swap(): lax.ppermute(value, 'head', [(i, i ^ step) for i in range(head_size)])  38.2 us
    ppermute x7, waiting for transfers between devices, group_shift(): lax.ppermute(value, 'seq', [(i * groups + g, i * groups + (g + step) % gr...  34.4 us
    pallas_call x12, Pallas kernels, call(): pl.pallas_call(body, out_shape=outs, in_specs=[SMEM_SPEC] + [space] * len...  30.7 us
    all_to_all x4, starting transfers between devices, far_exchange(): lax.all_to_all(blocks, 'seq', 0, 0, axis_index_groups=[[i * groups + g fo...  17.6 us
  transfers between devices with their start and end apart: 124, of which 54 were waited for; matrix products, arithmetic and copies ran while one was open for 17% of the time, Pallas kernels for 5%

profile of v6, /device:TPU:0, one launch (start us, length us, event | category | flops | bytes accessed | tf_op | source)
XLA Modules:
  0.0 533.8 jit_solution(12297605063592157703)
XLA Ops:
  2.9 5.1 collective-permute-start.4
  14.6 5.0 all-to-all-start
  28.1 9.7 %collective-permute-done.3 = bf16[64,2048]{1,0:T(8,128)(2,1)} collective-permute-done((bf16[64,2048]{1,0:T(8,128)(2,1)S(1)}, bf16[64,2048]{1,0:T(8,128)(2,1)}, u32[]{:S(2)}, u32[]{:S(2)}) %collective-permute-start.3) | collective-permute-done | bytes 262176 | tf_op jit(solution)/shard_map/ppermute | solution.py:368
  40.8 12.0 %all-to-all-done = bf16[4,256,512]{2,1,0:T(8,128)(2,1)} async-done(((bf16[4,256,512]{2,1,0:T(8,128)(2,1)}), bf16[4,256,512]{2,1,0:T(8,128)(2,1)}, u32[]{:S(2)}, u32[]{:S(2)}) %all-to-all-start) | async-done | bytes 1048608 | tf_op jit(solution)/shard_map/all_to_all | solution.py:384
  57.6 3.9 all-to-all-start.1
  62.9 7.0 %collective-permute-done.5 = bf16[128,2048]{1,0:T(8,128)(2,1)} collective-permute-done((bf16[128,2048]{1,0:T(8,128)(2,1)}, bf16[128,2048]{1,0:T(8,128)(2,1)}, u32[]{:S(2)}, u32[]{:S(2)}) %collective-permute-start.5) | collective-permute-done | bytes 524320 | tf_op jit(solution)/shard_map/ppermute | solution.py:405
  71.2 6.2 %collective-permute-done.10 = bf16[4,256,512]{2,1,0:T(8,128)(2,1)} collective-permute-done((bf16[4,256,512]{2,1,0:T(8,128)(2,1)}, bf16[4,256,512]{2,1,0:T(8,128)(2,1)}, u32[]{:S(2)}, u32[]{:S(2)}) %collective-permute-start.10) | collective-permute-done | bytes 1048608 | tf_op jit(solution)/shard_map/ppermute | solution.py:394
  90.8 10.0 %collective-permute-done.15.refs_1_ = bf16[1024,256]{1,0:T(8,128)(2,1)} collective-permute-done((bf16[1024,256]{1,0:T(8,128)(2,1)}, bf16[1024,256]{1,0:T(8,128)(2,1)}, u32[]{:S(2)}, u32[]{:S(2)}) %collective-permute-start.15) | collective-permute-done | bytes 524320 | tf_op jit(solution)/shard_map/ppermute | solution.py:394
  113.3 19.3 %all-to-all-done.1 = bf16[4,256,1536]{2,1,0:T(8,128)(2,1)S(1)} async-done(((bf16[4,256,1536]{2,1,0:T(8,128)(2,1)}), bf16[4,256,1536]{2,1,0:T(8,128)(2,1)S(1)}, u32[]{:S(2)}, u32[]{:S(2)}) %all-to-all-start.1) | async-done | bytes 3145760 | tf_op jit(solution)/shard_map/all_to_all | solution.py:384
  145.6 6.0 %collective-permute-done.24 = bf16[128,2048]{1,0:T(8,128)(2,1)S(1)} collective-permute-done((bf16[128,2048]{1,0:T(8,128)(2,1)}, bf16[128,2048]{1,0:T(8,128)(2,1)S(1)}, u32[]{:S(2)}, u32[]{:S(2)}) %collective-permute-start.24) | collective-permute-done | bytes 524320 | tf_op jit(solution)/shard_map/ppermute | solution.py:405
  153.0 6.1 %collective-permute-done.27 = bf16[64,2048]{1,0:T(8,128)(2,1)S(1)} collective-permute-done((bf16[64,2048]{1,0:T(8,128)(2,1)S(1)}, bf16[64,2048]{1,0:T(8,128)(2,1)S(1)}, u32[]{:S(2)}, u32[]{:S(2)}) %collective-permute-start.27) | collective-permute-done | bytes 262176 | tf_op jit(solution)/shard_map/ppermute | solution.py:368
  163.1 13.5 %collective-permute-done.28 = bf16[64,2048]{1,0:T(8,128)(2,1)S(1)} collective-permute-done((bf16[64,2048]{1,0:T(8,128)(2,1)S(1)}, bf16[64,2048]{1,0:T(8,128)(2,1)S(1)}, u32[]{:S(2)}, u32[]{:S(2)}) %collective-permute-start.28) | collective-permute-done | bytes 262176 | tf_op jit(solution)/shard_map/ppermute | solution.py:368
  180.1 6.3 %collective-permute-done.31 = bf16[64,2048]{1,0:T(8,128)(2,1)S(1)} collective-permute-done((bf16[64,2048]{1,0:T(8,128)(2,1)S(1)}, bf16[64,2048]{1,0:T(8,128)(2,1)S(1)}, u32[]{:S(2)}, u32[]{:S(2)}) %collective-permute-start.31) | collective-permute-done | bytes 262176 | tf_op jit(solution)/shard_map/ppermute | solution.py:368
  200.8 5.5 %collective-permute-done.38 = bf16[64,2048]{1,0:T(8,128)(2,1)S(1)} collective-permute-done((bf16[64,2048]{1,0:T(8,128)(2,1)S(1)}, bf16[64,2048]{1,0:T(8,128)(2,1)S(1)}, u32[]{:S(2)}, u32[]{:S(2)}) %collective-permute-start.38) | collective-permute-done | bytes 262176 | tf_op jit(solution)/shard_map/ppermute | solution.py:368
  207.2 4.5 collective-permute-done.34
  212.6 9.1 %collective-permute-done.37 = bf16[64,2048]{1,0:T(8,128)(2,1)S(1)} collective-permute-done((bf16[64,2048]{1,0:T(8,128)(2,1)S(1)}, bf16[64,2048]{1,0:T(8,128)(2,1)S(1)}, u32[]{:S(2)}, u32[]{:S(2)}) %collective-permute-start.37) | collective-permute-done | bytes 262176 | tf_op jit(solution)/shard_map/ppermute | solution.py:368
  231.0 8.3 %collective-permute-done.41 = bf16[128,2048]{1,0:T(8,128)(2,1)S(1)} collective-permute-done((bf16[128,2048]{1,0:T(8,128)(2,1)S(1)}, bf16[128,2048]{1,0:T(8,128)(2,1)S(1)}, u32[]{:S(2)}, u32[]{:S(2)}) %collective-permute-start.41) | collective-permute-done | bytes 524320 | tf_op jit(solution)/shard_map/ppermute | solution.py:405
  283.9 8.7 %collective-permute-done.67 = bf16[128,2048]{1,0:T(8,128)(2,1)S(1)} collective-permute-done((bf16[128,2048]{1,0:T(8,128)(2,1)S(1)}, bf16[128,2048]{1,0:T(8,128)(2,1)S(1)}, u32[]{:S(2)}, u32[]{:S(2)}) %collective-permute-start.67) | collective-permute-done | bytes 524320 | tf_op jit(solution)/shard_map/ppermute | solution.py:405
  295.5 10.7 %collective-permute-done.69 = bf16[64,2048]{1,0:T(8,128)(2,1)S(1)} collective-permute-done((bf16[64,2048]{1,0:T(8,128)(2,1)S(1)}, bf16[64,2048]{1,0:T(8,128)(2,1)S(1)}, u32[]{:S(2)}, u32[]{:S(2)}) %collective-permute-start.69) | collective-permute-done | bytes 262176 | tf_op jit(solution)/shard_map/ppermute | solution.py:368
  315.7 4.6 collective-permute-done.73
  320.4 13.4 %collective-permute-done.72 = bf16[64,2048]{1,0:T(8,128)(2,1)S(1)} collective-permute-done((bf16[64,2048]{1,0:T(8,128)(2,1)S(1)}, bf16[64,2048]{1,0:T(8,128)(2,1)S(1)}, u32[]{:S(2)}, u32[]{:S(2)}) %collective-permute-start.72) | collective-permute-done | bytes 262176 | tf_op jit(solution)/shard_map/ppermute | solution.py:368
  340.8 21.9 %collective-permute-done.82 = bf16[256,2048]{1,0:T(8,128)(2,1)S(1)} collective-permute-done((bf16[256,2048]{1,0:T(8,128)(2,1)S(1)}, bf16[256,2048]{1,0:T(8,128)(2,1)S(1)}, u32[]{:S(2)}, u32[]{:S(2)}) %collective-permute-start.82) | collective-permute-done | bytes 1048608 | tf_op jit(solution)/shard_map/ppermute | solution.py:405
  375.4 5.2 all-to-all-start.2
  383.7 7.7 %shard_map.209 = (f32[1024,128]{1,0:T(8,128)S(1)}, f32[1024,256]{1,0:T(8,128)S(1)}, bf16[1024,256]{1,0:T(8,128)(2,1)S(1)}) custom-call(s32[3]{0:T(128)S(1)} %pad_add_fusion.1.at, bf16[1024,128]{1,0:T(8,128)(2,1)S(1)} %copy-done.21, s32[1024,1]{1,0:T(8,128)S(1)} %copy-done.17, s32[2,1024]{1,0:T(2,128)S(1)} %pad_add_fusion.key_doc_ref, ...), custom_call_target="tpu_custom_call" | custom-call | flops 1342177280 | bytes 3682304 | tf_op jit(solution)/shard_map/pallas_call | solution.py:95
  395.6 11.1 %collective-permute-done.94.refs_1_ = bf16[1024,256]{1,0:T(8,128)(2,1)S(1)} collective-permute-done((bf16[1024,256]{1,0:T(8,128)(2,1)S(1)}, bf16[1024,256]{1,0:T(8,128)(2,1)S(1)}, u32[]{:S(2)}, u32[]{:S(2)}) %collective-permute-start.94) | collective-permute-done | bytes 524320 | tf_op jit(solution)/shard_map/ppermute | solution.py:394
  433.4 8.0 %collective-permute-done.104 = bf16[128,2048]{1,0:T(8,128)(2,1)S(1)} collective-permute-done((bf16[128,2048]{1,0:T(8,128)(2,1)S(1)}, bf16[128,2048]{1,0:T(8,128)(2,1)S(1)}, u32[]{:S(2)}, u32[]{:S(2)}) %collective-permute-start.104) | collective-permute-done | bytes 524320 | tf_op jit(solution)/shard_map/ppermute | solution.py:405
  441.6 7.1 %collective-permute-done.105 = bf16[4,256,512]{2,1,0:T(8,128)(2,1)S(1)} collective-permute-done((bf16[4,256,512]{2,1,0:T(8,128)(2,1)S(1)}, bf16[4,256,512]{2,1,0:T(8,128)(2,1)S(1)}, u32[]{:S(2)}, u32[]{:S(2)}) %collective-permute-start.105) | collective-permute-done | bytes 1048608 | tf_op jit(solution)/shard_map/ppermute | solution.py:394
  449.9 13.6 %all-to-all-done.2.piece_ref = bf16[4,256,1536]{2,1,0:T(8,128)(2,1)} async-done(((bf16[4,256,1536]{2,1,0:T(8,128)(2,1)}), bf16[4,256,1536]{2,1,0:T(8,128)(2,1)}, u32[]{:S(2)}, u32[]{:S(2)}) %all-to-all-start.2) | async-done | bytes 3145760 | tf_op jit(solution)/shard_map/all_to_all | solution.py:384
  472.5 9.5 %collective-permute-done.107 = bf16[64,2048]{1,0:T(8,128)(2,1)} collective-permute-done((bf16[64,2048]{1,0:T(8,128)(2,1)}, bf16[64,2048]{1,0:T(8,128)(2,1)}, u32[]{:S(2)}, u32[]{:S(2)}) %collective-permute-start.107) | collective-permute-done | bytes 262176 | tf_op jit(solution)/shard_map/ppermute | solution.py:368
  482.0 9.3 %collective-permute-done.108 = bf16[64,2048]{1,0:T(8,128)(2,1)S(1)} collective-permute-done((bf16[64,2048]{1,0:T(8,128)(2,1)S(1)}, bf16[64,2048]{1,0:T(8,128)(2,1)S(1)}, u32[]{:S(2)}, u32[]{:S(2)}) %collective-permute-start.108) | collective-permute-done | bytes 262176 | tf_op jit(solution)/shard_map/ppermute | solution.py:368
  501.6 5.2 shard_map.214
  509.1 9.9 %collective-permute-done.113 = bf16[64,2048]{1,0:T(8,128)(2,1)} collective-permute-done((bf16[64,2048]{1,0:T(8,128)(2,1)}, bf16[64,2048]{1,0:T(8,128)(2,1)}, u32[]{:S(2)}, u32[]{:S(2)}) %collective-permute-start.113) | collective-permute-done | bytes 262176 | tf_op jit(solution)/shard_map/ppermute | solution.py:368
  (557 shorter events, 247.2 us)
Async XLA Ops:
  2.9 25.2 %collective-permute-start.4 = (bf16[64,2048]{1,0:T(8,128)(2,1)S(1)}, bf16[64,2048]{1,0:T(8,128)(2,1)}, u32[]{:S(2)}, u32[]{:S(2)}) collective-permute-start(bf16[64,2048]{1,0:T(8,128)(2,1)S(1)} %fusion.13), channel_id=1, source_target_pairs={{0,24},{4,28},{8,16},{12,20},{16,8},{20,12},{24,0},{28,4},{1,25},{... | collective-permute-start | bytes 786440 | tf_op jit(solution)/shard_map/ppermute | solution.py:368
  8.0 29.8 %collective-permute-start.3 = (bf16[64,2048]{1,0:T(8,128)(2,1)S(1)}, bf16[64,2048]{1,0:T(8,128)(2,1)}, u32[]{:S(2)}, u32[]{:S(2)}) collective-permute-start(bf16[64,2048]{1,0:T(8,128)(2,1)S(1)} %fusion.13), channel_id=1, source_target_pairs={{0,16},{4,20},{8,24},{12,28},{16,0},{20,4},{24,8},{28,12},{1,17},{... | collective-permute-start | bytes 786440 | tf_op jit(solution)/shard_map/ppermute | solution.py:368
  8.0 31.7 %collective-permute-start.1 = (bf16[64,2048]{1,0:T(8,128)(2,1)S(1)}, bf16[64,2048]{1,0:T(8,128)(2,1)}, u32[]{:S(2)}, u32[]{:S(2)}) collective-permute-start(bf16[64,2048]{1,0:T(8,128)(2,1)S(1)} %fusion.13), channel_id=1, source_target_pairs={{0,2},{1,3},{2,0},{3,1},{4,6},{5,7},{6,4},{7,5},{8,10},{9,11},{10,... | collective-permute-start | bytes 786440 | tf_op jit(solution)/shard_map/ppermute | solution.py:405
  14.6 38.3 %all-to-all-start = ((bf16[4,256,512]{2,1,0:T(8,128)(2,1)}), bf16[4,256,512]{2,1,0:T(8,128)(2,1)}, u32[]{:S(2)}, u32[]{:S(2)}) async-start(bf16[4,256,512]{2,1,0:T(8,128)(2,1)} %pad_maximum_fusion.6), calls=%async_computation | async-start | bytes 2097152 | tf_op jit(solution)/shard_map/all_to_all | solution.py:384
  52.9 24.5 %collective-permute-start.10 = (bf16[4,256,512]{2,1,0:T(8,128)(2,1)}, bf16[4,256,512]{2,1,0:T(8,128)(2,1)}, u32[]{:S(2)}, u32[]{:S(2)}) collective-permute-start(bf16[4,256,512]{2,1,0:T(8,128)(2,1)} %all-to-all-done), channel_id=1, source_target_pairs={{0,4},{4,0},{8,12},{12,8},{16,20},{20,16},{24,28},{28,24},{1,5},{5... | collective-permute-start | bytes 3145736 | tf_op jit(solution)/shard_map/ppermute | solution.py:394
  57.6 75.1 %all-to-all-start.1 = ((bf16[4,256,1536]{2,1,0:T(8,128)(2,1)}), bf16[4,256,1536]{2,1,0:T(8,128)(2,1)S(1)}, u32[]{:S(2)}, u32[]{:S(2)}) async-start(bf16[4,256,1536]{2,1,0:T(8,128)(2,1)} %pad_maximum_fusion), calls=%async_computation.1 | async-start | bytes 6291456 | tf_op jit(solution)/shard_map/all_to_all | solution.py:384
  138.8 38.0 %collective-permute-start.26 = (bf16[4,256,768]{2,1,0:T(8,128)(2,1)S(1)}, bf16[4,256,768]{2,1,0:T(8,128)(2,1)S(1)}, u32[]{:S(2)}, u32[]{:S(2)}) collective-permute-start(bf16[4,256,768]{2,1,0:T(8,128)(2,1)S(1)} %copy-done.52), channel_id=1, source_target_pairs={{0,4},{4,0},{8,12},{12,8},{16,20},{20,16},{24,28},{28,24},{1,5},{5... | collective-permute-start | bytes 4718600 | tf_op jit(solution)/shard_map/ppermute | solution.py:394
  141.1 20.4 %collective-permute-start.29 = (bf16[64,2048]{1,0:T(8,128)(2,1)S(1)}, bf16[64,2048]{1,0:T(8,128)(2,1)S(1)}, u32[]{:S(2)}, u32[]{:S(2)}) collective-permute-start(bf16[64,2048]{1,0:T(8,128)(2,1)S(1)} %constant_dynamic-slice_fusion), channel_id=1, source_target_pairs={{0,24},{4,28},{8,16},{12,20},{16,8},{20,12},{24,0},{28,4},{1,25},{... | collective-permute-start | bytes 786440 | tf_op jit(solution)/shard_map/ppermute | solution.py:368
  142.6 34.1 %collective-permute-start.28 = (bf16[64,2048]{1,0:T(8,128)(2,1)S(1)}, bf16[64,2048]{1,0:T(8,128)(2,1)S(1)}, u32[]{:S(2)}, u32[]{:S(2)}) collective-permute-start(bf16[64,2048]{1,0:T(8,128)(2,1)S(1)} %constant_dynamic-slice_fusion), channel_id=1, source_target_pairs={{0,16},{4,20},{8,24},{12,28},{16,0},{20,4},{24,8},{28,12},{1,17},{... | collective-permute-start | bytes 786440 | tf_op jit(solution)/shard_map/ppermute | solution.py:368
  151.7 25.0 %collective-permute-start.25 = (bf16[128,2048]{1,0:T(8,128)(2,1)S(1)}, bf16[128,2048]{1,0:T(8,128)(2,1)S(1)}, u32[]{:S(2)}, u32[]{:S(2)}) collective-permute-start(bf16[128,2048]{1,0:T(8,128)(2,1)S(1)} %slice.748), channel_id=1, source_target_pairs={{0,2},{1,3},{2,0},{3,1},{4,6},{5,7},{6,4},{7,5},{8,10},{9,11},{10,... | collective-permute-start | bytes 1572872 | tf_op jit(solution)/shard_map/ppermute | solution.py:405
  159.1 20.1 %collective-permute-start.30 = (bf16[64,2048]{1,0:T(8,128)(2,1)S(1)}, bf16[64,2048]{1,0:T(8,128)(2,1)S(1)}, u32[]{:S(2)}, u32[]{:S(2)}) collective-permute-start(bf16[64,2048]{1,0:T(8,128)(2,1)S(1)} %get-tuple-element.414), channel_id=1, source_target_pairs={{0,24},{4,28},{8,16},{12,20},{16,8},{20,12},{24,0},{28,4},{1,25},{... | collective-permute-start | bytes 786440 | tf_op jit(solution)/shard_map/ppermute | solution.py:368
  161.5 24.9 %collective-permute-start.31 = (bf16[64,2048]{1,0:T(8,128)(2,1)S(1)}, bf16[64,2048]{1,0:T(8,128)(2,1)S(1)}, u32[]{:S(2)}, u32[]{:S(2)}) collective-permute-start(bf16[64,2048]{1,0:T(8,128)(2,1)S(1)} %get-tuple-element.415), channel_id=1, source_target_pairs={{0,16},{4,20},{8,24},{12,28},{16,0},{20,4},{24,8},{28,12},{1,17},{... | collective-permute-start | bytes 786440 | tf_op jit(solution)/shard_map/ppermute | solution.py:368
  178.4 20.2 %collective-permute-start.54 = (bf16[64,2048]{1,0:T(8,128)(2,1)S(1)}, bf16[64,2048]{1,0:T(8,128)(2,1)S(1)}, u32[]{:S(2)}, u32[]{:S(2)}) collective-permute-start(bf16[64,2048]{1,0:T(8,128)(2,1)S(1)} %collective-permute-done.28), channel_id=1, source_target_pairs={{0,1},{1,0},{2,3},{3,2},{4,5},{5,4},{6,7},{7,6},{8,9},{9,8},{10,11... | collective-permute-start | bytes 786440 | tf_op jit(solution)/shard_map/ppermute | solution.py:405
  178.8 21.1 %collective-permute-start.55 = (bf16[64,2048]{1,0:T(8,128)(2,1)S(1)}, bf16[64,2048]{1,0:T(8,128)(2,1)S(1)}, u32[]{:S(2)}, u32[]{:S(2)}) collective-permute-start(bf16[64,2048]{1,0:T(8,128)(2,1)S(1)} %collective-permute-done.29), channel_id=1, source_target_pairs={{0,1},{1,0},{2,3},{3,2},{4,5},{5,4},{6,7},{7,6},{8,9},{9,8},{10,11... | collective-permute-start | bytes 786440 | tf_op jit(solution)/shard_map/ppermute | solution.py:405
  186.4 38.0 %collective-permute-start.39 = (bf16[4,256,768]{2,1,0:T(8,128)(2,1)S(1)}, bf16[4,256,768]{2,1,0:T(8,128)(2,1)S(1)}, u32[]{:S(2)}, u32[]{:S(2)}) collective-permute-start(bf16[4,256,768]{2,1,0:T(8,128)(2,1)S(1)} %slice.508), channel_id=1, source_target_pairs={{0,4},{4,0},{8,12},{12,8},{16,20},{20,16},{24,28},{28,24},{1,5},{5... | collective-permute-start | bytes 4718600 | tf_op jit(solution)/shard_map/ppermute | solution.py:394
  198.7 23.0 %collective-permute-start.37 = (bf16[64,2048]{1,0:T(8,128)(2,1)S(1)}, bf16[64,2048]{1,0:T(8,128)(2,1)S(1)}, u32[]{:S(2)}, u32[]{:S(2)}) collective-permute-start(bf16[64,2048]{1,0:T(8,128)(2,1)S(1)} %multiply_convert_fusion.14), channel_id=1, source_target_pairs={{0,16},{4,20},{8,24},{12,28},{16,0},{20,4},{24,8},{28,12},{1,17},{... | collective-permute-start | bytes 786440 | tf_op jit(solution)/shard_map/ppermute | solution.py:368
  199.9 24.5 %collective-permute-start.40 = (bf16[128,2048]{1,0:T(8,128)(2,1)S(1)}, bf16[128,2048]{1,0:T(8,128)(2,1)S(1)}, u32[]{:S(2)}, u32[]{:S(2)}) collective-permute-start(bf16[128,2048]{1,0:T(8,128)(2,1)S(1)} %pad_maximum_fusion.22), channel_id=1, source_target_pairs={{0,2},{1,3},{2,0},{3,1},{4,6},{5,7},{6,4},{7,5},{8,10},{9,11},{10,... | collective-permute-start | bytes 1572872 | tf_op jit(solution)/shard_map/ppermute | solution.py:405
  283.9 22.3 %collective-permute-start.69 = (bf16[64,2048]{1,0:T(8,128)(2,1)S(1)}, bf16[64,2048]{1,0:T(8,128)(2,1)S(1)}, u32[]{:S(2)}, u32[]{:S(2)}) collective-permute-start(bf16[64,2048]{1,0:T(8,128)(2,1)S(1)} %get-tuple-element.409), channel_id=1, source_target_pairs={{0,16},{4,20},{8,24},{12,28},{16,0},{20,4},{24,8},{28,12},{1,17},{... | collective-permute-start | bytes 786440 | tf_op jit(solution)/shard_map/ppermute | solution.py:368
  293.9 68.8 %collective-permute-start.83 = (bf16[4,256,1536]{2,1,0:T(8,128)(2,1)S(1)}, bf16[4,256,1536]{2,1,0:T(8,128)(2,1)S(1)}, u32[]{:S(2)}, u32[]{:S(2)}) collective-permute-start(bf16[4,256,1536]{2,1,0:T(8,128)(2,1)S(1)} %pad_maximum_fusion.1), channel_id=1, source_target_pairs={{0,4},{4,0},{8,12},{12,8},{16,20},{20,16},{24,28},{28,24},{1,5},{5... | collective-permute-start | bytes 9437192 | tf_op jit(solution)/shard_map/ppermute | solution.py:394
  311.8 22.0 %collective-permute-start.72 = (bf16[64,2048]{1,0:T(8,128)(2,1)S(1)}, bf16[64,2048]{1,0:T(8,128)(2,1)S(1)}, u32[]{:S(2)}, u32[]{:S(2)}) collective-permute-start(bf16[64,2048]{1,0:T(8,128)(2,1)S(1)} %get-tuple-element.239), channel_id=1, source_target_pairs={{0,16},{4,20},{8,24},{12,28},{16,0},{20,4},{24,8},{28,12},{1,17},{... | collective-permute-start | bytes 786440 | tf_op jit(solution)/shard_map/ppermute | solution.py:368
  311.9 21.9 %collective-permute-start.71 = (bf16[64,2048]{1,0:T(8,128)(2,1)S(1)}, bf16[64,2048]{1,0:T(8,128)(2,1)S(1)}, u32[]{:S(2)}, u32[]{:S(2)}) collective-permute-start(bf16[64,2048]{1,0:T(8,128)(2,1)S(1)} %get-tuple-element.239), channel_id=1, source_target_pairs={{0,8},{4,12},{8,0},{12,4},{16,24},{20,28},{24,16},{28,20},{1,9},{5... | collective-permute-start | bytes 786440 | tf_op jit(solution)/shard_map/ppermute | solution.py:368
  336.8 26.0 %collective-permute-start.82 = (bf16[256,2048]{1,0:T(8,128)(2,1)S(1)}, bf16[256,2048]{1,0:T(8,128)(2,1)S(1)}, u32[]{:S(2)}, u32[]{:S(2)}) collective-permute-start(bf16[256,2048]{1,0:T(8,128)(2,1)S(1)} %pad_maximum_fusion.14), channel_id=1, source_target_pairs={{0,2},{1,3},{2,0},{3,1},{4,6},{5,7},{6,4},{7,5},{8,10},{9,11},{10,... | collective-permute-start | bytes 3145736 | tf_op jit(solution)/shard_map/ppermute | solution.py:405
  340.0 51.4 %collective-permute-start.92 = (bf16[128,2048]{1,0:T(8,128)(2,1)}, bf16[128,2048]{1,0:T(8,128)(2,1)}, u32[]{:S(2)}, u32[]{:S(2)}) collective-permute-start(bf16[128,2048]{1,0:T(8,128)(2,1)} %fusion.7), channel_id=1, source_target_pairs={{0,2},{1,3},{2,0},{3,1},{4,6},{5,7},{6,4},{7,5},{8,10},{9,11},{10,... | collective-permute-start | bytes 1572872 | tf_op jit(solution)/shard_map/ppermute | solution.py:405
  363.2 28.2 %collective-permute-start.93 = (bf16[128,2048]{1,0:T(8,128)(2,1)}, bf16[128,2048]{1,0:T(8,128)(2,1)}, u32[]{:S(2)}, u32[]{:S(2)}) collective-permute-start(bf16[128,2048]{1,0:T(8,128)(2,1)} %slice.745), channel_id=1, source_target_pairs={{0,2},{1,3},{2,0},{3,1},{4,6},{5,7},{6,4},{7,5},{8,10},{9,11},{10,... | collective-permute-start | bytes 1572872 | tf_op jit(solution)/shard_map/ppermute | solution.py:405
  375.4 88.1 %all-to-all-start.2 = ((bf16[4,256,1536]{2,1,0:T(8,128)(2,1)}), bf16[4,256,1536]{2,1,0:T(8,128)(2,1)}, u32[]{:S(2)}, u32[]{:S(2)}) async-start(bf16[4,256,1536]{2,1,0:T(8,128)(2,1)} %fusion), calls=%async_computation.2 | async-start | bytes 6291456 | tf_op jit(solution)/shard_map/all_to_all | solution.py:384
  423.4 25.3 %collective-permute-start.105 = (bf16[4,256,512]{2,1,0:T(8,128)(2,1)S(1)}, bf16[4,256,512]{2,1,0:T(8,128)(2,1)S(1)}, u32[]{:S(2)}, u32[]{:S(2)}) collective-permute-start(bf16[4,256,512]{2,1,0:T(8,128)(2,1)S(1)} %pad_maximum_fusion.16), channel_id=1, source_target_pairs={{0,4},{4,0},{8,12},{12,8},{16,20},{20,16},{24,28},{28,24},{1,5},{5... | collective-permute-start | bytes 3145736 | tf_op jit(solution)/shard_map/ppermute | solution.py:394
  429.9 42.6 %collective-permute-start.106 = (bf16[64,2048]{1,0:T(8,128)(2,1)}, bf16[64,2048]{1,0:T(8,128)(2,1)}, u32[]{:S(2)}, u32[]{:S(2)}) collective-permute-start(bf16[64,2048]{1,0:T(8,128)(2,1)} %get-tuple-element.402), channel_id=1, source_target_pairs={{0,24},{4,28},{8,16},{12,20},{16,8},{20,12},{24,0},{28,4},{1,25},{... | collective-permute-start | bytes 786440 | tf_op jit(solution)/shard_map/ppermute | solution.py:368
  433.4 48.6 %collective-permute-start.107 = (bf16[64,2048]{1,0:T(8,128)(2,1)}, bf16[64,2048]{1,0:T(8,128)(2,1)}, u32[]{:S(2)}, u32[]{:S(2)}) collective-permute-start(bf16[64,2048]{1,0:T(8,128)(2,1)} %get-tuple-element.403), channel_id=1, source_target_pairs={{0,16},{4,20},{8,24},{12,28},{16,0},{20,4},{24,8},{28,12},{1,17},{... | collective-permute-start | bytes 786440 | tf_op jit(solution)/shard_map/ppermute | solution.py:368
  463.6 57.5 %all-to-all-start.3 = ((bf16[4,256,512]{2,1,0:T(8,128)(2,1)}), bf16[4,256,512]{2,1,0:T(8,128)(2,1)S(1)}, u32[]{:S(2)}, u32[]{:S(2)}) async-start(bf16[4,256,512]{2,1,0:T(8,128)(2,1)} %fusion.2), calls=%async_computation.3 | async-start | bytes 2097152 | tf_op jit(solution)/shard_map/all_to_all | solution.py:384
  467.2 24.1 %collective-permute-start.108 = (bf16[64,2048]{1,0:T(8,128)(2,1)S(1)}, bf16[64,2048]{1,0:T(8,128)(2,1)S(1)}, u32[]{:S(2)}, u32[]{:S(2)}) collective-permute-start(bf16[64,2048]{1,0:T(8,128)(2,1)S(1)} %slice.750), channel_id=1, source_target_pairs={{0,8},{4,12},{8,0},{12,4},{16,24},{20,28},{24,16},{28,20},{1,9},{5... | collective-permute-start | bytes 786440 | tf_op jit(solution)/shard_map/ppermute | solution.py:368
  470.1 39.0 %collective-permute-start.112 = (bf16[64,2048]{1,0:T(8,128)(2,1)}, bf16[64,2048]{1,0:T(8,128)(2,1)}, u32[]{:S(2)}, u32[]{:S(2)}) collective-permute-start(bf16[64,2048]{1,0:T(8,128)(2,1)} %get-tuple-element.339), channel_id=1, source_target_pairs={{0,24},{4,28},{8,16},{12,20},{16,8},{20,12},{24,0},{28,4},{1,25},{... | collective-permute-start | bytes 786440 | tf_op jit(solution)/shard_map/ppermute | solution.py:368
  497.2 21.7 %collective-permute-start.113 = (bf16[64,2048]{1,0:T(8,128)(2,1)}, bf16[64,2048]{1,0:T(8,128)(2,1)}, u32[]{:S(2)}, u32[]{:S(2)}) collective-permute-start(bf16[64,2048]{1,0:T(8,128)(2,1)} %get-tuple-element.341), channel_id=1, source_target_pairs={{0,16},{4,20},{8,24},{12,28},{16,0},{20,4},{24,8},{28,12},{1,17},{... | collective-permute-start | bytes 786440 | tf_op jit(solution)/shard_map/ppermute | solution.py:368
  (160 other events, 1490.9 us)
